TPU v7x, 768 devices: a whole 4x8x12 slice. The times are simulated.
768 devices in a mesh: section: 192 (over z, x, y_lo), dp: 4 (over y_hi, core).
Axes of the slice: x: 4, y: 8 (y_hi: 2, y_lo: 4; y = y_hi * 4 + y_lo), z: 12, core: 2. Of those that a mesh axis runs over, the one named last changes fastest.
Arguments:
- activations: bfloat16 [192, 4, 1, 14, 14, 1024], P('section', 'dp'), may hold values from -6 to 6
- incoming: bfloat16 [192, 4, 1, 14, 14, 1024], P('section', 'dp'), may hold values from -6 to 6
- saved: bfloat16 [2, 192, 4, 1, 14, 14, 1024], P(None, 'section', 'dp'), may hold values from -6 to 6
- images: bfloat16 [2, 4, 1, 14, 14, 1024], P(None, 'dp'), may hold values from -6 to 6
- head_grads: bfloat16 [2, 4, 1, 14, 14, 1024], P(None, 'dp'), may hold values from -6 to 6
- pw_weight: bfloat16 [192, 1024, 1024], P('section'), may hold values from -0.1875 to 0.1875
- dw_kernel: float32 [192, 25, 1024], P('section'), may hold values from -1.25 to 1.25
Outputs:
- act_out: bfloat16 [192, 4, 1, 14, 14, 1024], P('section', 'dp')
- grad_out: bfloat16 [192, 4, 1, 14, 14, 1024], P('section', 'dp')
- w_grad: float32 [192, 1024, 1024], P('section', 'dp')
- k_grad: float32 [192, 25, 1024], P('section', None, 'dp')
All inputs are finite; a program needn't handle non-finite values.
Results may differ from a plain program's by a relative error of at most 0.013.
Values may be sent and summed in bfloat16 or wider, within the bound.
No kernel may reach another device: no remote copies, remote signals or barrier semaphores. Data moves between devices by JAX's collectives and lax.ppermute only.
A program may use at most 64 MiB of HBM per device.

v0:
```python
import jax
import jax.numpy as jnp
from jax import lax
from jax.sharding import PartitionSpec as P

KW = 5
TICKS = 2


def shifted(value, axis, by):
    peers = lax.axis_size(axis)
    pairs = [(i, i + by) for i in range(peers) if 0 <= i + by < peers]
    return lax.ppermute(value, axis, pairs)


def depth_conv(field, kernel):
    channels = field.shape[-1]
    taps = kernel.reshape(KW, KW, 1, channels)
    return lax.conv_general_dilated(
        field,
        taps,
        (1, 1),
        ((2, 2), (2, 2)),
        dimension_numbers=("NHWC", "HWIO", "NHWC"),
        feature_group_count=channels,
        precision=lax.Precision.HIGHEST,
    )


def depthwise(field, kernel):
    return depth_conv(field, kernel)


def depthwise_back(grad, kernel):
    flipped = kernel.reshape(KW, KW, -1)[::-1, ::-1].reshape(KW * KW, -1)
    return depth_conv(grad, flipped)


def kernel_terms(rectified, grad):
    count, size, size_two, channels = grad.shape
    lhs_field = jnp.transpose(rectified, (1, 2, 3, 0)).reshape(1, size, size_two, channels * count)
    rhs_field = jnp.transpose(grad, (1, 2, 0, 3))
    result = lax.conv_general_dilated(
        lhs_field,
        rhs_field,
        (1, 1),
        ((2, 2), (2, 2)),
        dimension_numbers=("NHWC", "HWIO", "NHWC"),
        feature_group_count=channels,
        precision=lax.Precision.HIGHEST,
    )
    return result.reshape(KW * KW, channels)


def cell_forward(inputs, kernel, weight):
    channels = inputs.shape[-1]
    widened = inputs.astype(jnp.float32)
    rectified = jnp.maximum(widened, 0.0)
    mixed = depthwise(rectified, kernel).astype(jnp.bfloat16)
    branch = jnp.dot(mixed.reshape(-1, channels), weight, preferred_element_type=jnp.float32)
    return (widened + branch.reshape(inputs.shape)).astype(jnp.bfloat16)


def cell_backward(inputs, upstream, kernel, weight):
    channels = inputs.shape[-1]
    widened = inputs.astype(jnp.float32)
    rectified = jnp.maximum(widened, 0.0)
    mixed = depthwise(rectified, kernel).astype(jnp.bfloat16).reshape(-1, channels)
    grad_rows = upstream.reshape(-1, channels)
    grad_mixed = lax.dot_general(
        grad_rows, weight, (((1,), (1,)), ((), ())), preferred_element_type=jnp.float32
    ).reshape(inputs.shape)
    grad_rect = depthwise_back(grad_mixed, kernel)
    kernel_term = kernel_terms(rectified, grad_mixed)
    grad_in = (upstream.astype(jnp.float32) + jnp.where(widened > 0, grad_rect, 0.0)).astype(
        jnp.bfloat16
    )
    return (grad_in, mixed, grad_rows, kernel_term)


def per_device(activations, incoming, saved, images, head_grads, pw_weight, dw_kernel):
    section_pos = lax.axis_index("section")
    section_count = lax.axis_size("section")
    weight = pw_weight[0]
    kernel = dw_kernel[0]
    current = activations[0, 0]
    upstream = incoming[0, 0]
    mixed_list = []
    grads_list = []
    kernel_total = jnp.zeros(kernel.shape, jnp.float32)
    for tick in range(TICKS):
        result = cell_forward(current, kernel, weight)
        forward_arrived = shifted(result, "section", 1)
        current = jnp.where(section_pos == 0, images[tick, 0], forward_arrived)
        grad_in, mixed, grad_rows, kernel_term = cell_backward(
            saved[tick, 0, 0], upstream, kernel, weight
        )
        arrived = shifted(grad_in, "section", -1)
        upstream, mixed, grad_rows, kernel_term = (
            jnp.where(section_pos == section_count - 1, head_grads[tick, 0], arrived),
            mixed,
            grad_rows,
            kernel_term,
        )
        mixed_list.append(mixed)
        grads_list.append(grad_rows)
        kernel_total = kernel_total + kernel_term
    mixed_all = jnp.concatenate(mixed_list, axis=0)
    grads_all = jnp.concatenate(grads_list, axis=0)
    scale = 1.0 / (lax.axis_size("dp") * TICKS)
    full_term = lax.dot_general(
        mixed_all, grads_all, (((0,), (0,)), ((), ())), preferred_element_type=jnp.float32
    )
    reduced = lax.psum_scatter(
        full_term.astype(jnp.bfloat16), "dp", scatter_dimension=0, tiled=True
    ).astype(jnp.float32)
    w_grad = (reduced * scale)[None]
    k_grad = (
        lax.psum_scatter(
            kernel_total[None].astype(jnp.bfloat16), "dp", scatter_dimension=2, tiled=True
        ).astype(jnp.float32)
        * scale
    )
    return (current[None, None], upstream[None, None], w_grad, k_grad)


def solution(mesh):
    in_specs = (
        P("section", "dp", None, None, None, None),
        P("section", "dp", None, None, None, None),
        P(None, "section", "dp", None, None, None, None),
        P(None, "dp", None, None, None, None),
        P(None, "dp", None, None, None, None),
        P("section", None, None),
        P("section", None, None),
    )
    out_specs = (
        P("section", "dp", None, None, None, None),
        P("section", "dp", None, None, None, None),
        P("section", "dp", None),
        P("section", None, "dp"),
    )
    return jax.shard_map(
        per_device, mesh=mesh, in_specs=in_specs, out_specs=out_specs, check_vma=False
    )
```

profile of v0, /device:TPU:1, one launch (start us, length us, event | category | flops | bytes accessed | tf_op | source)
XLA Modules:
  0.0 198.8 jit_solution(6269679281592739524)
XLA Ops:
  7.2 1.3 reshape_squeeze.14
  8.5 0.4 copy-done
  8.9 0.8 fusion.6
  9.7 1.8 reshape.165
  11.6 1.1 reduce
  12.7 0.3 rev.4
  13.0 0.1 reshape_reshape.4
  13.1 2.9 %fusion.63 = (bf16[1,1,1,1,14,14,1024]{6,0,5,4,3,2,1:T(2,128)(2,1)S(1)}, bf16[1,1,1,1,14,14,1024]{6,0,5,4,3,2,1:T(2,128)(2,1)S(1)}) fusion(bf16[2,1,1,1,14,14,1024]{6,0,5,4,3,2,1:T(2,128)(2,1)} %param.9), kind=kLoop, calls=%fused_computation.73 | loop fusion | bytes 1605632 | tf_op jit(solution)/shard_map/slice | solution.py:96
  16.0 4.6 %fusion.65 = f32[1,14,14,1024]{3,0,2,1:T(1,128)S(1)} fusion(f32[1,14,14,1024]{3,0,2,1:T(1,128)S(1)} %copy-done.12, f32[5,5,1,1024]{3,2,1,0:T(1,128)S(1)} %reshape_reshape.4), kind=kOutput, calls=%fused_computation.75 | convolution fusion | flops 50331648 | bytes 1708032 | tf_op jit(solution)/shard_map/conv_general_dilated | solution.py:19
  20.6 0.5 fusion.33
  21.1 1.5 collective-permute-start.2
  22.6 2.3 %fusion.62 = (bf16[1,1,1,14,14,1024]{5,0,4,3,2,1:T(2,128)(2,1)}, bf16[1,1,1,14,14,1024]{5,0,4,3,2,1:T(2,128)(2,1)}) fusion(bf16[2,1,1,14,14,1024]{5,0,4,3,2,1:T(2,128)(2,1)S(1)} %copy-done.3), kind=kLoop, calls=%fused_computation.72 | loop fusion | bytes 1605632 | tf_op jit(solution)/shard_map/slice | solution.py:100
  24.9 0.4 fusion.30
  25.4 0.4 copy-done.14
  25.8 5.2 %fusion.28 = bf16[14,14,1024]{2,1,0:T(8,128)(2,1)} fusion(f32[5,5,1,1024]{3,2,1,0:T(1,128)S(1)} %bitcast.100, f32[1,14,14,1024]{3,2,1,0:T(8,128)S(1)} %get-tuple-element.15), kind=kOutput, calls=%fused_computation.29 | convolution fusion | flops 50532352 | bytes 1306624 | tf_op jit(solution)/shard_map/conv_general_dilated | solution.py:19
  31.0 5.2 %fusion.27 = bf16[14,14,1024]{2,1,0:T(8,128)(2,1)} fusion(f32[5,5,1,1024]{3,2,1,0:T(1,128)S(1)} %bitcast.101, f32[1,14,14,1024]{3,2,1,0:T(8,128)S(1)} %get-tuple-element.14), kind=kOutput, calls=%fused_computation.28 | convolution fusion | flops 50532352 | bytes 1306624 | tf_op jit(solution)/shard_map/conv_general_dilated | solution.py:19
  36.2 1.8 transpose_reshape.8
  38.1 1.9 reshape.161
  40.0 1.9 reshape.160
  41.9 5.7 %fusion.58 = f32[1,5,5,1024]{3,0,2,1:T(1,128)} fusion(f32[14,14,1,1024]{3,2,1,0:T(1,128)} %transpose_reshape.8, f32[1,14,14,1024]{3,2,1,0:T(8,128)} %copy-done.10), kind=kOutput, calls=%fused_computation.67 | convolution fusion | flops 50331648 | bytes 1708032 | tf_op jit(solution)/shard_map/conv_general_dilated | solution.py:43
  47.6 1.2 fusion.46
  48.8 0.9 reshape.158
  49.6 1.8 fusion.4
  51.5 1.8 transpose_reshape.9
  53.3 6.0 %fusion.29 = bf16[5,5,1024]{2,1,0:T(8,128)(2,1)} fusion(f32[1,5,5,1024]{3,0,2,1:T(1,128)} %fusion.58, f32[14,14,1,1024]{3,2,1,0:T(1,128)} %transpose_reshape.9, f32[1,14,14,1024]{3,2,1,0:T(8,128)} %copy-done.9), kind=kOutput, calls=%fused_computation.30 | convolution fusion | flops 50382848 | bytes 1759232 | tf_op jit(solution)/shard_map/conv_general_dilated | solution.py:43
  59.3 1.5 convert_element_type.140
  60.9 4.0 %convolution_convert_fusion = bf16[1024,1024]{1,0:T(8,128)(2,1)} fusion(bf16[196,1024]{1,0:T(8,128)(2,1)} %reshape.161, bf16[196,1024]{1,0:T(8,128)(2,1)} %reshape.160, bf16[196,1024]{1,0:T(8,128)(2,1)} %reshape.158, bf16[196,1024]{1,0:T(8,128)(2,1)} %copy-done.8), kind=kOutput, calls=%fused_computation.8 | convolution fusion | flops 826343424 | bytes 3702784 | tf_op jit(solution)/shard_map/dot_general | solution.py:111
  64.9 1.1 fusion.32
  66.0 2.9 %convolution_convert_fusion.4 = bf16[1,14,14,1024]{3,0,2,1:T(2,128)(2,1)S(1)} fusion(f32[5,5,1,1024]{3,2,1,0:T(1,128)S(1)} %bitcast.102, f32[1,14,14,1024]{3,2,1,0:T(8,128)S(1)} %fusion.32), kind=kOutput, calls=%fused_computation.14 | convolution fusion | flops 50532352 | bytes 1306624 | tf_op jit(solution)/shard_map/conv_general_dilated | solution.py:19
  69.0 1.4 fusion.23
  70.4 5.4 %collective-permute-start = (bf16[1,14,14,1024]{3,2,1,0:T(8,128)(2,1)}, bf16[1,14,14,1024]{3,2,1,0:T(8,128)(2,1)}, u32[]{:S(2)}, u32[]{:S(2)}) collective-permute-start(bf16[1,14,14,1024]{3,2,1,0:T(8,128)(2,1)} %fusion.23), channel_id=1, source_target_pairs={{0,4},{4,8},{8,12},{12,16},{16,20},{20,24},{24,28},{28,32},{32,36}... | collective-permute-start | bytes 1204232 | tf_op jit(solution)/shard_map/ppermute | solution.py:13
  75.8 4.0 %fusion.64 = (bf16[1,1,1,14,14,1024]{5,0,4,3,2,1:T(2,128)(2,1)}, bf16[1,1,1,14,14,1024]{5,0,4,3,2,1:T(2,128)(2,1)}) fusion(bf16[2,1,1,14,14,1024]{5,0,4,3,2,1:T(2,128)(2,1)} %param.10), kind=kLoop, calls=%fused_computation.74 | loop fusion | bytes 1605632 | tf_op jit(solution)/shard_map/slice | solution.py:94
  79.9 1.8 reshape.166
  81.7 1.4 convert_maximum_fusion.3
  83.1 2.9 %convolution_convert_fusion.3 = bf16[1,14,14,1024]{3,0,2,1:T(2,128)(2,1)S(1)} fusion(f32[5,5,1,1024]{3,2,1,0:T(1,128)S(1)} %bitcast.103, f32[1,14,14,1024]{3,2,1,0:T(8,128)S(1)} %convert_maximum_fusion.3), kind=kOutput, calls=%fused_computation.13 | convolution fusion | flops 50532352 | bytes 1306624 | tf_op jit(solution)/shard_map/conv_general_dilated | solution.py:19
  86.1 1.5 fusion.17
  87.6 5.0 %collective-permute-start.1 = (bf16[1,14,14,1024]{3,2,1,0:T(8,128)(2,1)}, bf16[1,14,14,1024]{3,2,1,0:T(8,128)(2,1)}, u32[]{:S(2)}, u32[]{:S(2)}) collective-permute-start(bf16[1,14,14,1024]{3,2,1,0:T(8,128)(2,1)} %fusion.17), channel_id=1, source_target_pairs={{0,4},{4,8},{8,12},{12,16},{16,20},{20,24},{24,28},{28,32},{32,36}... | collective-permute-start | bytes 1204232 | tf_op jit(solution)/shard_map/ppermute | solution.py:13
  92.6 4.6 %fusion.66 = f32[1,14,14,1024]{3,0,2,1:T(1,128)S(1)} fusion(f32[1,14,14,1024]{3,0,2,1:T(1,128)S(1)} %copy-done.11, f32[5,5,1,1024]{3,2,1,0:T(1,128)S(1)} %copy-done.16), kind=kOutput, calls=%fused_computation.76 | convolution fusion | flops 50331648 | bytes 1708032 | tf_op jit(solution)/shard_map/conv_general_dilated | solution.py:19
  97.3 1.2 fusion.35
  98.4 1.3 collective-permute-start.3
  99.7 14.9 %reduce-scatter.5.cloned.1.call-done = bf16[1,25,256]{2,1,0:T(8,128)(2,1)} async-done(((bf16[1,25,1024]{2,1,0:T(8,128)(2,1)}), bf16[1,25,256]{2,1,0:T(8,128)(2,1)}) %reduce-scatter.5.cloned.1.call-update) | async-done | bytes 12816 | tf_op jit(solution)/shard_map/reduce_scatter | solution.py:119
  114.7 0.7 convert_multiply_fusion
  115.4 0.6 copy.48
  116.0 2.1 %fusion.50 = bf16[1,1,1,14,14,1024]{5,4,3,2,1,0:T(8,128)(2,1)} fusion(bf16[1,14,14,1024]{3,2,1,0:T(8,128)(2,1)} %collective-permute-done.1, bf16[1,1,1,14,14,1024]{5,0,4,3,2,1:T(2,128)(2,1)} %get-tuple-element.12, pred[]{:T(512)S(6)} %eq.8), kind=kLoop, calls=%fused_computation.58 | loop fusion | flops 200704 | bytes 1204225 | tf_op jit(solution)/shard_map/broadcast_in_dim | solution.py:124
  118.1 6.6 %collective-permute-done.3 = bf16[1,14,14,1024]{3,2,1,0:T(8,128)(2,1)S(1)} collective-permute-done((bf16[1,14,14,1024]{3,2,1,0:T(8,128)(2,1)}, bf16[1,14,14,1024]{3,2,1,0:T(8,128)(2,1)S(1)}, u32[]{:S(2)}, u32[]{:S(2)}) %collective-permute-start.3) | collective-permute-done | bytes 401440 | tf_op jit(solution)/shard_map/ppermute | solution.py:13
  124.7 0.9 fusion.48
  125.7 64.1 %reduce-scatter.3.cloned.1.call-done = bf16[256,1024]{1,0:T(8,128)(2,1)} async-done(((bf16[1024,1024]{1,0:T(8,128)(2,1)}), bf16[256,1024]{1,0:T(8,128)(2,1)}) %reduce-scatter.3.cloned.1.call-update) | async-done | bytes 524304 | tf_op jit(solution)/shard_map/reduce_scatter | solution.py:114
  189.8 2.1 %multiply_bitcast_fusion = f32[1,256,1024]{2,1,0:T(8,128)} fusion(bf16[256,1024]{1,0:T(8,128)(2,1)} %reduce-scatter.3.cloned.1.call-done), kind=kLoop, calls=%fused_computation.31 | loop fusion | flops 524288 | bytes 1572864 | tf_op jit(solution)/shard_map/broadcast_in_dim | solution.py:117
  (40 shorter events, 0.2 us)
Async XLA Ops:
  7.2 1.7 copy-start
  7.2 107.5 %reduce-scatter.5.cloned.1.call-start = ((), (), s32[]{:S(2)}) async-start(), calls=%async_computation.3 | async-start | bytes 81920 | tf_op jit(solution)/shard_map/reduce_scatter | solution.py:119
  8.9 2.7 %copy-start.8 = (bf16[196,1024]{1,0:T(8,128)(2,1)}, bf16[196,1024]{1,0:T(8,128)(2,1)S(1)}, u32[]{:S(2)}) copy-start(bf16[196,1024]{1,0:T(8,128)(2,1)S(1)} %reshape_squeeze.14) | copy-start | bytes 1204228
  13.0 3.0 %copy-start.12 = (f32[1,14,14,1024]{3,0,2,1:T(1,128)S(1)}, f32[1,14,14,1024]{3,0,2,1:T(1,128)}, u32[]{:S(2)}) copy-start(f32[1,14,14,1024]{3,0,2,1:T(1,128)} %reshape.165) | copy-start | bytes 2408452
  13.1 7.5 %copy-start.15 = (f32[5,5,1,1024]{3,2,1,0:T(1,128)}, f32[5,5,1,1024]{3,2,1,0:T(1,128)S(1)}, u32[]{:S(2)}) copy-start(f32[5,5,1,1024]{3,2,1,0:T(1,128)S(1)} %reshape_reshape.4) | copy-start | bytes 307204
  16.0 8.9 %copy-start.1 = (bf16[1,1,1,1,14,14,1024]{6,0,5,4,3,2,1:T(2,128)(2,1)}, bf16[1,1,1,1,14,14,1024]{6,0,5,4,3,2,1:T(2,128)(2,1)S(1)}, u32[]{:S(2)}) copy-start(bf16[1,1,1,1,14,14,1024]{6,0,5,4,3,2,1:T(2,128)(2,1)S(1)} %get-tuple-element.10) | copy-start | bytes 1204228
  16.0 4.7 %copy-start.7 = (bf16[1,1,1,14,14,1024]{5,4,3,2,1,0:T(8,128)(2,1)S(1)}, bf16[1,1,1,14,14,1024]{5,4,3,2,1,0:T(8,128)(2,1)}, u32[]{:S(2)}) copy-start(bf16[1,1,1,14,14,1024]{5,4,3,2,1,0:T(8,128)(2,1)} %param.8) | copy-start | bytes 1204228
  20.6 2.0 %copy-start.3 = (bf16[2,1,1,14,14,1024]{5,0,4,3,2,1:T(2,128)(2,1)S(1)}, bf16[2,1,1,14,14,1024]{5,0,4,3,2,1:T(2,128)(2,1)}, u32[]{:S(2)}) copy-start(bf16[2,1,1,14,14,1024]{5,0,4,3,2,1:T(2,128)(2,1)} %param.11) | copy-start | bytes 2408452
  21.1 26.4 %collective-permute-start.2 = (bf16[1,14,14,1024]{3,2,1,0:T(8,128)(2,1)S(1)}, bf16[1,14,14,1024]{3,2,1,0:T(8,128)(2,1)}, u32[]{:S(2)}, u32[]{:S(2)}) collective-permute-start(bf16[1,14,14,1024]{3,2,1,0:T(8,128)(2,1)S(1)} %fusion.33), channel_id=1, source_target_pairs={{4,0},{8,4},{12,8},{16,12},{20,16},{24,20},{28,24},{32,28},{36,32}... | collective-permute-start | bytes 1204232 | tf_op jit(solution)/shard_map/ppermute | solution.py:13
  24.9 0.9 copy-start.14
  25.4 5.7 %copy-start.9 = (f32[1,14,14,1024]{3,2,1,0:T(8,128)}, f32[1,14,14,1024]{3,2,1,0:T(8,128)S(1)}, u32[]{:S(2)}) copy-start(f32[1,14,14,1024]{3,2,1,0:T(8,128)S(1)} %get-tuple-element.15) | copy-start | bytes 2408452
  25.4 5.7 %copy-start.10 = (f32[1,14,14,1024]{3,2,1,0:T(8,128)}, f32[1,14,14,1024]{3,2,1,0:T(8,128)S(1)}, u32[]{:S(2)}) copy-start(f32[1,14,14,1024]{3,2,1,0:T(8,128)S(1)} %get-tuple-element.14) | copy-start | bytes 2408452
  41.8 5.7 %copy-start.5 = (bf16[1,1,1,14,14,1024]{5,0,4,3,2,1:T(2,128)(2,1)S(1)}, bf16[1,1,1,14,14,1024]{5,0,4,3,2,1:T(2,128)(2,1)}, u32[]{:S(2)}) copy-start(bf16[1,1,1,14,14,1024]{5,0,4,3,2,1:T(2,128)(2,1)} %get-tuple-element.9) | copy-start | bytes 1204228
  60.8 129.0 %reduce-scatter.3.cloned.1.call-start = ((), (), s32[]{:S(2)}) async-start(), calls=%async_computation.2 | async-start | bytes 2621440 | tf_op jit(solution)/shard_map/reduce_scatter | solution.py:114
  66.0 2.9 %copy-start.13 = (bf16[1,1,1,14,14,1024]{5,4,3,2,1,0:T(8,128)(2,1)S(1)}, bf16[1,1,1,14,14,1024]{5,4,3,2,1,0:T(8,128)(2,1)}, u32[]{:S(2)}) copy-start(bf16[1,1,1,14,14,1024]{5,4,3,2,1,0:T(8,128)(2,1)} %param.7) | copy-start | bytes 1204228
  70.4 11.3 %collective-permute-start = (bf16[1,14,14,1024]{3,2,1,0:T(8,128)(2,1)}, bf16[1,14,14,1024]{3,2,1,0:T(8,128)(2,1)}, u32[]{:S(2)}, u32[]{:S(2)}) collective-permute-start(bf16[1,14,14,1024]{3,2,1,0:T(8,128)(2,1)} %fusion.23), channel_id=1, source_target_pairs={{0,4},{4,8},{8,12},{12,16},{16,20},{20,24},{24,28},{28,32},{32,36}... | collective-permute-start | bytes 1204232 | tf_op jit(solution)/shard_map/ppermute | solution.py:13
  83.1 2.9 %copy-start.6 = (bf16[1,1,1,14,14,1024]{5,0,4,3,2,1:T(2,128)(2,1)S(1)}, bf16[1,1,1,14,14,1024]{5,0,4,3,2,1:T(2,128)(2,1)}, u32[]{:S(2)}) copy-start(bf16[1,1,1,14,14,1024]{5,0,4,3,2,1:T(2,128)(2,1)} %get-tuple-element.13) | copy-start | bytes 1204228
  86.1 6.6 %copy-start.11 = (f32[1,14,14,1024]{3,0,2,1:T(1,128)S(1)}, f32[1,14,14,1024]{3,0,2,1:T(1,128)}, u32[]{:S(2)}) copy-start(f32[1,14,14,1024]{3,0,2,1:T(1,128)} %reshape.166) | copy-start | bytes 2408452
  86.1 6.6 %copy-start.16 = (f32[5,5,1,1024]{3,2,1,0:T(1,128)S(1)}, f32[5,5,1,1024]{3,2,1,0:T(1,128)}, u32[]{:S(2)}) copy-start(f32[5,5,1,1024]{3,2,1,0:T(1,128)} %copy-done.15) | copy-start | bytes 307204
  87.6 9.7 %copy-start.2 = (bf16[1,1,1,1,14,14,1024]{6,0,5,4,3,2,1:T(2,128)(2,1)S(1)}, bf16[1,1,1,1,14,14,1024]{6,0,5,4,3,2,1:T(2,128)(2,1)}, u32[]{:S(2)}) copy-start(bf16[1,1,1,1,14,14,1024]{6,0,5,4,3,2,1:T(2,128)(2,1)} %copy-done.1) | copy-start | bytes 1204228
  87.6 28.4 %collective-permute-start.1 = (bf16[1,14,14,1024]{3,2,1,0:T(8,128)(2,1)}, bf16[1,14,14,1024]{3,2,1,0:T(8,128)(2,1)}, u32[]{:S(2)}, u32[]{:S(2)}) collective-permute-start(bf16[1,14,14,1024]{3,2,1,0:T(8,128)(2,1)} %fusion.17), channel_id=1, source_target_pairs={{0,4},{4,8},{8,12},{12,16},{16,20},{20,24},{24,28},{28,32},{32,36}... | collective-permute-start | bytes 1204232 | tf_op jit(solution)/shard_map/ppermute | solution.py:13
  97.3 27.4 %copy-start.4 = (bf16[1,1,1,14,14,1024]{5,0,4,3,2,1:T(2,128)(2,1)S(1)}, bf16[1,1,1,14,14,1024]{5,0,4,3,2,1:T(2,128)(2,1)}, u32[]{:S(2)}) copy-start(bf16[1,1,1,14,14,1024]{5,0,4,3,2,1:T(2,128)(2,1)} %get-tuple-element.8) | copy-start | bytes 1204228
  98.4 26.3 %collective-permute-start.3 = (bf16[1,14,14,1024]{3,2,1,0:T(8,128)(2,1)}, bf16[1,14,14,1024]{3,2,1,0:T(8,128)(2,1)S(1)}, u32[]{:S(2)}, u32[]{:S(2)}) collective-permute-start(bf16[1,14,14,1024]{3,2,1,0:T(8,128)(2,1)} %fusion.35), channel_id=1, source_target_pairs={{4,0},{8,4},{12,8},{16,12},{20,16},{24,20},{28,24},{32,28},{36,32}... | collective-permute-start | bytes 1204232 | tf_op jit(solution)/shard_map/ppermute | solution.py:13
Sparse Core Ops, SparseCore 0:
  60.9 53.6 reduce-scatter.4
  118.4 71.3 reduce-scatter.2
where the time goes:
time: 200 us; the launch traced here: 199 us
  waiting for transfers between devices  85.7 us (43%)
  matrix products  46.7 us (23%)
  local copies, waits for them, and re-layouts  25.9 us (13%)
  between operations  14.3 us (7%)
  starting transfers between devices  13.3 us (7%)
  other arithmetic  12.8 us (6%)
    reduce_scatter x1, waiting for transfers between devices, per_device(): lax.psum_scatter(full_term.astype(jnp.bfloat16), 'dp', scatter_dimension=...  64.1 us
    conv_general_dilated x6, matrix products, depth_conv(): lax.conv_general_dilated(field, taps, (1, 1), ((2, 2), (2, 2)), dimension...  25.5 us
    reduce_scatter x1, waiting for transfers between devices, per_device(): lax.psum_scatter(kernel_total[None].astype(jnp.bfloat16), 'dp', scatter_d...  14.9 us
    ppermute x4, starting transfers between devices, shifted(): return lax.ppermute(value, axis, pairs)  13.2 us
    conv_general_dilated x2, matrix products, kernel_terms(): lax.conv_general_dilated(lhs_field, rhs_field, (1, 1), ((2, 2), (2, 2)),...  11.7 us
    ppermute x4, waiting for transfers between devices, shifted(): return lax.ppermute(value, axis, pairs)  6.64 us
    slice x1, local copies, waits for them, and re-layouts, per_device(): current = jnp.where(section_pos == 0, images[tick, 0], forward_arrived)  4.04 us
    dot_general x1, matrix products, per_device(): lax.dot_general(mixed_all, grads_all, (((0,), (0,)), ((), ())), preferred...  4.01 us
  transfers between devices with their start and end apart: 6, of which 3 were waited for; matrix products, arithmetic and copies ran while one was open for 28% of the time, Pallas kernels for 0%

commit v1 on v0

v1 whole, which is shorter than its diff:
```python
import jax
import jax.numpy as jnp
from jax import lax
from jax.experimental import pallas as pl
from jax.experimental.pallas import tpu as pltpu
from jax.sharding import PartitionSpec as P

KW = 5
TAPS = KW * KW
TICKS = 2
HW = 14
PIX = HW * HW
C = 1024
LANES = 128
GROUPS = C // LANES
ROW = HW * GROUPS
HALF = C // 2
QUARTER = C // 4
PAD_ROWS = (HW + KW - 1) * ROW
DENSE_ROWS = PIX * GROUPS
TOP = (KW // 2) * ROW

f32 = jnp.float32
bf16 = jnp.bfloat16


def cols(group):
    return slice(group * LANES, (group + 1) * LANES)


def zero_pad(spread):
    zeros = jnp.zeros((TOP, LANES), f32)
    spread[0:TOP, :] = zeros
    spread[PAD_ROWS - TOP : PAD_ROWS, :] = zeros


def tile_at(spread, pixel):
    return spread[pl.ds(pl.multiple_of(pixel * GROUPS, GROUPS), GROUPS), :]


def conv(padded, taps, emit, flip):
    def row(p, carry):
        acc = [None] * HW
        for a in range(KW):
            tiles = [tile_at(padded, (p + a) * HW + q) for q in range(HW)]
            for b in range(KW):
                index = KW * a + b
                tap = taps[TAPS - 1 - index if flip else index]
                for q in range(HW):
                    src = q + b - KW // 2
                    if 0 <= src < HW:
                        term = tiles[src] * tap
                        acc[q] = term if acc[q] is None else acc[q] + term
        for q in range(HW):
            emit(p * HW + q, acc[q])
        return carry

    lax.fori_loop(0, HW, row, 0)


def tap_sums(rect_padded, grad_padded):
    def row(p, acc):
        acc = list(acc)
        grads = [tile_at(grad_padded, (p + KW // 2) * HW + q) for q in range(HW)]
        for a in range(KW):
            tiles = [tile_at(rect_padded, (p + a) * HW + q) for q in range(HW)]
            for b in range(KW):
                index = KW * a + b
                for q in range(HW):
                    src = q + b - KW // 2
                    if 0 <= src < HW:
                        acc[index] = acc[index] + tiles[src] * grads[q]
        return tuple(acc)

    return lax.fori_loop(0, HW, row, (jnp.zeros((GROUPS, LANES), f32),) * TAPS)


def store_tile(dense):
    def emit(pixel, value):
        dense[pl.ds(pl.multiple_of(pixel * GROUPS, GROUPS), GROUPS), :] = value

    return emit


def spread_rows(padded, group, value):
    padded[pl.ds(TOP + group, PIX, stride=GROUPS), :] = value


def rows_of(dense, group):
    return dense[pl.ds(group, PIX, stride=GROUPS), :]


def pack_rows(image, dst):
    for p in range(HW):
        dst[p * HW : (p + 1) * HW, :] = image[p].astype(f32)


def widen_pair(pair, wide):
    def step(p, carry):
        wide[pl.ds(pl.multiple_of(p * HW * 16, 16), HW * 16), :] = (
            pair[pl.ds(p * HW, HW)].astype(f32).reshape(HW * 16, LANES)
        )
        return carry

    lax.fori_loop(0, HW, step, 0)


def pair_tick_spread(wide, tick):
    return wide[pl.ds(tick, DENSE_ROWS, stride=TICKS), :]


def pair_tick_rows(wide, tick, group):
    return wide[pl.ds(tick + TICKS * group, PIX, stride=TICKS * GROUPS), :]


def replace_at_edge(edge, pair_hbm, tick, pair, wide, rows, sem):
    @pl.when(edge)
    def _():
        copy = pltpu.make_async_copy(pair_hbm, pair, sem)
        copy.start()
        copy.wait()
        widen_pair(pair, wide)
        for group in range(GROUPS):
            rows[:, cols(group)] = pair_tick_rows(wide, tick, group)


def mix(rows, padded, dense, mixed, taps):
    zero_pad(padded)
    for group in range(GROUPS):
        spread_rows(padded, group, jnp.maximum(rows[:, cols(group)], 0.0))
    conv(padded, taps, store_tile(dense), False)
    for group in range(GROUPS):
        mixed[:, cols(group)] = rows_of(dense, group).astype(bf16)


def finish_forward(tick, weight, images, out, rows, mixed, pair, wide, sem):
    rows[...] += jnp.dot(mixed[...], weight[...], preferred_element_type=f32)
    last = lax.axis_index("section") == lax.axis_size("section") - 1
    replace_at_edge(last, images, tick, pair, wide, rows, sem)
    out[...] = rows[...].astype(bf16)


def forward_first(
    x_hbm, w_hbm, taps_hbm, images, out, weight, taps, x, rows, padded, dense, mixed, pair, wide, sems
):
    copies = [
        pltpu.make_async_copy(src, dst, sems.at[i])
        for i, (src, dst) in enumerate([(x_hbm, x), (taps_hbm, taps), (w_hbm, weight)])
    ]
    for copy in copies:
        copy.start()
    copies[0].wait()
    pack_rows(x, rows)
    copies[1].wait()
    mix(rows, padded, dense, mixed, taps)
    copies[2].wait()
    finish_forward(0, weight, images, out, rows, mixed, pair, wide, sems.at[3])


def forward_second(x, weight, taps, images, token, out, rows, padded, dense, mixed, pair, wide, sem):
    rows[...] = x[...].astype(f32)
    mix(rows, padded, dense, mixed, taps)
    finish_forward(1, weight, images, out, rows, mixed, pair, wide, sem)


def spread_grad(g, weight, grad_mixed):
    product = lax.dot_general(
        g[...], weight[...], (((1,), (1,)), ((), ())), preferred_element_type=f32
    )
    zero_pad(grad_mixed)
    for group in range(GROUPS):
        spread_rows(grad_mixed, group, product[:, cols(group)])


def finish_backward(tick, taps, wide, heads, out, grad_mixed, rows, dense, mask, pair, spare, sem):
    mask[...] = pair_tick_spread(wide, tick)

    def emit(pixel, value):
        keep = tile_at(mask, pixel) > 0.0
        store_tile(dense)(pixel, jnp.where(keep, value, 0.0))

    conv(grad_mixed, taps, emit, True)
    for group in range(GROUPS):
        rows[:, cols(group)] += rows_of(dense, group)
    first = lax.axis_index("section") == 0
    replace_at_edge(first, heads, tick, pair, spare, rows, sem)
    out[...] = rows[...].astype(bf16)


def backward_first(
    g_hbm, saved, heads, weight, taps, token, out, grad_mixed, wide, g_rows, g, rows, dense, mask, pair, spare, sems
):
    copies = [
        pltpu.make_async_copy(src, dst, sems.at[i])
        for i, (src, dst) in enumerate([(g_hbm, g), (saved, pair)])
    ]
    for copy in copies:
        copy.start()
    copies[0].wait()
    pack_rows(g, rows)
    g_rows[...] = rows[...].astype(bf16)
    spread_grad(g_rows, weight, grad_mixed)
    copies[1].wait()
    widen_pair(pair, wide)
    finish_backward(0, taps, wide, heads, out, grad_mixed, rows, dense, mask, pair, spare, sems.at[2])


def backward_second(
    g, wide, heads, weight, taps, token, out, grad_mixed, rows, dense, mask, pair, spare, sem
):
    rows[...] = g[...].astype(f32)
    spread_grad(g, weight, grad_mixed)
    finish_backward(1, taps, wide, heads, out, grad_mixed, rows, dense, mask, pair, spare, sem)


def factors_kernel(wide, g_rows, taps, token, keep, send, rows, padded, dense):
    core = lax.rem(lax.axis_index("dp"), 2)
    high = lax.div(lax.axis_index("dp"), 2)
    send[:, C : 2 * C] = g_rows[...]
    zero_pad(padded)
    for tick in range(TICKS):
        padded[TOP : TOP + DENSE_ROWS, :] = jnp.maximum(pair_tick_spread(wide, tick), 0.0)
        conv(padded, taps, store_tile(dense), False)
        for group in range(GROUPS):
            rows[:, cols(group)] = rows_of(dense, group)
        for place in range(2):
            side = high if place == 0 else 1 - high
            at = tick * HALF + place * QUARTER
            own = pl.multiple_of((side * 2 + core) * QUARTER, QUARTER)
            other = pl.multiple_of((side * 2 + 1 - core) * QUARTER, QUARTER)
            keep[:, at : at + QUARTER] = rows[:, pl.ds(own, QUARTER)].astype(bf16)
            send[:, at : at + QUARTER] = rows[:, pl.ds(other, QUARTER)].astype(bf16)


def weight_kernel(keep, g_own0, g_own1, peer, g_peer1, token, own, other):
    def term(factor, grads):
        return lax.dot_general(factor, grads, (((0,), (0,)), ((), ())), preferred_element_type=f32)

    for place in range(2):
        first = slice(place * QUARTER, (place + 1) * QUARTER)
        second = slice(HALF + place * QUARTER, HALF + (place + 1) * QUARTER)
        total = term(keep[:, first], g_own0[...])
        total += term(peer[:, first], peer[:, C : 2 * C])
        total += term(keep[:, second], g_own1[...])
        total += term(peer[:, second], g_peer1[...])
        if place == 0:
            own[...] = total
        else:
            other[...] = total.astype(bf16)


def taps_kernel(wide, grad0, grad1, token, out, padded):
    zero_pad(padded)
    for tick in range(TICKS):
        padded[TOP : TOP + DENSE_ROWS, :] = jnp.maximum(pair_tick_spread(wide, tick), 0.0)
        sums = tap_sums(padded, (grad0, grad1)[tick])
        for index in range(TAPS):
            if tick == 0:
                out[index] = sums[index]
            else:
                out[index] += sums[index]


def final_kernel(own, arrived, out):
    out[...] = (own[...] + arrived[...].astype(f32)) * (1.0 / (2 * 2 * TICKS))


def unpack_kernel(message, out):
    rows = message[...].astype(f32)
    for p in range(HW):
        out[p] = rows[p * HW : (p + 1) * HW, :].astype(bf16)


VMEM = pl.BlockSpec(memory_space=pltpu.VMEM)
HBM = pl.BlockSpec(memory_space=pltpu.HBM)
ANY = pl.BlockSpec(memory_space=pl.ANY)


def call(kernel, ins, out_shape, scratch, args, cost=1):
    return pl.pallas_call(
        kernel,
        in_specs=ins,
        out_specs=jax.tree.map(lambda _: VMEM, out_shape),
        out_shape=out_shape,
        scratch_shapes=scratch,
        compiler_params=pltpu.CompilerParams(vmem_limit_bytes=20 * 1024 * 1024),
        cost_estimate=pl.CostEstimate(flops=0, bytes_accessed=cost << 10, transcendentals=0),
    )(*args)


PAIR = pltpu.VMEM((PIX, TICKS * GROUPS, LANES), bf16)
WIDE = pltpu.VMEM((PIX * TICKS * GROUPS, LANES), f32)
ROWS = pltpu.VMEM((PIX, C), f32)
PADDED = pltpu.VMEM((PAD_ROWS, LANES), f32)
DENSE = pltpu.VMEM((DENSE_ROWS, LANES), f32)
MIXED = pltpu.VMEM((PIX, C), bf16)
TILED = pltpu.VMEM((HW, HW, C), bf16)
IMAGE = jax.ShapeDtypeStruct((HW, HW, C), bf16)
MESSAGE = jax.ShapeDtypeStruct((PIX, C), bf16)
GRAD = jax.ShapeDtypeStruct((PAD_ROWS, LANES), f32)


def sems(count):
    return pltpu.SemaphoreType.DMA((count,)) if count > 1 else pltpu.SemaphoreType.DMA


def in_hbm(array):
    return pltpu.with_memory_space_constraint(array, pltpu.HBM)


def pair_view(array):
    moved = jnp.transpose(array, (1, 2, 0, 3)).reshape(HW, HW, TICKS, GROUPS, LANES)
    return jnp.transpose(moved, (0, 1, 3, 2, 4)).reshape(PIX, TICKS * GROUPS, LANES)


def ring(value, axis, by):
    peers = lax.axis_size(axis)
    return lax.ppermute(value, axis, [(i, (i + by) % peers) for i in range(peers)])


def other_core(value):
    return lax.ppermute(value, "dp", [(0, 1), (1, 0), (2, 3), (3, 2)])


def other_chip(value):
    return lax.ppermute(value, "dp", [(0, 2), (2, 0), (1, 3), (3, 1)])


def per_device(activations, incoming, saved, images, head_grads, pw_weight, dw_kernel):
    weight = pw_weight[0]
    taps = dw_kernel[0].reshape(TAPS, GROUPS, LANES)
    saved_pair = pair_view(saved[:, 0, 0, 0])
    image_pair = pair_view(images[:, 0, 0])
    head_pair = pair_view(head_grads[:, 0, 0])

    out0, w, t = call(
        forward_first,
        [HBM] * 4,
        (MESSAGE, jax.ShapeDtypeStruct((C, C), bf16), jax.ShapeDtypeStruct((TAPS, GROUPS, LANES), f32)),
        [TILED, ROWS, PADDED, DENSE, MIXED, PAIR, WIDE, sems(4)],
        tuple(map(in_hbm, (activations[0, 0, 0], weight, taps, image_pair))),
    )
    act1 = ring(out0, "section", 1)
    grad_in0, mixed_grad0, wide, g0 = call(
        backward_first,
        [HBM] * 3 + [VMEM, VMEM, ANY],
        (MESSAGE, GRAD, jax.ShapeDtypeStruct(WIDE.shape, f32), MESSAGE),
        [TILED, ROWS, DENSE, DENSE, PAIR, WIDE, sems(3)],
        tuple(map(in_hbm, (incoming[0, 0, 0], saved_pair, head_pair))) + (w, t, out0),
    )
    g1 = ring(grad_in0, "section", -1)
    keep, send = call(
        factors_kernel,
        [VMEM, VMEM, VMEM, ANY],
        (MESSAGE, jax.ShapeDtypeStruct((PIX, 2 * C), bf16)),
        [ROWS, PADDED, DENSE],
        (wide, g0, t, grad_in0),
    )
    peer = other_core(send)

    out1 = call(
        forward_second,
        [VMEM] * 3 + [HBM, ANY],
        MESSAGE,
        [ROWS, PADDED, DENSE, MIXED, PAIR, WIDE, sems(1)],
        (act1, w, t, in_hbm(image_pair), keep),
        8192,
    )
    act2 = ring(out1, "section", 1)
    g1, _ = lax.optimization_barrier((g1, out1))
    g1_peer = other_core(g1)
    grad_in1, mixed_grad1 = call(
        backward_second,
        [VMEM, VMEM, HBM, VMEM, VMEM, ANY],
        (MESSAGE, GRAD),
        [ROWS, DENSE, DENSE, PAIR, WIDE, sems(1)],
        (g1, wide, in_hbm(head_pair), w, t, out1),
    )
    g2 = ring(grad_in1, "section", -1)

    own, other = call(
        weight_kernel,
        [VMEM] * 5 + [ANY],
        (jax.ShapeDtypeStruct((QUARTER, C), f32), jax.ShapeDtypeStruct((QUARTER, C), bf16)),
        [],
        (keep, g0, g1, peer, g1_peer, grad_in1),
    )
    arrived = other_chip(other)

    terms = call(
        taps_kernel,
        [VMEM, VMEM, VMEM, ANY],
        jax.ShapeDtypeStruct((TAPS, GROUPS, LANES), f32),
        [PADDED],
        (wide, mixed_grad0, mixed_grad1, other),
    )
    core = lax.axis_index("dp") % 2
    high = lax.axis_index("dp") // 2
    by_core = terms.reshape(TAPS, 2, 2, QUARTER)
    mine = lax.dynamic_index_in_dim(by_core, core, 2, False)
    theirs = lax.dynamic_index_in_dim(by_core, 1 - core, 2, False)
    chip = mine + other_core(theirs.astype(bf16)).astype(f32)
    keep_k = lax.dynamic_index_in_dim(chip, high, 1, False)
    send_k = lax.dynamic_index_in_dim(chip, 1 - high, 1, False)
    scale = 1.0 / (lax.axis_size("dp") * TICKS)
    k_grad = (keep_k + other_chip(send_k.astype(bf16)).astype(f32)) * scale
    act_out = call(unpack_kernel, [VMEM], IMAGE, [], (act2,))
    grad_out = call(unpack_kernel, [VMEM], IMAGE, [], (g2,))
    w_grad = call(
        final_kernel, [VMEM, VMEM], jax.ShapeDtypeStruct((QUARTER, C), f32), [], (own, arrived)
    )
    return (act_out[None, None, None], grad_out[None, None, None], w_grad[None], k_grad[None])


def solution(mesh):
    in_specs = (
        P("section", "dp", None, None, None, None),
        P("section", "dp", None, None, None, None),
        P(None, "section", "dp", None, None, None, None),
        P(None, "dp", None, None, None, None),
        P(None, "dp", None, None, None, None),
        P("section", None, None),
        P("section", None, None),
    )
    out_specs = (
        P("section", "dp", None, None, None, None),
        P("section", "dp", None, None, None, None),
        P("section", "dp", None),
        P("section", None, "dp"),
    )
    return jax.shard_map(
        per_device, mesh=mesh, in_specs=in_specs, out_specs=out_specs, check_vma=False
    )
```

time: 200 us -> 99.8 us (0.50)
  waiting for transfers between devices: 85.7 us -> 12.4 us
  matrix products: 46.7 us -> 0 us
  starting transfers between devices: 13.3 us -> 50.9 us
  Pallas kernels: 0 us -> 30.6 us
  local copies, waits for them, and re-layouts: 25.9 us -> 4.37 us
  between operations: 14.3 us -> 0.93 us
  other arithmetic: 12.8 us -> 0.02 us
    reduce_scatter x2 -> x0, waiting for transfers between devices: 79 us -> none  [the longest x1 64.1 us: per_device(): lax.psum_scatter(full_term.astype(jnp.bfloat16), 'dp', scatter_dimension=...]
    ppermute x4 -> x9, starting transfers between devices: 13.2 us -> 50.9 us  [the longest x4 33.7 us: ring(): lax.ppermute(value, axis, [(i, (i + by) % peers) for i in range(peers)])]
    conv_general_dilated x8 -> x0, matrix products: 37.1 us -> none  [the longest x6 25.5 us: depth_conv(): lax.conv_general_dilated(field, taps, (1, 1), ((2, 2), (2, 2)), dimension...]
    pallas_call x0 -> x10, Pallas kernels: none -> 30.6 us  [call(): pl.pallas_call(kernel, in_specs=ins, out_specs=jax.tree.map(lambda _: VME...]
    dot_general x5 -> x0, matrix products: 9.6 us -> none  [the longest x1 4.01 us: per_device(): lax.dot_general(mixed_all, grads_all, (((0,), (0,)), ((), ())), preferred...]
    slice x3 -> x0, local copies, waits for them, and re-layouts: 9.17 us -> none  [the longest x1 4.04 us: per_device(): current = jnp.where(section_pos == 0, images[tick, 0], forward_arrived)]
    reshape x5 -> x1, local copies, waits for them, and re-layouts: 8.33 us -> 0.07 us  [per_device(): by_core = terms.reshape(TAPS, 2, 2, QUARTER)]
    ppermute x4 -> x9, waiting for transfers between devices: 6.64 us -> 12.4 us  [the longest x2 11.6 us: other_chip(): return lax.ppermute(value, 'dp', [(0, 2), (2, 0), (1, 3), (3, 1)])]
  transfers between devices with their start and end apart: 6 -> 9, of which waited for: 3 -> 2; matrix products, arithmetic and copies ran while one was open for 28% -> 1% of each run, Pallas kernels for 0% -> 26%
where the time goes in v1:
time: 99.8 us; the launch traced here: 99.2 us
  starting transfers between devices  50.9 us (51%)
  Pallas kernels  30.6 us (31%)
  waiting for transfers between devices  12.4 us (12%)
  local copies, waits for them, and re-layouts  4.37 us (4%)
    ppermute x4, starting transfers between devices, ring(): lax.ppermute(value, axis, [(i, (i + by) % peers) for i in range(peers)])  33.7 us
    pallas_call x10, Pallas kernels, call(): pl.pallas_call(kernel, in_specs=ins, out_specs=jax.tree.map(lambda _: VME...  30.6 us
    ppermute x2, waiting for transfers between devices, other_chip(): return lax.ppermute(value, 'dp', [(0, 2), (2, 0), (1, 3), (3, 1)])  11.6 us
    ppermute x2, starting transfers between devices, other_chip(): return lax.ppermute(value, 'dp', [(0, 2), (2, 0), (1, 3), (3, 1)])  9.18 us
    ppermute x3, starting transfers between devices, other_core(): return lax.ppermute(value, 'dp', [(0, 1), (1, 0), (2, 3), (3, 2)])  8.03 us
    unnamed x15, local copies, waits for them, and re-layouts  3.57 us
  transfers between devices with their start and end apart: 9, of which 2 were waited for; matrix products, arithmetic and copies ran while one was open for 1% of the time, Pallas kernels for 26%

profile of v1, /device:TPU:1, one launch (start us, length us, event | category | flops | bytes accessed | tf_op | source)
XLA Modules:
  0.0 99.2 jit_solution(1812708157141759234)
XLA Ops:
  0.6 3.5 %shard_map.102 = (bf16[196,1024]{1,0:T(8,128)(2,1)S(1)}, bf16[1024,1024]{1,0:T(8,128)(2,1)S(1)}, f32[25,8,128]{2,1,0:T(8,128)S(1)}) custom-call(bf16[14,14,1024]{2,1,0:T(8,128)(2,1)} %bitcast.54, bf16[1024,1024]{1,0:T(8,128)(2,1)} %bitcast.49, f32[25,8,128]{2,1,0:T(8,128)} %bitcast.56, bf16[196,16,128]{2,1,0:T(8,128)(2,1)} %bitcast.45), custom_call_target="tpu_custom_call" | custom-call | bytes 1024 | tf_op jit(solution)/shard_map/pallas_call | solution.py:280
  4.1 4.0 %collective-permute-start = (bf16[196,1024]{1,0:T(8,128)(2,1)S(1)}, bf16[196,1024]{1,0:T(8,128)(2,1)S(1)}, u32[]{:S(2)}, u32[]{:S(2)}) collective-permute-start(bf16[196,1024]{1,0:T(8,128)(2,1)S(1)} %get-tuple-element.18.token), channel_id=1, source_target_pairs={{0,4},{4,8},{8,12},{12,16},{16,20},{20,24},{24,28},{28,32},{32,36}... | collective-permute-start | bytes 1204232 | tf_op jit(solution)/shard_map/ppermute | solution.py:318
  8.2 5.2 %shard_map.103 = (bf16[196,1024]{1,0:T(8,128)(2,1)S(1)}, f32[2016,128]{1,0:T(8,128)S(1)}, f32[3136,128]{1,0:T(8,128)S(1)}, bf16[196,1024]{1,0:T(8,128)(2,1)S(1)}) custom-call(bf16[14,14,1024]{2,1,0:T(8,128)(2,1)} %bitcast.55, bf16[196,16,128]{2,1,0:T(8,128)(2,1)} %bitcast.51, bf16[196,16,128]{2,1,0:T(8,128)(2,1)} %bitcast.47, ...), custom_call_target="tpu_custom_call" | custom-call | bytes 1024 | tf_op jit(solution)/shard_map/pallas_call | solution.py:280
  13.3 0.0 copy-start.5
  13.4 1.0 copy-done.5
  14.3 18.2 %collective-permute-start.2 = (bf16[196,1024]{1,0:T(8,128)(2,1)S(1)}, bf16[196,1024]{1,0:T(8,128)(2,1)S(1)}, u32[]{:S(2)}, u32[]{:S(2)}) collective-permute-start(bf16[196,1024]{1,0:T(8,128)(2,1)S(1)} %get-tuple-element.23.token), channel_id=1, source_target_pairs={{0,764},{4,0},{8,4},{12,8},{16,12},{20,16},{24,20},{28,24},{32,28}... | collective-permute-start | bytes 1204232 | tf_op jit(solution)/shard_map/ppermute | solution.py:318
  32.5 4.1 %shard_map.104 = (bf16[196,1024]{1,0:T(8,128)(2,1)S(1)}, bf16[196,2048]{1,0:T(8,128)(2,1)}) custom-call(f32[3136,128]{1,0:T(8,128)S(1)} %get-tuple-element.21.wide, bf16[196,1024]{1,0:T(8,128)(2,1)S(1)} %get-tuple-element.22.g_rows.g_own0, f32[25,8,128]{2,1,0:T(8,128)S(1)} %get-tuple-element.20.taps, bf16[196,1024]{1,0:T(8,128)(2,1)S(1)} %get-tuple-element.23.token), custom_call_target="tpu_custom_call" | custom-call | bytes 1024 | tf_op jit(solution)/shard_map/pallas_call | solution.py:280
  36.6 0.0 copy-start
  36.6 1.2 %copy-done = f32[3136,128]{1,0:T(8,128)} copy-done((f32[3136,128]{1,0:T(8,128)}, f32[3136,128]{1,0:T(8,128)S(1)}, u32[]{:S(2)}) %copy-start) | copy-done | bytes 1605656
  37.8 0.0 copy-start.3
  37.8 2.9 %collective-permute-start.4 = (bf16[196,2048]{1,0:T(8,128)(2,1)}, bf16[196,2048]{1,0:T(8,128)(2,1)}, u32[]{:S(2)}, u32[]{:S(2)}) collective-permute-start(bf16[196,2048]{1,0:T(8,128)(2,1)} %get-tuple-element.27), channel_id=1, source_target_pairs={{0,1},{1,0},{2,3},{3,2},{4,5},{5,4},{6,7},{7,6},{8,9},{9,8},{10,11... | collective-permute-start | bytes 2408456 | tf_op jit(solution)/shard_map/ppermute | solution.py:322
  40.7 0.0 collective-permute-done.x
  40.7 2.3 %shard_map.105.token = bf16[196,1024]{1,0:T(8,128)(2,1)S(1)} custom-call(bf16[196,1024]{1,0:T(8,128)(2,1)S(1)} %collective-permute-done.x, bf16[1024,1024]{1,0:T(8,128)(2,1)S(1)} %get-tuple-element.19.weight, f32[25,8,128]{2,1,0:T(8,128)S(1)} %get-tuple-element.20.taps, bf16[196,16,128]{2,1,0:T(8,128)(2,1)} %bitcast.46, ...), custom_call_target="tpu_custom_call" | custom-call | bytes 8388608 | tf_op jit(solution)/shard_map/pallas_call | solution.py:280
  43.0 0.0 copy-done.3
  43.0 0.0 collective-permute-done.2.g.g_own1
  43.0 1.9 %collective-permute-start.5 = (bf16[196,1024]{1,0:T(8,128)(2,1)S(1)}, bf16[196,1024]{1,0:T(8,128)(2,1)}, u32[]{:S(2)}, u32[]{:S(2)}) collective-permute-start(bf16[196,1024]{1,0:T(8,128)(2,1)S(1)} %collective-permute-done.2.g.g_own1), channel_id=1, source_target_pairs={{0,1},{1,0},{2,3},{3,2},{4,5},{5,4},{6,7},{7,6},{8,9},{9,8},{10,11... | collective-permute-start | bytes 1204232 | tf_op jit(solution)/shard_map/ppermute | solution.py:322
  45.0 0.0 copy-start.1
  45.0 1.4 %copy-done.1 = f32[3136,128]{1,0:T(8,128)S(1)} copy-done((f32[3136,128]{1,0:T(8,128)S(1)}, f32[3136,128]{1,0:T(8,128)}, u32[]{:S(2)}) %copy-start.1) | copy-done | bytes 1605656
  46.4 0.0 copy-start.4
  46.4 4.6 %shard_map.107 = (bf16[196,1024]{1,0:T(8,128)(2,1)}, f32[2016,128]{1,0:T(8,128)S(1)}) custom-call(bf16[196,1024]{1,0:T(8,128)(2,1)S(1)} %collective-permute-done.2.g.g_own1, f32[3136,128]{1,0:T(8,128)S(1)} %copy-done.1, bf16[196,16,128]{2,1,0:T(8,128)(2,1)} %bitcast.48, bf16[1024,1024]{1,0:T(8,128)(2,1)S(1)} %get-tuple-element.19.weight, ...), custom_call_target="tpu_custom_call" | custom-call | bytes 1024 | tf_op jit(solution)/shard_map/pallas_call | solution.py:280
  51.1 0.0 copy-start.2
  51.1 0.0 copy-start.6
  51.1 2.1 %collective-permute-start.1 = (bf16[196,1024]{1,0:T(8,128)(2,1)S(1)}, bf16[196,1024]{1,0:T(8,128)(2,1)}, u32[]{:S(2)}, u32[]{:S(2)}) collective-permute-start(bf16[196,1024]{1,0:T(8,128)(2,1)S(1)} %shard_map.105.token), channel_id=1, source_target_pairs={{0,4},{4,8},{8,12},{12,16},{16,20},{20,24},{24,28},{28,32},{32,36}... | collective-permute-start | bytes 1204232 | tf_op jit(solution)/shard_map/ppermute | solution.py:318
  53.1 9.4 %collective-permute-start.3 = (bf16[196,1024]{1,0:T(8,128)(2,1)}, bf16[196,1024]{1,0:T(8,128)(2,1)}, u32[]{:S(2)}, u32[]{:S(2)}) collective-permute-start(bf16[196,1024]{1,0:T(8,128)(2,1)} %get-tuple-element.26.token), channel_id=1, source_target_pairs={{0,764},{4,0},{8,4},{12,8},{16,12},{20,16},{24,20},{28,24},{32,28}... | collective-permute-start | bytes 1204232 | tf_op jit(solution)/shard_map/ppermute | solution.py:318
  62.5 0.0 collective-permute-done.5.g_peer1
  62.5 0.0 collective-permute-done.4.peer
  62.5 0.0 copy-done.4
  62.6 3.4 %shard_map.109 = (f32[256,1024]{1,0:T(8,128)S(1)}, bf16[256,1024]{1,0:T(8,128)(2,1)}) custom-call(bf16[196,1024]{1,0:T(8,128)(2,1)S(1)} %copy-done.4, bf16[196,1024]{1,0:T(8,128)(2,1)S(1)} %get-tuple-element.22.g_rows.g_own0, bf16[196,1024]{1,0:T(8,128)(2,1)S(1)} %collective-permute-done.2.g.g_own1, bf16[196,2048]{1,0:T(8,128)(2,1)} %collective-permute-done.4.peer, ...), custom_call_target="tpu_custom_call" | custom-call | bytes 1024 | tf_op jit(solution)/shard_map/pallas_call | solution.py:280
  65.9 4.7 %collective-permute-start.6 = (bf16[256,1024]{1,0:T(8,128)(2,1)}, bf16[256,1024]{1,0:T(8,128)(2,1)S(1)}, u32[]{:S(2)}, u32[]{:S(2)}) collective-permute-start(bf16[256,1024]{1,0:T(8,128)(2,1)} %get-tuple-element.29.token), channel_id=1, source_target_pairs={{0,2},{2,0},{1,3},{3,1},{4,6},{6,4},{5,7},{7,5},{8,10},{10,8},{9,1... | collective-permute-start | bytes 1572872 | tf_op jit(solution)/shard_map/ppermute | solution.py:326
  70.7 0.0 copy-done.2
  70.7 0.0 copy-done.6
  70.7 2.8 %shard_map.111 = f32[25,8,128]{2,1,0:T(8,128)S(1)} custom-call(f32[3136,128]{1,0:T(8,128)S(1)} %copy-done.2, f32[2016,128]{1,0:T(8,128)S(1)} %copy-done.6, f32[2016,128]{1,0:T(8,128)S(1)} %get-tuple-element.31.grad1, bf16[256,1024]{1,0:T(8,128)(2,1)} %get-tuple-element.29.token), custom_call_target="tpu_custom_call" | custom-call | bytes 1024 | tf_op jit(solution)/shard_map/pallas_call | solution.py:280
  73.5 0.1 reshape.37
  73.6 0.1 constant_dynamic-slice_fusion
  73.7 3.2 %collective-permute-start.7 = (bf16[25,2,256]{2,0,1:T(8,128)(2,1)S(1)}, bf16[25,2,256]{2,0,1:T(8,128)(2,1)S(1)}, u32[]{:S(2)}, u32[]{:S(2)}) collective-permute-start(bf16[25,2,256]{2,0,1:T(8,128)(2,1)S(1)} %bitcast.57), channel_id=1, source_target_pairs={{0,1},{1,0},{2,3},{3,2},{4,5},{5,4},{6,7},{7,6},{8,9},{9,8},{10,11... | collective-permute-start | bytes 76808 | tf_op jit(solution)/shard_map/ppermute | solution.py:322
  77.0 0.8 collective-permute-done.7
  77.8 4.4 %collective-permute-start.8 = (bf16[25,256]{1,0:T(8,128)(2,1)S(1)}, bf16[25,256]{1,0:T(8,128)(2,1)S(1)}, u32[]{:S(2)}, u32[]{:S(2)}) collective-permute-start(bf16[25,256]{1,0:T(8,128)(2,1)S(1)} %fusion.2), channel_id=1, source_target_pairs={{0,2},{2,0},{1,3},{3,1},{4,6},{6,4},{5,7},{7,5},{8,10},{10,8},{9,1... | collective-permute-start | bytes 38408 | tf_op jit(solution)/shard_map/ppermute | solution.py:326
  82.2 0.0 collective-permute-done.3.message
  82.3 1.8 %shard_map.108 = bf16[14,14,1024]{2,1,0:T(8,128)(2,1)} custom-call(bf16[196,1024]{1,0:T(8,128)(2,1)} %collective-permute-done.3.message), custom_call_target="tpu_custom_call" | custom-call | bytes 1024 | tf_op jit(solution)/shard_map/pallas_call | solution.py:280
  84.1 0.0 collective-permute-done.1.message
  84.1 1.8 %shard_map.106 = bf16[14,14,1024]{2,1,0:T(8,128)(2,1)} custom-call(bf16[196,1024]{1,0:T(8,128)(2,1)} %collective-permute-done.1.message), custom_call_target="tpu_custom_call" | custom-call | bytes 1024 | tf_op jit(solution)/shard_map/pallas_call | solution.py:280
  85.9 11.6 %collective-permute-done.8 = bf16[25,256]{1,0:T(8,128)(2,1)S(1)} collective-permute-done((bf16[25,256]{1,0:T(8,128)(2,1)S(1)}, bf16[25,256]{1,0:T(8,128)(2,1)S(1)}, u32[]{:S(2)}, u32[]{:S(2)}) %collective-permute-start.8) | collective-permute-done | bytes 12832 | tf_op jit(solution)/shard_map/ppermute | solution.py:326
  97.5 0.6 broadcast_in_dim.15
  98.1 0.0 collective-permute-done.6.arrived
  98.1 1.1 %shard_map.110 = f32[256,1024]{1,0:T(8,128)} custom-call(f32[256,1024]{1,0:T(8,128)S(1)} %get-tuple-element.28.own, bf16[256,1024]{1,0:T(8,128)(2,1)S(1)} %collective-permute-done.6.arrived), custom_call_target="tpu_custom_call" | custom-call | bytes 1024 | tf_op jit(solution)/shard_map/pallas_call | solution.py:280
  (5 shorter events, 0.1 us)
Async XLA Ops:
  4.1 36.5 %collective-permute-start = (bf16[196,1024]{1,0:T(8,128)(2,1)S(1)}, bf16[196,1024]{1,0:T(8,128)(2,1)S(1)}, u32[]{:S(2)}, u32[]{:S(2)}) collective-permute-start(bf16[196,1024]{1,0:T(8,128)(2,1)S(1)} %get-tuple-element.18.token), channel_id=1, source_target_pairs={{0,4},{4,8},{8,12},{12,16},{16,20},{20,24},{24,28},{28,32},{32,36}... | collective-permute-start | bytes 1204232 | tf_op jit(solution)/shard_map/ppermute | solution.py:318
  13.3 1.0 copy-start.5
  14.3 28.7 %collective-permute-start.2 = (bf16[196,1024]{1,0:T(8,128)(2,1)S(1)}, bf16[196,1024]{1,0:T(8,128)(2,1)S(1)}, u32[]{:S(2)}, u32[]{:S(2)}) collective-permute-start(bf16[196,1024]{1,0:T(8,128)(2,1)S(1)} %get-tuple-element.23.token), channel_id=1, source_target_pairs={{0,764},{4,0},{8,4},{12,8},{16,12},{20,16},{24,20},{28,24},{32,28}... | collective-permute-start | bytes 1204232 | tf_op jit(solution)/shard_map/ppermute | solution.py:318
  36.6 1.2 %copy-start = (f32[3136,128]{1,0:T(8,128)}, f32[3136,128]{1,0:T(8,128)S(1)}, u32[]{:S(2)}) copy-start(f32[3136,128]{1,0:T(8,128)S(1)} %get-tuple-element.21.wide) | copy-start | bytes 4816900
  37.8 5.2 %copy-start.3 = (bf16[196,1024]{1,0:T(8,128)(2,1)}, bf16[196,1024]{1,0:T(8,128)(2,1)S(1)}, u32[]{:S(2)}) copy-start(bf16[196,1024]{1,0:T(8,128)(2,1)S(1)} %get-tuple-element.24.token.keep) | copy-start | bytes 1204228
  37.8 24.7 %collective-permute-start.4 = (bf16[196,2048]{1,0:T(8,128)(2,1)}, bf16[196,2048]{1,0:T(8,128)(2,1)}, u32[]{:S(2)}, u32[]{:S(2)}) collective-permute-start(bf16[196,2048]{1,0:T(8,128)(2,1)} %get-tuple-element.27), channel_id=1, source_target_pairs={{0,1},{1,0},{2,3},{3,2},{4,5},{5,4},{6,7},{7,6},{8,9},{9,8},{10,11... | collective-permute-start | bytes 2408456 | tf_op jit(solution)/shard_map/ppermute | solution.py:322
  43.0 19.5 %collective-permute-start.5 = (bf16[196,1024]{1,0:T(8,128)(2,1)S(1)}, bf16[196,1024]{1,0:T(8,128)(2,1)}, u32[]{:S(2)}, u32[]{:S(2)}) collective-permute-start(bf16[196,1024]{1,0:T(8,128)(2,1)S(1)} %collective-permute-done.2.g.g_own1), channel_id=1, source_target_pairs={{0,1},{1,0},{2,3},{3,2},{4,5},{5,4},{6,7},{7,6},{8,9},{9,8},{10,11... | collective-permute-start | bytes 1204232 | tf_op jit(solution)/shard_map/ppermute | solution.py:322
  45.0 1.4 %copy-start.1 = (f32[3136,128]{1,0:T(8,128)S(1)}, f32[3136,128]{1,0:T(8,128)}, u32[]{:S(2)}) copy-start(f32[3136,128]{1,0:T(8,128)} %copy-done) | copy-start | bytes 4816900
  46.4 16.1 %copy-start.4 = (bf16[196,1024]{1,0:T(8,128)(2,1)S(1)}, bf16[196,1024]{1,0:T(8,128)(2,1)}, u32[]{:S(2)}) copy-start(bf16[196,1024]{1,0:T(8,128)(2,1)} %copy-done.3) | copy-start | bytes 1204228
  51.1 19.6 %copy-start.2 = (f32[3136,128]{1,0:T(8,128)S(1)}, f32[3136,128]{1,0:T(8,128)}, u32[]{:S(2)}) copy-start(f32[3136,128]{1,0:T(8,128)} %copy-done) | copy-start | bytes 4816900
  51.1 19.6 %copy-start.6 = (f32[2016,128]{1,0:T(8,128)S(1)}, f32[2016,128]{1,0:T(8,128)}, u32[]{:S(2)}) copy-start(f32[2016,128]{1,0:T(8,128)} %copy-done.5) | copy-start | bytes 3096580
  51.1 33.0 %collective-permute-start.1 = (bf16[196,1024]{1,0:T(8,128)(2,1)S(1)}, bf16[196,1024]{1,0:T(8,128)(2,1)}, u32[]{:S(2)}, u32[]{:S(2)}) collective-permute-start(bf16[196,1024]{1,0:T(8,128)(2,1)S(1)} %shard_map.105.token), channel_id=1, source_target_pairs={{0,4},{4,8},{8,12},{12,16},{16,20},{20,24},{24,28},{28,32},{32,36}... | collective-permute-start | bytes 1204232 | tf_op jit(solution)/shard_map/ppermute | solution.py:318
  53.1 29.1 %collective-permute-start.3 = (bf16[196,1024]{1,0:T(8,128)(2,1)}, bf16[196,1024]{1,0:T(8,128)(2,1)}, u32[]{:S(2)}, u32[]{:S(2)}) collective-permute-start(bf16[196,1024]{1,0:T(8,128)(2,1)} %get-tuple-element.26.token), channel_id=1, source_target_pairs={{0,764},{4,0},{8,4},{12,8},{16,12},{20,16},{24,20},{28,24},{32,28}... | collective-permute-start | bytes 1204232 | tf_op jit(solution)/shard_map/ppermute | solution.py:318
  65.9 32.2 %collective-permute-start.6 = (bf16[256,1024]{1,0:T(8,128)(2,1)}, bf16[256,1024]{1,0:T(8,128)(2,1)S(1)}, u32[]{:S(2)}, u32[]{:S(2)}) collective-permute-start(bf16[256,1024]{1,0:T(8,128)(2,1)} %get-tuple-element.29.token), channel_id=1, source_target_pairs={{0,2},{2,0},{1,3},{3,1},{4,6},{6,4},{5,7},{7,5},{8,10},{10,8},{9,1... | collective-permute-start | bytes 1572872 | tf_op jit(solution)/shard_map/ppermute | solution.py:326
  73.7 4.1 %collective-permute-start.7 = (bf16[25,2,256]{2,0,1:T(8,128)(2,1)S(1)}, bf16[25,2,256]{2,0,1:T(8,128)(2,1)S(1)}, u32[]{:S(2)}, u32[]{:S(2)}) collective-permute-start(bf16[25,2,256]{2,0,1:T(8,128)(2,1)S(1)} %bitcast.57), channel_id=1, source_target_pairs={{0,1},{1,0},{2,3},{3,2},{4,5},{5,4},{6,7},{7,6},{8,9},{9,8},{10,11... | collective-permute-start | bytes 76808 | tf_op jit(solution)/shard_map/ppermute | solution.py:322
  77.8 19.7 %collective-permute-start.8 = (bf16[25,256]{1,0:T(8,128)(2,1)S(1)}, bf16[25,256]{1,0:T(8,128)(2,1)S(1)}, u32[]{:S(2)}, u32[]{:S(2)}) collective-permute-start(bf16[25,256]{1,0:T(8,128)(2,1)S(1)} %fusion.2), channel_id=1, source_target_pairs={{0,2},{2,0},{1,3},{3,1},{4,6},{6,4},{5,7},{7,5},{8,10},{10,8},{9,1... | collective-permute-start | bytes 38408 | tf_op jit(solution)/shard_map/ppermute | solution.py:326

commit v2 on v1

v2 whole, which is shorter than its diff:
```python
import functools

import jax
import jax.numpy as jnp
from jax import lax
from jax.experimental import pallas as pl
from jax.experimental.pallas import tpu as pltpu
from jax.sharding import PartitionSpec as P

KW = 5
TAPS = KW * KW
TICKS = 2
HW = 14
PIX = HW * HW
C = 1024
LANES = 128
GROUPS = C // LANES
ROW = HW * GROUPS
HALF = C // 2
QUARTER = C // 4
PAD_ROWS = (HW + KW - 1) * ROW
DENSE_ROWS = PIX * GROUPS
TOP = (KW // 2) * ROW

f32 = jnp.float32
bf16 = jnp.bfloat16


def cols(group):
    return slice(group * LANES, (group + 1) * LANES)


def zero_pad(spread):
    zeros = jnp.zeros((TOP, LANES), f32)
    spread[0:TOP, :] = zeros
    spread[PAD_ROWS - TOP : PAD_ROWS, :] = zeros


def tile_at(spread, pixel):
    return spread[pl.ds(pl.multiple_of(pixel * GROUPS, GROUPS), GROUPS), :]


def conv(padded, taps, emit, flip):
    def row(p, carry):
        acc = [None] * HW
        for a in range(KW):
            tiles = [tile_at(padded, (p + a) * HW + q) for q in range(HW)]
            for b in range(KW):
                index = KW * a + b
                tap = taps[TAPS - 1 - index if flip else index]
                for q in range(HW):
                    src = q + b - KW // 2
                    if 0 <= src < HW:
                        term = tiles[src] * tap
                        acc[q] = term if acc[q] is None else acc[q] + term
        for q in range(HW):
            emit(p * HW + q, acc[q])
        return carry

    lax.fori_loop(0, HW, row, 0)


def tap_sums(rect_padded, grad_padded):
    def row(p, acc):
        acc = list(acc)
        grads = [tile_at(grad_padded, (p + KW // 2) * HW + q) for q in range(HW)]
        for a in range(KW):
            tiles = [tile_at(rect_padded, (p + a) * HW + q) for q in range(HW)]
            for b in range(KW):
                index = KW * a + b
                for q in range(HW):
                    src = q + b - KW // 2
                    if 0 <= src < HW:
                        acc[index] = acc[index] + tiles[src] * grads[q]
        return tuple(acc)

    return lax.fori_loop(0, HW, row, (jnp.zeros((GROUPS, LANES), f32),) * TAPS)


def store_tile(dense):
    def emit(pixel, value):
        dense[pl.ds(pl.multiple_of(pixel * GROUPS, GROUPS), GROUPS), :] = value

    return emit


def spread_rows(padded, group, value):
    padded[pl.ds(TOP + group, PIX, stride=GROUPS), :] = value


def rows_of(dense, group):
    return dense[pl.ds(group, PIX, stride=GROUPS), :]


def pack_rows(image, dst):
    for p in range(HW):
        dst[p * HW : (p + 1) * HW, :] = image[p].astype(f32)


def widen_pair(pair, wide):
    def step(p, carry):
        wide[pl.ds(pl.multiple_of(p * HW * 16, 16), HW * 16), :] = (
            pair[pl.ds(p * HW, HW)].astype(f32).reshape(HW * 16, LANES)
        )
        return carry

    lax.fori_loop(0, HW, step, 0)


def pair_tick_spread(wide, tick):
    return wide[pl.ds(tick, DENSE_ROWS, stride=TICKS), :]


def pair_tick_rows(wide, tick, group):
    return wide[pl.ds(tick + TICKS * group, PIX, stride=TICKS * GROUPS), :]


def replace_at_edge(edge, pair_hbm, tick, pair, wide, rows, sem):
    @pl.when(edge)
    def _():
        fetch(pair_hbm, pair, sem)
        widen_pair(pair, wide)
        for group in range(GROUPS):
            rows[:, cols(group)] = pair_tick_rows(wide, tick, group).astype(rows.dtype)


def fetch(src, dst, sem):
    copy = pltpu.make_async_copy(src, dst, sem)
    copy.start()
    copy.wait()


def is_first():
    return lax.axis_index("section") == 0


def is_last():
    return lax.axis_index("section") == lax.axis_size("section") - 1


def mix(rows, padded, dense, mixed, taps):
    zero_pad(padded)
    for group in range(GROUPS):
        spread_rows(padded, group, jnp.maximum(rows[:, cols(group)], 0.0))
    conv(padded, taps, store_tile(dense), False)
    for group in range(GROUPS):
        mixed[:, cols(group)] = rows_of(dense, group).astype(bf16)


def forward_first(x_hbm, w_hbm, taps_hbm, out, weight, taps, x, rows, padded, dense, mixed, sems):
    copies = [
        pltpu.make_async_copy(src, dst, sems.at[i])
        for i, (src, dst) in enumerate([(x_hbm, x), (taps_hbm, taps), (w_hbm, weight)])
    ]
    for copy in copies:
        copy.start()
    copies[0].wait()
    pack_rows(x, rows)
    copies[1].wait()
    mix(rows, padded, dense, mixed, taps)
    copies[2].wait()
    out[...] = (rows[...] + jnp.dot(mixed[...], weight[...], preferred_element_type=f32)).astype(bf16)


def forward_second(x, weight, taps, images, token, out, rows, padded, dense, mixed, pair, wide, sem):
    rows[...] = x[...].astype(f32)
    replace_at_edge(is_first(), images, 0, pair, wide, rows, sem)
    mix(rows, padded, dense, mixed, taps)
    out[...] = (rows[...] + jnp.dot(mixed[...], weight[...], preferred_element_type=f32)).astype(bf16)


def head_kernel(g_in, heads, g_out, pair, wide, rows, sem):
    @pl.when(is_last())
    def _():
        fetch(heads, pair, sem)
        widen_pair(pair, wide)
        for group in range(GROUPS):
            rows[:, cols(group)] = pair_tick_rows(wide, 0, group).astype(bf16)
        fetch(rows, g_out, sem)


def spread_grad(g, weight, grad_mixed):
    product = lax.dot_general(
        g[...], weight[...], (((1,), (1,)), ((), ())), preferred_element_type=f32
    )
    zero_pad(grad_mixed)
    for group in range(GROUPS):
        spread_rows(grad_mixed, group, product[:, cols(group)])


def finish_backward(tick, taps, wide, out, grad_mixed, rows, dense, mask):
    mask[...] = pair_tick_spread(wide, tick)

    def emit(pixel, value):
        keep = tile_at(mask, pixel) > 0.0
        store_tile(dense)(pixel, jnp.where(keep, value, 0.0))

    conv(grad_mixed, taps, emit, True)
    for group in range(GROUPS):
        out[:, cols(group)] = (rows[:, cols(group)] + rows_of(dense, group)).astype(bf16)


def backward_first(
    g_hbm, saved, weight, taps, token, out, g_rows, g, rows, grad_mixed, dense, mask, pair, wide, sems
):
    copies = [
        pltpu.make_async_copy(src, dst, sems.at[i])
        for i, (src, dst) in enumerate([(g_hbm, g), (saved, pair)])
    ]
    for copy in copies:
        copy.start()
    copies[0].wait()
    pack_rows(g, rows)
    g_rows[...] = rows[...].astype(bf16)
    spread_grad(g_rows, weight, grad_mixed)
    copies[1].wait()
    widen_pair(pair, wide)
    finish_backward(0, taps, wide, out, grad_mixed, rows, dense, mask)


def backward_second(
    g, saved, weight, taps, token, out, rows, grad_mixed, dense, mask, pair, wide, sem
):
    copy = pltpu.make_async_copy(saved, pair, sem)
    copy.start()
    rows[...] = g[...].astype(f32)
    spread_grad(g, weight, grad_mixed)
    copy.wait()
    widen_pair(pair, wide)
    finish_backward(1, taps, wide, out, grad_mixed, rows, dense, mask)


def halves(core):
    return [2 * core, 2 * core + 1, 4 + 2 * core, 5 + 2 * core]


def factors_kernel(saved, taps, token, keep, send, keep_rect, rows, padded, dense, pair, wide, sem):
    core = lax.rem(lax.axis_index("dp"), 2)
    high = lax.div(lax.axis_index("dp"), 2)
    fetch(saved, pair, sem)
    widen_pair(pair, wide)
    zero_pad(padded)
    for tick in range(TICKS):
        padded[TOP : TOP + DENSE_ROWS, :] = jnp.maximum(pair_tick_spread(wide, tick), 0.0)
        for at, (mine, theirs) in enumerate(zip(halves(core), halves(1 - core))):
            place = tick * HALF + at * LANES
            keep_rect[:, place : place + LANES] = rows_of(padded, TOP + mine).astype(bf16)
            send[:, C + place : C + place + LANES] = rows_of(padded, TOP + theirs).astype(bf16)
        conv(padded, taps, store_tile(dense), False)
        for group in range(GROUPS):
            rows[:, cols(group)] = rows_of(dense, group)
        for place in range(2):
            side = high if place == 0 else 1 - high
            at = tick * HALF + place * QUARTER
            own = pl.multiple_of((side * 2 + core) * QUARTER, QUARTER)
            other = pl.multiple_of((side * 2 + 1 - core) * QUARTER, QUARTER)
            keep[:, at : at + QUARTER] = rows[:, pl.ds(own, QUARTER)].astype(bf16)
            send[:, at : at + QUARTER] = rows[:, pl.ds(other, QUARTER)].astype(bf16)


def weight_term(factor, grads):
    return lax.dot_general(factor, grads, (((0,), (0,)), ((), ())), preferred_element_type=f32)


def weight_first(keep, g_own, peer, g_peer, out):
    out[...] = weight_term(keep[:, :HALF], g_own[...])
    out[...] += weight_term(peer[:, :HALF], g_peer[...])


def weight_second(total, keep, g_own, peer, g_peer, own, other):
    for place in range(2):
        rows = slice(place * QUARTER, (place + 1) * QUARTER)
        part = slice(HALF + place * QUARTER, HALF + (place + 1) * QUARTER)
        value = total[rows, :] + weight_term(keep[:, part], g_own[...])
        value += weight_term(peer[:, part], g_peer[...])
        if place == 0:
            own[...] = value
        else:
            other[...] = value.astype(bf16)


def taps_kernel(keep_rect, peer, g0, g0_peer, g1, g1_peer, weight, token, own, far, rect, grad, sums):
    core = lax.rem(lax.axis_index("dp"), 2)
    high = lax.div(lax.axis_index("dp"), 2)
    zero_pad(rect)
    zero_pad(grad)
    sums[...] = jnp.zeros_like(sums)
    for tick in range(TICKS):
        grads = (g0, g1)[tick][...], (g0_peer, g1_peer)[tick][...]
        for image in range(2):
            for side in range(2):
                rows = weight[pl.ds(pl.multiple_of((2 * side + core) * QUARTER, QUARTER), QUARTER), :]
                product = lax.dot_general(
                    grads[image], rows, (((1,), (1,)), ((), ())), preferred_element_type=f32
                )
                for part in range(2):
                    at = 2 * side + part
                    spread_rows(grad, 4 * image + at, product[:, cols(part)])
                    place = tick * HALF + at * LANES
                    source = keep_rect if image == 0 else peer
                    place += 0 if image == 0 else C
                    spread_rows(rect, 4 * image + at, source[:, place : place + LANES].astype(f32))
        terms = tap_sums(rect, grad)
        for index in range(TAPS):
            both = terms[index][0:4] + terms[index][4:8]
            sums[index : index + 1, :HALF] += jnp.concatenate(
                [both[i : i + 1] for i in range(4)], axis=1
            )
    low, top = sums[0:TAPS, 0:QUARTER], sums[0:TAPS, QUARTER:HALF]
    own[...] = jnp.where(high == 0, low, top)
    far[...] = jnp.where(high == 0, top, low).astype(bf16)


def final_kernel(own, arrived, out):
    out[...] = (own[...] + arrived[...].astype(f32)) * (1.0 / (2 * 2 * TICKS))


def unpack_kernel(edge, message, images, out, rows, pair, wide, sem):
    rows[...] = message[...].astype(f32)
    replace_at_edge(edge(), images, 1, pair, wide, rows, sem)
    for p in range(HW):
        out[p] = rows[p * HW : (p + 1) * HW, :].astype(bf16)


VMEM = pl.BlockSpec(memory_space=pltpu.VMEM)
HBM = pl.BlockSpec(memory_space=pltpu.HBM)
ANY = pl.BlockSpec(memory_space=pl.ANY)


def call(kernel, ins, out_shape, scratch, args, cost=1, outs=None, **options):
    pinned = [in_hbm(arg) if spec is HBM else arg for spec, arg in zip(ins, args)]
    return pl.pallas_call(
        kernel,
        in_specs=ins,
        out_specs=jax.tree.map(lambda _: VMEM, out_shape) if outs is None else outs,
        out_shape=out_shape,
        scratch_shapes=scratch,
        compiler_params=pltpu.CompilerParams(vmem_limit_bytes=20 * 1024 * 1024),
        cost_estimate=pl.CostEstimate(flops=0, bytes_accessed=cost << 10, transcendentals=0),
        **options,
    )(*pinned)


def in_hbm(array):
    return pltpu.with_memory_space_constraint(array, pltpu.HBM)


PAIR = pltpu.VMEM((PIX, TICKS * GROUPS, LANES), bf16)
WIDE = pltpu.VMEM((PIX * TICKS * GROUPS, LANES), f32)
ROWS = pltpu.VMEM((PIX, C), f32)
PADDED = pltpu.VMEM((PAD_ROWS, LANES), f32)
DENSE = pltpu.VMEM((DENSE_ROWS, LANES), f32)
MIXED = pltpu.VMEM((PIX, C), bf16)
TILED = pltpu.VMEM((HW, HW, C), bf16)
IMAGE = jax.ShapeDtypeStruct((HW, HW, C), bf16)
MESSAGE = jax.ShapeDtypeStruct((PIX, C), bf16)


def sems(count):
    return pltpu.SemaphoreType.DMA((count,)) if count > 1 else pltpu.SemaphoreType.DMA


def pair_view(array):
    moved = jnp.transpose(array, (1, 2, 0, 3)).reshape(HW, HW, TICKS, GROUPS, LANES)
    return jnp.transpose(moved, (0, 1, 3, 2, 4)).reshape(PIX, TICKS * GROUPS, LANES)


def shifted(value, by):
    peers = lax.axis_size("section")
    pairs = [(i, i + by) for i in range(peers) if 0 <= i + by < peers]
    return lax.ppermute(value, "section", pairs)


def other_core(value):
    return lax.ppermute(value, "dp", [(0, 1), (1, 0), (2, 3), (3, 2)])


def other_chip(value):
    return lax.ppermute(value, "dp", [(0, 2), (2, 0), (1, 3), (3, 1)])


def per_device(activations, incoming, saved, images, head_grads, pw_weight, dw_kernel):
    weight = pw_weight[0]
    taps = dw_kernel[0].reshape(TAPS, GROUPS, LANES)
    saved_pair = pair_view(saved[:, 0, 0, 0])
    image_pair = pair_view(images[:, 0, 0])
    head_pair = pair_view(head_grads[:, 0, 0])

    out0, w, t = call(
        forward_first,
        [HBM] * 3,
        (MESSAGE, jax.ShapeDtypeStruct((C, C), bf16), jax.ShapeDtypeStruct((TAPS, GROUPS, LANES), f32)),
        [TILED, ROWS, PADDED, DENSE, MIXED, sems(3)],
        (activations[0, 0, 0], weight, taps),
    )
    act1 = shifted(out0, 1)
    grad_in0, g0 = call(
        backward_first,
        [HBM] * 2 + [VMEM, VMEM, ANY],
        (MESSAGE, MESSAGE),
        [TILED, ROWS, PADDED, DENSE, DENSE, PAIR, WIDE, sems(2)],
        (incoming[0, 0, 0], saved_pair, w, t, out0),
    )
    g1 = shifted(grad_in0, -1)
    keep, send, keep_rect = call(
        factors_kernel,
        [HBM, VMEM, ANY],
        (MESSAGE, jax.ShapeDtypeStruct((PIX, 2 * C), bf16), MESSAGE),
        [ROWS, PADDED, DENSE, PAIR, WIDE, sems(1)],
        (saved_pair, t, grad_in0),
    )
    peer = other_core(send)
    g0_peer = other_core(g0)

    out1 = call(
        forward_second,
        [VMEM] * 3 + [HBM, ANY],
        MESSAGE,
        [ROWS, PADDED, DENSE, MIXED, PAIR, WIDE, sems(1)],
        (act1, w, t, image_pair, keep),
        8192,
    )
    act2 = shifted(out1, 1)
    g1, _ = lax.optimization_barrier((g1, out1))
    g1 = call(
        head_kernel,
        [ANY, HBM],
        MESSAGE,
        [PAIR, WIDE, MIXED, sems(1)],
        (g1, head_pair),
        outs=ANY,
        input_output_aliases={0: 0},
    )
    g1_peer = other_core(g1)
    total = call(
        weight_first,
        [VMEM] * 4,
        jax.ShapeDtypeStruct((HALF, C), f32),
        [],
        (keep, g0, peer, g0_peer),
    )
    own, other = call(
        weight_second,
        [VMEM] * 5,
        (jax.ShapeDtypeStruct((QUARTER, C), f32), jax.ShapeDtypeStruct((QUARTER, C), bf16)),
        [],
        (total, keep, g1, peer, g1_peer),
    )
    arrived = other_chip(other)
    grad_in1 = call(
        backward_second,
        [VMEM, HBM, VMEM, VMEM, ANY],
        MESSAGE,
        [ROWS, PADDED, DENSE, DENSE, PAIR, WIDE, sems(1)],
        (g1, saved_pair, w, t, other),
    )
    g2 = shifted(grad_in1, -1)

    act_out = call(
        functools.partial(unpack_kernel, is_first),
        [VMEM, HBM],
        IMAGE,
        [ROWS, PAIR, WIDE, sems(1)],
        (act2, image_pair),
    )
    own_k, far_k = call(
        taps_kernel,
        [VMEM] * 7 + [HBM],
        (jax.ShapeDtypeStruct((TAPS, QUARTER), f32), jax.ShapeDtypeStruct((TAPS, QUARTER), bf16)),
        [PADDED, PADDED, pltpu.VMEM((32, HALF), f32)],
        (keep_rect, peer, g0, g0_peer, g1, g1_peer, w, act_out),
    )
    scale = 1.0 / (lax.axis_size("dp") * TICKS)
    k_grad = (own_k + other_chip(far_k).astype(f32)) * scale
    grad_out = call(
        functools.partial(unpack_kernel, is_last),
        [VMEM, HBM],
        IMAGE,
        [ROWS, PAIR, WIDE, sems(1)],
        (g2, head_pair),
    )
    w_grad = call(
        final_kernel, [VMEM, VMEM], jax.ShapeDtypeStruct((QUARTER, C), f32), [], (own, arrived)
    )
    return (act_out[None, None, None], grad_out[None, None, None], w_grad[None], k_grad[None])


def solution(mesh):
    in_specs = (
        P("section", "dp", None, None, None, None),
        P("section", "dp", None, None, None, None),
        P(None, "section", "dp", None, None, None, None),
        P(None, "dp", None, None, None, None),
        P(None, "dp", None, None, None, None),
        P("section", None, None),
        P("section", None, None),
    )
    out_specs = (
        P("section", "dp", None, None, None, None),
        P("section", "dp", None, None, None, None),
        P("section", "dp", None),
        P("section", None, "dp"),
    )
    return jax.shard_map(
        per_device, mesh=mesh, in_specs=in_specs, out_specs=out_specs, check_vma=False
    )
```

time: 99.8 us -> 89.3 us (0.89)
  the two profiles are of different devices: /device:TPU:1 before, /device:TPU:254 now
where the time goes in v2:
time: 89.3 us; the launch traced here: 88.8 us
  waiting for transfers between devices  33.8 us (38%)
  Pallas kernels  27 us (30%)
  starting transfers between devices  26.4 us (30%)
    pallas_call x12, Pallas kernels, call(): pl.pallas_call(kernel, in_specs=ins, out_specs=jax.tree.map(lambda _: VME...  27 us
    ppermute x4, waiting for transfers between devices, shifted(): return lax.ppermute(value, 'section', pairs)  26.3 us
    ppermute x4, starting transfers between devices, shifted(): return lax.ppermute(value, 'section', pairs)  16.2 us
    ppermute x2, waiting for transfers between devices, other_chip(): return lax.ppermute(value, 'dp', [(0, 2), (2, 0), (1, 3), (3, 1)])  7.52 us
    ppermute x3, starting transfers between devices, other_core(): return lax.ppermute(value, 'dp', [(0, 1), (1, 0), (2, 3), (3, 2)])  6.25 us
    ppermute x2, starting transfers between devices, other_chip(): return lax.ppermute(value, 'dp', [(0, 2), (2, 0), (1, 3), (3, 1)])  4.02 us
  transfers between devices with their start and end apart: 9, of which 3 were waited for; matrix products, arithmetic and copies ran while one was open for 1% of the time, Pallas kernels for 25%

profile of v2, /device:TPU:254, one launch (start us, length us, event | category | flops | bytes accessed | tf_op | source)
XLA Modules:
  0.0 88.8 jit_solution(1350024701203586313)
XLA Ops:
  0.6 3.5 %shard_map.102 = (bf16[196,1024]{1,0:T(8,128)(2,1)S(1)}, bf16[1024,1024]{1,0:T(8,128)(2,1)S(1)}, f32[25,8,128]{2,1,0:T(8,128)S(1)}) custom-call(bf16[14,14,1024]{2,1,0:T(8,128)(2,1)} %bitcast.48, bf16[1024,1024]{1,0:T(8,128)(2,1)} %bitcast.43, f32[25,8,128]{2,1,0:T(8,128)} %bitcast.49), custom_call_target="tpu_custom_call" | custom-call | bytes 1024 | tf_op jit(solution)/shard_map/pallas_call | solution.py:332
  4.1 7.8 %collective-permute-start = (bf16[196,1024]{1,0:T(8,128)(2,1)S(1)}, bf16[196,1024]{1,0:T(8,128)(2,1)S(1)}, u32[]{:S(2)}, u32[]{:S(2)}) collective-permute-start(bf16[196,1024]{1,0:T(8,128)(2,1)S(1)} %get-tuple-element.17.token), channel_id=1, source_target_pairs={{0,4},{4,8},{8,12},{12,16},{16,20},{20,24},{24,28},{28,32},{32,36}... | collective-permute-start | bytes 1204232 | tf_op jit(solution)/shard_map/ppermute | solution.py:371
  11.9 3.7 %shard_map.103 = (bf16[196,1024]{1,0:T(8,128)(2,1)S(1)}, bf16[196,1024]{1,0:T(8,128)(2,1)S(1)}) custom-call(bf16[14,14,1024]{2,1,0:T(8,128)(2,1)} %bitcast.46, bf16[196,16,128]{2,1,0:T(8,128)(2,1)} %bitcast.36, bf16[1024,1024]{1,0:T(8,128)(2,1)S(1)} %get-tuple-element.18.weight, f32[25,8,128]{2,1,0:T(8,128)S(1)} %get-tuple-element.19.taps, ...), custom_call_target="tpu_custom_call" | custom-call | bytes 1024 | tf_op jit(solution)/shard_map/pallas_call | solution.py:332
  15.6 1.9 %collective-permute-start.2 = (bf16[196,1024]{1,0:T(8,128)(2,1)S(1)}, bf16[196,1024]{1,0:T(8,128)(2,1)S(1)}, u32[]{:S(2)}, u32[]{:S(2)}) collective-permute-start(bf16[196,1024]{1,0:T(8,128)(2,1)S(1)} %get-tuple-element.20.token), channel_id=1, source_target_pairs={{4,0},{8,4},{12,8},{16,12},{20,16},{24,20},{28,24},{32,28},{36,32}... | collective-permute-start | bytes 1204232 | tf_op jit(solution)/shard_map/ppermute | solution.py:371
  17.5 4.9 %shard_map.104 = (bf16[196,1024]{1,0:T(8,128)(2,1)S(1)}, bf16[196,2048]{1,0:T(8,128)(2,1)S(1)}, bf16[196,1024]{1,0:T(8,128)(2,1)S(1)}) custom-call(bf16[196,16,128]{2,1,0:T(8,128)(2,1)} %bitcast.37, f32[25,8,128]{2,1,0:T(8,128)S(1)} %get-tuple-element.19.taps, bf16[196,1024]{1,0:T(8,128)(2,1)S(1)} %get-tuple-element.20.token), custom_call_target="tpu_custom_call" | custom-call | bytes 1024 | tf_op jit(solution)/shard_map/pallas_call | solution.py:332
  22.4 1.9 %collective-permute-start.3 = (bf16[196,2048]{1,0:T(8,128)(2,1)S(1)}, bf16[196,2048]{1,0:T(8,128)(2,1)S(1)}, u32[]{:S(2)}, u32[]{:S(2)}) collective-permute-start(bf16[196,2048]{1,0:T(8,128)(2,1)S(1)} %get-tuple-element.24), channel_id=1, source_target_pairs={{0,1},{1,0},{2,3},{3,2},{4,5},{5,4},{6,7},{7,6},{8,9},{9,8},{10,11... | collective-permute-start | bytes 2408456 | tf_op jit(solution)/shard_map/ppermute | solution.py:375
  24.3 2.4 %collective-permute-start.4 = (bf16[196,1024]{1,0:T(8,128)(2,1)S(1)}, bf16[196,1024]{1,0:T(8,128)(2,1)S(1)}, u32[]{:S(2)}, u32[]{:S(2)}) collective-permute-start(bf16[196,1024]{1,0:T(8,128)(2,1)S(1)} %get-tuple-element.23.g_own.g0), channel_id=1, source_target_pairs={{0,1},{1,0},{2,3},{3,2},{4,5},{5,4},{6,7},{7,6},{8,9},{9,8},{10,11... | collective-permute-start | bytes 1204232 | tf_op jit(solution)/shard_map/ppermute | solution.py:375
  26.7 0.0 collective-permute-done.x
  26.7 2.3 %shard_map.105 = bf16[196,1024]{1,0:T(8,128)(2,1)S(1)} custom-call(bf16[196,1024]{1,0:T(8,128)(2,1)S(1)} %collective-permute-done.x, bf16[1024,1024]{1,0:T(8,128)(2,1)S(1)} %get-tuple-element.18.weight, f32[25,8,128]{2,1,0:T(8,128)S(1)} %get-tuple-element.19.taps, bf16[196,16,128]{2,1,0:T(8,128)(2,1)} %bitcast.39, ...), custom_call_target="tpu_custom_call" | custom-call | bytes 8388608 | tf_op jit(solution)/shard_map/pallas_call | solution.py:332
  29.0 5.4 %collective-permute-done.2.g_in = bf16[196,1024]{1,0:T(8,128)(2,1)S(1)} collective-permute-done((bf16[196,1024]{1,0:T(8,128)(2,1)S(1)}, bf16[196,1024]{1,0:T(8,128)(2,1)S(1)}, u32[]{:S(2)}, u32[]{:S(2)}) %collective-permute-start.2) | collective-permute-done | bytes 401440 | tf_op jit(solution)/shard_map/ppermute | solution.py:371
  34.4 1.9 %collective-permute-start.5 = (bf16[196,1024]{1,0:T(8,128)(2,1)S(1)}, bf16[196,1024]{1,0:T(8,128)(2,1)S(1)}, u32[]{:S(2)}, u32[]{:S(2)}) collective-permute-start(bf16[196,1024]{1,0:T(8,128)(2,1)S(1)} %shard_map.107.g_own.g.g1), channel_id=1, source_target_pairs={{0,1},{1,0},{2,3},{3,2},{4,5},{5,4},{6,7},{7,6},{8,9},{9,8},{10,11... | collective-permute-start | bytes 1204232 | tf_op jit(solution)/shard_map/ppermute | solution.py:375
  36.4 4.6 %collective-permute-start.1 = (bf16[196,1024]{1,0:T(8,128)(2,1)S(1)}, bf16[196,1024]{1,0:T(8,128)(2,1)S(1)}, u32[]{:S(2)}, u32[]{:S(2)}) collective-permute-start(bf16[196,1024]{1,0:T(8,128)(2,1)S(1)} %shard_map.105), channel_id=1, source_target_pairs={{0,4},{4,8},{8,12},{12,16},{16,20},{20,24},{24,28},{28,32},{32,36}... | collective-permute-start | bytes 1204232 | tf_op jit(solution)/shard_map/ppermute | solution.py:371
  40.9 0.0 collective-permute-done.4.g_peer.g0_peer
  40.9 0.0 collective-permute-done.3.peer
  41.0 0.7 shard_map.108.total
  41.7 0.0 collective-permute-done.5.g_peer.g1_peer
  41.7 0.7 shard_map.109
  42.5 2.0 %collective-permute-start.7 = (bf16[256,1024]{1,0:T(8,128)(2,1)S(1)}, bf16[256,1024]{1,0:T(8,128)(2,1)S(1)}, u32[]{:S(2)}, u32[]{:S(2)}) collective-permute-start(bf16[256,1024]{1,0:T(8,128)(2,1)S(1)} %get-tuple-element.25.token), channel_id=1, source_target_pairs={{0,2},{2,0},{1,3},{3,1},{4,6},{6,4},{5,7},{7,5},{8,10},{10,8},{9,1... | collective-permute-start | bytes 1572872 | tf_op jit(solution)/shard_map/ppermute | solution.py:379
  44.5 3.6 %shard_map.110 = bf16[196,1024]{1,0:T(8,128)(2,1)S(1)} custom-call(bf16[196,1024]{1,0:T(8,128)(2,1)S(1)} %shard_map.107.g_own.g.g1, bf16[196,16,128]{2,1,0:T(8,128)(2,1)} %bitcast.38, bf16[1024,1024]{1,0:T(8,128)(2,1)S(1)} %get-tuple-element.18.weight, f32[25,8,128]{2,1,0:T(8,128)S(1)} %get-tuple-element.19.taps, bf16[256,1024]{1,0:T(8,128)(2,1)S(1)} %get-tuple-element.25.token), custom_call_target="tpu_custom_call" | custom-call | bytes 1024 | tf_op jit(solution)/shard_map/pallas_call | solution.py:332
  48.1 1.9 %collective-permute-start.6 = (bf16[196,1024]{1,0:T(8,128)(2,1)S(1)}, bf16[196,1024]{1,0:T(8,128)(2,1)S(1)}, u32[]{:S(2)}, u32[]{:S(2)}) collective-permute-start(bf16[196,1024]{1,0:T(8,128)(2,1)S(1)} %shard_map.110), channel_id=1, source_target_pairs={{4,0},{8,4},{12,8},{16,12},{20,16},{24,20},{28,24},{32,28},{36,32}... | collective-permute-start | bytes 1204232 | tf_op jit(solution)/shard_map/ppermute | solution.py:371
  50.0 20.9 %collective-permute-done.1.message = bf16[196,1024]{1,0:T(8,128)(2,1)S(1)} collective-permute-done((bf16[196,1024]{1,0:T(8,128)(2,1)S(1)}, bf16[196,1024]{1,0:T(8,128)(2,1)S(1)}, u32[]{:S(2)}, u32[]{:S(2)}) %collective-permute-start.1) | collective-permute-done | bytes 401440 | tf_op jit(solution)/shard_map/ppermute | solution.py:371
  70.9 0.9 %shard_map.106.token = bf16[14,14,1024]{2,1,0:T(8,128)(2,1)} custom-call(bf16[196,1024]{1,0:T(8,128)(2,1)S(1)} %collective-permute-done.1.message, bf16[196,16,128]{2,1,0:T(8,128)(2,1)} %bitcast.40), custom_call_target="tpu_custom_call" | custom-call | bytes 1024 | tf_op jit(solution)/shard_map/pallas_call | solution.py:332
  71.8 4.7 %shard_map.113 = (f32[25,256]{1,0:T(8,128)S(1)}, bf16[25,256]{1,0:T(8,128)(2,1)S(1)}) custom-call(bf16[196,1024]{1,0:T(8,128)(2,1)S(1)} %get-tuple-element.27.keep_rect, bf16[196,2048]{1,0:T(8,128)(2,1)S(1)} %collective-permute-done.3.peer, bf16[196,1024]{1,0:T(8,128)(2,1)S(1)} %get-tuple-element.23.g_own.g0, ...), custom_call_target="tpu_custom_call" | custom-call | bytes 1024 | tf_op jit(solution)/shard_map/pallas_call | solution.py:332
  76.5 2.0 %collective-permute-start.8 = (bf16[25,256]{1,0:T(8,128)(2,1)S(1)}, bf16[25,256]{1,0:T(8,128)(2,1)S(1)}, u32[]{:S(2)}, u32[]{:S(2)}) collective-permute-start(bf16[25,256]{1,0:T(8,128)(2,1)S(1)} %get-tuple-element.29), channel_id=1, source_target_pairs={{0,2},{2,0},{1,3},{3,1},{4,6},{6,4},{5,7},{7,5},{8,10},{10,8},{9,1... | collective-permute-start | bytes 38408 | tf_op jit(solution)/shard_map/ppermute | solution.py:379
  78.6 7.5 %collective-permute-done.8 = bf16[25,256]{1,0:T(8,128)(2,1)S(1)} collective-permute-done((bf16[25,256]{1,0:T(8,128)(2,1)S(1)}, bf16[25,256]{1,0:T(8,128)(2,1)S(1)}, u32[]{:S(2)}, u32[]{:S(2)}) %collective-permute-start.8) | collective-permute-done | bytes 12832 | tf_op jit(solution)/shard_map/ppermute | solution.py:379
  86.1 0.6 copy.15
  86.7 0.0 collective-permute-done.6.message
  86.7 0.9 %shard_map.111 = bf16[14,14,1024]{2,1,0:T(8,128)(2,1)} custom-call(bf16[196,1024]{1,0:T(8,128)(2,1)S(1)} %collective-permute-done.6.message, bf16[196,16,128]{2,1,0:T(8,128)(2,1)} %bitcast.42), custom_call_target="tpu_custom_call" | custom-call | bytes 1024 | tf_op jit(solution)/shard_map/pallas_call | solution.py:332
  87.6 0.0 collective-permute-done.7.arrived
  87.7 1.1 %shard_map.112 = f32[256,1024]{1,0:T(8,128)} custom-call(f32[256,1024]{1,0:T(8,128)S(1)} %get-tuple-element.26.own, bf16[256,1024]{1,0:T(8,128)(2,1)S(1)} %collective-permute-done.7.arrived), custom_call_target="tpu_custom_call" | custom-call | bytes 1024 | tf_op jit(solution)/shard_map/pallas_call | solution.py:332
  (2 shorter events, 0.0 us)
Async XLA Ops:
  4.1 22.6 %collective-permute-start = (bf16[196,1024]{1,0:T(8,128)(2,1)S(1)}, bf16[196,1024]{1,0:T(8,128)(2,1)S(1)}, u32[]{:S(2)}, u32[]{:S(2)}) collective-permute-start(bf16[196,1024]{1,0:T(8,128)(2,1)S(1)} %get-tuple-element.17.token), channel_id=1, source_target_pairs={{0,4},{4,8},{8,12},{12,16},{16,20},{20,24},{24,28},{28,32},{32,36}... | collective-permute-start | bytes 1204232 | tf_op jit(solution)/shard_map/ppermute | solution.py:371
  15.6 18.8 %collective-permute-start.2 = (bf16[196,1024]{1,0:T(8,128)(2,1)S(1)}, bf16[196,1024]{1,0:T(8,128)(2,1)S(1)}, u32[]{:S(2)}, u32[]{:S(2)}) collective-permute-start(bf16[196,1024]{1,0:T(8,128)(2,1)S(1)} %get-tuple-element.20.token), channel_id=1, source_target_pairs={{4,0},{8,4},{12,8},{16,12},{20,16},{24,20},{28,24},{32,28},{36,32}... | collective-permute-start | bytes 1204232 | tf_op jit(solution)/shard_map/ppermute | solution.py:371
  22.4 18.6 %collective-permute-start.3 = (bf16[196,2048]{1,0:T(8,128)(2,1)S(1)}, bf16[196,2048]{1,0:T(8,128)(2,1)S(1)}, u32[]{:S(2)}, u32[]{:S(2)}) collective-permute-start(bf16[196,2048]{1,0:T(8,128)(2,1)S(1)} %get-tuple-element.24), channel_id=1, source_target_pairs={{0,1},{1,0},{2,3},{3,2},{4,5},{5,4},{6,7},{7,6},{8,9},{9,8},{10,11... | collective-permute-start | bytes 2408456 | tf_op jit(solution)/shard_map/ppermute | solution.py:375
  24.3 16.6 %collective-permute-start.4 = (bf16[196,1024]{1,0:T(8,128)(2,1)S(1)}, bf16[196,1024]{1,0:T(8,128)(2,1)S(1)}, u32[]{:S(2)}, u32[]{:S(2)}) collective-permute-start(bf16[196,1024]{1,0:T(8,128)(2,1)S(1)} %get-tuple-element.23.g_own.g0), channel_id=1, source_target_pairs={{0,1},{1,0},{2,3},{3,2},{4,5},{5,4},{6,7},{7,6},{8,9},{9,8},{10,11... | collective-permute-start | bytes 1204232 | tf_op jit(solution)/shard_map/ppermute | solution.py:375
  34.4 7.3 %collective-permute-start.5 = (bf16[196,1024]{1,0:T(8,128)(2,1)S(1)}, bf16[196,1024]{1,0:T(8,128)(2,1)S(1)}, u32[]{:S(2)}, u32[]{:S(2)}) collective-permute-start(bf16[196,1024]{1,0:T(8,128)(2,1)S(1)} %shard_map.107.g_own.g.g1), channel_id=1, source_target_pairs={{0,1},{1,0},{2,3},{3,2},{4,5},{5,4},{6,7},{7,6},{8,9},{9,8},{10,11... | collective-permute-start | bytes 1204232 | tf_op jit(solution)/shard_map/ppermute | solution.py:375
  36.4 34.5 %collective-permute-start.1 = (bf16[196,1024]{1,0:T(8,128)(2,1)S(1)}, bf16[196,1024]{1,0:T(8,128)(2,1)S(1)}, u32[]{:S(2)}, u32[]{:S(2)}) collective-permute-start(bf16[196,1024]{1,0:T(8,128)(2,1)S(1)} %shard_map.105), channel_id=1, source_target_pairs={{0,4},{4,8},{8,12},{12,16},{16,20},{20,24},{24,28},{28,32},{32,36}... | collective-permute-start | bytes 1204232 | tf_op jit(solution)/shard_map/ppermute | solution.py:371
  42.5 45.2 %collective-permute-start.7 = (bf16[256,1024]{1,0:T(8,128)(2,1)S(1)}, bf16[256,1024]{1,0:T(8,128)(2,1)S(1)}, u32[]{:S(2)}, u32[]{:S(2)}) collective-permute-start(bf16[256,1024]{1,0:T(8,128)(2,1)S(1)} %get-tuple-element.25.token), channel_id=1, source_target_pairs={{0,2},{2,0},{1,3},{3,1},{4,6},{6,4},{5,7},{7,5},{8,10},{10,8},{9,1... | collective-permute-start | bytes 1572872 | tf_op jit(solution)/shard_map/ppermute | solution.py:379
  48.1 38.7 %collective-permute-start.6 = (bf16[196,1024]{1,0:T(8,128)(2,1)S(1)}, bf16[196,1024]{1,0:T(8,128)(2,1)S(1)}, u32[]{:S(2)}, u32[]{:S(2)}) collective-permute-start(bf16[196,1024]{1,0:T(8,128)(2,1)S(1)} %shard_map.110), channel_id=1, source_target_pairs={{4,0},{8,4},{12,8},{16,12},{20,16},{24,20},{28,24},{32,28},{36,32}... | collective-permute-start | bytes 1204232 | tf_op jit(solution)/shard_map/ppermute | solution.py:371
  76.5 9.5 %collective-permute-start.8 = (bf16[25,256]{1,0:T(8,128)(2,1)S(1)}, bf16[25,256]{1,0:T(8,128)(2,1)S(1)}, u32[]{:S(2)}, u32[]{:S(2)}) collective-permute-start(bf16[25,256]{1,0:T(8,128)(2,1)S(1)} %get-tuple-element.29), channel_id=1, source_target_pairs={{0,2},{2,0},{1,3},{3,1},{4,6},{6,4},{5,7},{7,5},{8,10},{10,8},{9,1... | collective-permute-start | bytes 38408 | tf_op jit(solution)/shard_map/ppermute | solution.py:379

commit v3 on v2

--- a/solution.py
+++ b/solution.py
@@ -147,18 +147,10 @@
         mixed[:, cols(group)] = rows_of(dense, group).astype(bf16)
 
 
-def forward_first(x_hbm, w_hbm, taps_hbm, out, weight, taps, x, rows, padded, dense, mixed, sems):
-    copies = [
-        pltpu.make_async_copy(src, dst, sems.at[i])
-        for i, (src, dst) in enumerate([(x_hbm, x), (taps_hbm, taps), (w_hbm, weight)])
-    ]
-    for copy in copies:
-        copy.start()
-    copies[0].wait()
+def forward_first(x_hbm, weight, taps, token, out, x, rows, padded, dense, mixed, sem):
+    fetch(x_hbm, x, sem)
     pack_rows(x, rows)
-    copies[1].wait()
     mix(rows, padded, dense, mixed, taps)
-    copies[2].wait()
     out[...] = (rows[...] + jnp.dot(mixed[...], weight[...], preferred_element_type=f32)).astype(bf16)
 
 
@@ -169,7 +161,7 @@
     out[...] = (rows[...] + jnp.dot(mixed[...], weight[...], preferred_element_type=f32)).astype(bf16)
 
 
-def head_kernel(g_in, heads, g_out, pair, wide, rows, sem):
+def head_kernel(g_in, heads, token, g_out, pair, wide, rows, sem):
     @pl.when(is_last())
     def _():
         fetch(heads, pair, sem)
@@ -201,20 +193,24 @@
 
 
 def backward_first(
-    g_hbm, saved, weight, taps, token, out, g_rows, g, rows, grad_mixed, dense, mask, pair, wide, sems
+    g_hbm, saved, w_hbm, taps_hbm, out, g_rows, weight, taps, g, rows, grad_mixed, dense, mask, pair, wide, sems
 ):
     copies = [
         pltpu.make_async_copy(src, dst, sems.at[i])
-        for i, (src, dst) in enumerate([(g_hbm, g), (saved, pair)])
+        for i, (src, dst) in enumerate(
+            [(g_hbm, g), (w_hbm, weight), (saved, pair), (taps_hbm, taps)]
+        )
     ]
     for copy in copies:
         copy.start()
     copies[0].wait()
     pack_rows(g, rows)
     g_rows[...] = rows[...].astype(bf16)
+    copies[1].wait()
     spread_grad(g_rows, weight, grad_mixed)
-    copies[1].wait()
+    copies[2].wait()
     widen_pair(pair, wide)
+    copies[3].wait()
     finish_backward(0, taps, wide, out, grad_mixed, rows, dense, mask)
 
 
@@ -386,48 +382,43 @@
     image_pair = pair_view(images[:, 0, 0])
     head_pair = pair_view(head_grads[:, 0, 0])
 
-    out0, w, t = call(
+    grad_in0, g0, w, t = call(
+        backward_first,
+        [HBM] * 4,
+        (
+            MESSAGE,
+            MESSAGE,
+            jax.ShapeDtypeStruct((C, C), bf16),
+            jax.ShapeDtypeStruct((TAPS, GROUPS, LANES), f32),
+        ),
+        [TILED, ROWS, PADDED, DENSE, DENSE, PAIR, WIDE, sems(4)],
+        (incoming[0, 0, 0], saved_pair, weight, taps),
+    )
+    g1 = shifted(grad_in0, -1)
+    out0 = call(
         forward_first,
-        [HBM] * 3,
-        (MESSAGE, jax.ShapeDtypeStruct((C, C), bf16), jax.ShapeDtypeStruct((TAPS, GROUPS, LANES), f32)),
-        [TILED, ROWS, PADDED, DENSE, MIXED, sems(3)],
-        (activations[0, 0, 0], weight, taps),
+        [HBM, VMEM, VMEM, ANY],
+        MESSAGE,
+        [TILED, ROWS, PADDED, DENSE, MIXED, sems(1)],
+        (activations[0, 0, 0], w, t, grad_in0),
     )
     act1 = shifted(out0, 1)
-    grad_in0, g0 = call(
-        backward_first,
-        [HBM] * 2 + [VMEM, VMEM, ANY],
-        (MESSAGE, MESSAGE),
-        [TILED, ROWS, PADDED, DENSE, DENSE, PAIR, WIDE, sems(2)],
-        (incoming[0, 0, 0], saved_pair, w, t, out0),
-    )
-    g1 = shifted(grad_in0, -1)
     keep, send, keep_rect = call(
         factors_kernel,
         [HBM, VMEM, ANY],
         (MESSAGE, jax.ShapeDtypeStruct((PIX, 2 * C), bf16), MESSAGE),
         [ROWS, PADDED, DENSE, PAIR, WIDE, sems(1)],
-        (saved_pair, t, grad_in0),
+        (saved_pair, t, out0),
     )
     peer = other_core(send)
     g0_peer = other_core(g0)
 
-    out1 = call(
-        forward_second,
-        [VMEM] * 3 + [HBM, ANY],
-        MESSAGE,
-        [ROWS, PADDED, DENSE, MIXED, PAIR, WIDE, sems(1)],
-        (act1, w, t, image_pair, keep),
-        8192,
-    )
-    act2 = shifted(out1, 1)
-    g1, _ = lax.optimization_barrier((g1, out1))
     g1 = call(
         head_kernel,
-        [ANY, HBM],
+        [ANY, HBM, ANY],
         MESSAGE,
         [PAIR, WIDE, MIXED, sems(1)],
-        (g1, head_pair),
+        (g1, head_pair, act1),
         outs=ANY,
         input_output_aliases={0: 0},
     )
@@ -447,12 +438,20 @@
         (total, keep, g1, peer, g1_peer),
     )
     arrived = other_chip(other)
+    out1 = call(
+        forward_second,
+        [VMEM] * 3 + [HBM, ANY],
+        MESSAGE,
+        [ROWS, PADDED, DENSE, MIXED, PAIR, WIDE, sems(1)],
+        (act1, w, t, image_pair, other),
+    )
+    act2 = shifted(out1, 1)
     grad_in1 = call(
         backward_second,
         [VMEM, HBM, VMEM, VMEM, ANY],
         MESSAGE,
         [ROWS, PADDED, DENSE, DENSE, PAIR, WIDE, sems(1)],
-        (g1, saved_pair, w, t, other),
+        (g1, saved_pair, w, t, out1),
     )
     g2 = shifted(grad_in1, -1)
 
@@ -465,10 +464,10 @@
     )
     own_k, far_k = call(
         taps_kernel,
-        [VMEM] * 7 + [HBM],
+        [VMEM] * 7 + [ANY],
         (jax.ShapeDtypeStruct((TAPS, QUARTER), f32), jax.ShapeDtypeStruct((TAPS, QUARTER), bf16)),
         [PADDED, PADDED, pltpu.VMEM((32, HALF), f32)],
-        (keep_rect, peer, g0, g0_peer, g1, g1_peer, w, act_out),
+        (keep_rect, peer, g0, g0_peer, g1, g1_peer, w, grad_in1),
     )
     scale = 1.0 / (lax.axis_size("dp") * TICKS)
     k_grad = (own_k + other_chip(far_k).astype(f32)) * scale

time: 89.3 us -> 92.7 us (1.038)
  the two profiles are of different devices: /device:TPU:254 before, /device:TPU:1 now
where the time goes in v3:
time: 92.7 us; the launch traced here: 91.3 us
  starting transfers between devices  37.3 us (40%)
  Pallas kernels  30.7 us (33%)
  waiting for transfers between devices  21.9 us (24%)
    pallas_call x12, Pallas kernels, call(): pl.pallas_call(kernel, in_specs=ins, out_specs=jax.tree.map(lambda _: VME...  30.7 us
    ppermute x2, waiting for transfers between devices, other_chip(): return lax.ppermute(value, 'dp', [(0, 2), (2, 0), (1, 3), (3, 1)])  21.3 us
    ppermute x3, starting transfers between devices, other_core(): return lax.ppermute(value, 'dp', [(0, 1), (1, 0), (2, 3), (3, 2)])  16.8 us
    ppermute x4, starting transfers between devices, shifted(): return lax.ppermute(value, 'section', pairs)  11.3 us
    ppermute x2, starting transfers between devices, other_chip(): return lax.ppermute(value, 'dp', [(0, 2), (2, 0), (1, 3), (3, 1)])  9.19 us
  transfers between devices with their start and end apart: 9, of which 2 were waited for; matrix products, arithmetic and copies ran while one was open for 1% of the time, Pallas kernels for 27%

profile of v3, /device:TPU:1, one launch (start us, length us, event | category | flops | bytes accessed | tf_op | source)
XLA Modules:
  0.0 91.3 jit_solution(16126921757774563711)
XLA Ops:
  0.6 4.4 %shard_map.102 = (bf16[196,1024]{1,0:T(8,128)(2,1)S(1)}, bf16[196,1024]{1,0:T(8,128)(2,1)S(1)}, bf16[1024,1024]{1,0:T(8,128)(2,1)S(1)}, f32[25,8,128]{2,1,0:T(8,128)S(1)}) custom-call(bf16[14,14,1024]{2,1,0:T(8,128)(2,1)} %bitcast.47, bf16[196,16,128]{2,1,0:T(8,128)(2,1)} %bitcast.36, bf16[1024,1024]{1,0:T(8,128)(2,1)} %bitcast.43, f32[25,8,128]{2,1,0:T(8,128)} %bitcast.49), custom_call_target="tpu_custom_call" | custom-call | bytes 1024 | tf_op jit(solution)/shard_map/pallas_call | solution.py:328
  5.0 1.3 %collective-permute-start.3 = (bf16[196,1024]{1,0:T(8,128)(2,1)S(1)}, bf16[196,1024]{1,0:T(8,128)(2,1)S(1)}, u32[]{:S(2)}, u32[]{:S(2)}) collective-permute-start(bf16[196,1024]{1,0:T(8,128)(2,1)S(1)} %get-tuple-element.17.token), channel_id=1, source_target_pairs={{4,0},{8,4},{12,8},{16,12},{20,16},{24,20},{28,24},{32,28},{36,32}... | collective-permute-start | bytes 1204232 | tf_op jit(solution)/shard_map/ppermute | solution.py:367
  6.3 3.3 %shard_map.103.token = bf16[196,1024]{1,0:T(8,128)(2,1)S(1)} custom-call(bf16[14,14,1024]{2,1,0:T(8,128)(2,1)} %bitcast.48, bf16[1024,1024]{1,0:T(8,128)(2,1)S(1)} %get-tuple-element.15.weight, f32[25,8,128]{2,1,0:T(8,128)S(1)} %get-tuple-element.16.taps, bf16[196,1024]{1,0:T(8,128)(2,1)S(1)} %get-tuple-element.17.token), custom_call_target="tpu_custom_call" | custom-call | bytes 1024 | tf_op jit(solution)/shard_map/pallas_call | solution.py:328
  9.7 4.7 %collective-permute-start = (bf16[196,1024]{1,0:T(8,128)(2,1)S(1)}, bf16[196,1024]{1,0:T(8,128)(2,1)S(1)}, u32[]{:S(2)}, u32[]{:S(2)}) collective-permute-start(bf16[196,1024]{1,0:T(8,128)(2,1)S(1)} %shard_map.103.token), channel_id=1, source_target_pairs={{0,4},{4,8},{8,12},{12,16},{16,20},{20,24},{24,28},{28,32},{32,36}... | collective-permute-start | bytes 1204232 | tf_op jit(solution)/shard_map/ppermute | solution.py:367
  14.4 4.8 %shard_map.104 = (bf16[196,1024]{1,0:T(8,128)(2,1)S(1)}, bf16[196,2048]{1,0:T(8,128)(2,1)S(1)}, bf16[196,1024]{1,0:T(8,128)(2,1)S(1)}) custom-call(bf16[196,16,128]{2,1,0:T(8,128)(2,1)} %bitcast.37, f32[25,8,128]{2,1,0:T(8,128)S(1)} %get-tuple-element.16.taps, bf16[196,1024]{1,0:T(8,128)(2,1)S(1)} %shard_map.103.token), custom_call_target="tpu_custom_call" | custom-call | bytes 1024 | tf_op jit(solution)/shard_map/pallas_call | solution.py:328
  19.2 12.3 %collective-permute-start.1 = (bf16[196,2048]{1,0:T(8,128)(2,1)S(1)}, bf16[196,2048]{1,0:T(8,128)(2,1)S(1)}, u32[]{:S(2)}, u32[]{:S(2)}) collective-permute-start(bf16[196,2048]{1,0:T(8,128)(2,1)S(1)} %get-tuple-element.20), channel_id=1, source_target_pairs={{0,1},{1,0},{2,3},{3,2},{4,5},{5,4},{6,7},{7,6},{8,9},{9,8},{10,11... | collective-permute-start | bytes 2408456 | tf_op jit(solution)/shard_map/ppermute | solution.py:371
  31.5 1.9 %collective-permute-start.2 = (bf16[196,1024]{1,0:T(8,128)(2,1)S(1)}, bf16[196,1024]{1,0:T(8,128)(2,1)S(1)}, u32[]{:S(2)}, u32[]{:S(2)}) collective-permute-start(bf16[196,1024]{1,0:T(8,128)(2,1)S(1)} %get-tuple-element.19.g_own.g0), channel_id=1, source_target_pairs={{0,1},{1,0},{2,3},{3,2},{4,5},{5,4},{6,7},{7,6},{8,9},{9,8},{10,11... | collective-permute-start | bytes 1204232 | tf_op jit(solution)/shard_map/ppermute | solution.py:371
  33.5 0.0 collective-permute-done.token.x
  33.5 0.0 collective-permute-done.3.g_in
  33.5 2.6 %collective-permute-start.4 = (bf16[196,1024]{1,0:T(8,128)(2,1)S(1)}, bf16[196,1024]{1,0:T(8,128)(2,1)S(1)}, u32[]{:S(2)}, u32[]{:S(2)}) collective-permute-start(bf16[196,1024]{1,0:T(8,128)(2,1)S(1)} %shard_map.106.g_own.g.g1), channel_id=1, source_target_pairs={{0,1},{1,0},{2,3},{3,2},{4,5},{5,4},{6,7},{7,6},{8,9},{9,8},{10,11... | collective-permute-start | bytes 1204232 | tf_op jit(solution)/shard_map/ppermute | solution.py:371
  36.1 0.0 collective-permute-done.2.g_peer.g0_peer
  36.1 0.0 collective-permute-done.1.peer
  36.1 0.7 shard_map.105.total
  36.9 0.6 collective-permute-done.4.g_peer.g1_peer
  37.5 0.7 shard_map.107
  38.2 3.2 %collective-permute-start.7 = (bf16[256,1024]{1,0:T(8,128)(2,1)S(1)}, bf16[256,1024]{1,0:T(8,128)(2,1)S(1)}, u32[]{:S(2)}, u32[]{:S(2)}) collective-permute-start(bf16[256,1024]{1,0:T(8,128)(2,1)S(1)} %get-tuple-element.21.token), channel_id=1, source_target_pairs={{0,2},{2,0},{1,3},{3,1},{4,6},{6,4},{5,7},{7,5},{8,10},{10,8},{9,1... | collective-permute-start | bytes 1572872 | tf_op jit(solution)/shard_map/ppermute | solution.py:375
  41.4 3.9 %shard_map.108.token = bf16[196,1024]{1,0:T(8,128)(2,1)S(1)} custom-call(bf16[196,1024]{1,0:T(8,128)(2,1)S(1)} %collective-permute-done.token.x, bf16[1024,1024]{1,0:T(8,128)(2,1)S(1)} %get-tuple-element.15.weight, f32[25,8,128]{2,1,0:T(8,128)S(1)} %get-tuple-element.16.taps, bf16[196,16,128]{2,1,0:T(8,128)(2,1)} %bitcast.39, ...), custom_call_target="tpu_custom_call" | custom-call | bytes 1024 | tf_op jit(solution)/shard_map/pallas_call | solution.py:328
  45.3 3.6 %shard_map.110.token = bf16[196,1024]{1,0:T(8,128)(2,1)S(1)} custom-call(bf16[196,1024]{1,0:T(8,128)(2,1)S(1)} %shard_map.106.g_own.g.g1, bf16[196,16,128]{2,1,0:T(8,128)(2,1)} %bitcast.38, bf16[1024,1024]{1,0:T(8,128)(2,1)S(1)} %get-tuple-element.15.weight, f32[25,8,128]{2,1,0:T(8,128)S(1)} %get-tuple-element.16.taps, bf16[196,1024]{1,0:T(8,128)(2,1)S(1)} %shard_map.108.token), custom_call_target="tpu_custom_call" | custom-call | bytes 1024 | tf_op jit(solution)/shard_map/pallas_call | solution.py:328
  48.9 1.3 %collective-permute-start.6 = (bf16[196,1024]{1,0:T(8,128)(2,1)S(1)}, bf16[196,1024]{1,0:T(8,128)(2,1)S(1)}, u32[]{:S(2)}, u32[]{:S(2)}) collective-permute-start(bf16[196,1024]{1,0:T(8,128)(2,1)S(1)} %shard_map.110.token), channel_id=1, source_target_pairs={{4,0},{8,4},{12,8},{16,12},{20,16},{24,20},{28,24},{32,28},{36,32}... | collective-permute-start | bytes 1204232 | tf_op jit(solution)/shard_map/ppermute | solution.py:367
  50.2 4.0 %collective-permute-start.5 = (bf16[196,1024]{1,0:T(8,128)(2,1)S(1)}, bf16[196,1024]{1,0:T(8,128)(2,1)S(1)}, u32[]{:S(2)}, u32[]{:S(2)}) collective-permute-start(bf16[196,1024]{1,0:T(8,128)(2,1)S(1)} %shard_map.108.token), channel_id=1, source_target_pairs={{0,4},{4,8},{8,12},{12,16},{16,20},{20,24},{24,28},{28,32},{32,36}... | collective-permute-start | bytes 1204232 | tf_op jit(solution)/shard_map/ppermute | solution.py:367
  54.2 4.7 %shard_map.113 = (f32[25,256]{1,0:T(8,128)S(1)}, bf16[25,256]{1,0:T(8,128)(2,1)S(1)}) custom-call(bf16[196,1024]{1,0:T(8,128)(2,1)S(1)} %get-tuple-element.23.keep_rect, bf16[196,2048]{1,0:T(8,128)(2,1)S(1)} %collective-permute-done.1.peer, bf16[196,1024]{1,0:T(8,128)(2,1)S(1)} %get-tuple-element.19.g_own.g0, ...), custom_call_target="tpu_custom_call" | custom-call | bytes 1024 | tf_op jit(solution)/shard_map/pallas_call | solution.py:328
  58.9 6.0 %collective-permute-start.8 = (bf16[25,256]{1,0:T(8,128)(2,1)S(1)}, bf16[25,256]{1,0:T(8,128)(2,1)S(1)}, u32[]{:S(2)}, u32[]{:S(2)}) collective-permute-start(bf16[25,256]{1,0:T(8,128)(2,1)S(1)} %get-tuple-element.25), channel_id=1, source_target_pairs={{0,2},{2,0},{1,3},{3,1},{4,6},{6,4},{5,7},{7,5},{8,10},{10,8},{9,1... | collective-permute-start | bytes 38408 | tf_op jit(solution)/shard_map/ppermute | solution.py:375
  64.9 21.3 %collective-permute-done.8 = bf16[25,256]{1,0:T(8,128)(2,1)S(1)} collective-permute-done((bf16[25,256]{1,0:T(8,128)(2,1)S(1)}, bf16[25,256]{1,0:T(8,128)(2,1)S(1)}, u32[]{:S(2)}, u32[]{:S(2)}) %collective-permute-start.8) | collective-permute-done | bytes 12832 | tf_op jit(solution)/shard_map/ppermute | solution.py:375
  86.2 0.6 copy.15
  86.8 0.0 collective-permute-done.6.message
  86.8 0.9 shard_map.111
  87.7 0.0 collective-permute-done.5.message
  87.7 2.5 %shard_map.109 = bf16[14,14,1024]{2,1,0:T(8,128)(2,1)} custom-call(bf16[196,1024]{1,0:T(8,128)(2,1)S(1)} %collective-permute-done.5.message, bf16[196,16,128]{2,1,0:T(8,128)(2,1)} %bitcast.40), custom_call_target="tpu_custom_call" | custom-call | bytes 1024 | tf_op jit(solution)/shard_map/pallas_call | solution.py:328
  90.2 0.0 collective-permute-done.7.arrived
  90.2 1.1 %shard_map.112 = f32[256,1024]{1,0:T(8,128)} custom-call(f32[256,1024]{1,0:T(8,128)S(1)} %get-tuple-element.22.own, bf16[256,1024]{1,0:T(8,128)(2,1)S(1)} %collective-permute-done.7.arrived), custom_call_target="tpu_custom_call" | custom-call | bytes 1024 | tf_op jit(solution)/shard_map/pallas_call | solution.py:328
  (2 shorter events, 0.0 us)
Async XLA Ops:
  5.0 28.4 %collective-permute-start.3 = (bf16[196,1024]{1,0:T(8,128)(2,1)S(1)}, bf16[196,1024]{1,0:T(8,128)(2,1)S(1)}, u32[]{:S(2)}, u32[]{:S(2)}) collective-permute-start(bf16[196,1024]{1,0:T(8,128)(2,1)S(1)} %get-tuple-element.17.token), channel_id=1, source_target_pairs={{4,0},{8,4},{12,8},{16,12},{20,16},{24,20},{28,24},{32,28},{36,32}... | collective-permute-start | bytes 1204232 | tf_op jit(solution)/shard_map/ppermute | solution.py:367
  9.7 23.8 %collective-permute-start = (bf16[196,1024]{1,0:T(8,128)(2,1)S(1)}, bf16[196,1024]{1,0:T(8,128)(2,1)S(1)}, u32[]{:S(2)}, u32[]{:S(2)}) collective-permute-start(bf16[196,1024]{1,0:T(8,128)(2,1)S(1)} %shard_map.103.token), channel_id=1, source_target_pairs={{0,4},{4,8},{8,12},{12,16},{16,20},{20,24},{24,28},{28,32},{32,36}... | collective-permute-start | bytes 1204232 | tf_op jit(solution)/shard_map/ppermute | solution.py:367
  19.2 16.9 %collective-permute-start.1 = (bf16[196,2048]{1,0:T(8,128)(2,1)S(1)}, bf16[196,2048]{1,0:T(8,128)(2,1)S(1)}, u32[]{:S(2)}, u32[]{:S(2)}) collective-permute-start(bf16[196,2048]{1,0:T(8,128)(2,1)S(1)} %get-tuple-element.20), channel_id=1, source_target_pairs={{0,1},{1,0},{2,3},{3,2},{4,5},{5,4},{6,7},{7,6},{8,9},{9,8},{10,11... | collective-permute-start | bytes 2408456 | tf_op jit(solution)/shard_map/ppermute | solution.py:371
  31.5 4.6 %collective-permute-start.2 = (bf16[196,1024]{1,0:T(8,128)(2,1)S(1)}, bf16[196,1024]{1,0:T(8,128)(2,1)S(1)}, u32[]{:S(2)}, u32[]{:S(2)}) collective-permute-start(bf16[196,1024]{1,0:T(8,128)(2,1)S(1)} %get-tuple-element.19.g_own.g0), channel_id=1, source_target_pairs={{0,1},{1,0},{2,3},{3,2},{4,5},{5,4},{6,7},{7,6},{8,9},{9,8},{10,11... | collective-permute-start | bytes 1204232 | tf_op jit(solution)/shard_map/ppermute | solution.py:371
  33.5 3.9 %collective-permute-start.4 = (bf16[196,1024]{1,0:T(8,128)(2,1)S(1)}, bf16[196,1024]{1,0:T(8,128)(2,1)S(1)}, u32[]{:S(2)}, u32[]{:S(2)}) collective-permute-start(bf16[196,1024]{1,0:T(8,128)(2,1)S(1)} %shard_map.106.g_own.g.g1), channel_id=1, source_target_pairs={{0,1},{1,0},{2,3},{3,2},{4,5},{5,4},{6,7},{7,6},{8,9},{9,8},{10,11... | collective-permute-start | bytes 1204232 | tf_op jit(solution)/shard_map/ppermute | solution.py:371
  38.2 52.0 %collective-permute-start.7 = (bf16[256,1024]{1,0:T(8,128)(2,1)S(1)}, bf16[256,1024]{1,0:T(8,128)(2,1)S(1)}, u32[]{:S(2)}, u32[]{:S(2)}) collective-permute-start(bf16[256,1024]{1,0:T(8,128)(2,1)S(1)} %get-tuple-element.21.token), channel_id=1, source_target_pairs={{0,2},{2,0},{1,3},{3,1},{4,6},{6,4},{5,7},{7,5},{8,10},{10,8},{9,1... | collective-permute-start | bytes 1572872 | tf_op jit(solution)/shard_map/ppermute | solution.py:375
  48.9 37.9 %collective-permute-start.6 = (bf16[196,1024]{1,0:T(8,128)(2,1)S(1)}, bf16[196,1024]{1,0:T(8,128)(2,1)S(1)}, u32[]{:S(2)}, u32[]{:S(2)}) collective-permute-start(bf16[196,1024]{1,0:T(8,128)(2,1)S(1)} %shard_map.110.token), channel_id=1, source_target_pairs={{4,0},{8,4},{12,8},{16,12},{20,16},{24,20},{28,24},{32,28},{36,32}... | collective-permute-start | bytes 1204232 | tf_op jit(solution)/shard_map/ppermute | solution.py:367
  50.2 37.5 %collective-permute-start.5 = (bf16[196,1024]{1,0:T(8,128)(2,1)S(1)}, bf16[196,1024]{1,0:T(8,128)(2,1)S(1)}, u32[]{:S(2)}, u32[]{:S(2)}) collective-permute-start(bf16[196,1024]{1,0:T(8,128)(2,1)S(1)} %shard_map.108.token), channel_id=1, source_target_pairs={{0,4},{4,8},{8,12},{12,16},{16,20},{20,24},{24,28},{28,32},{32,36}... | collective-permute-start | bytes 1204232 | tf_op jit(solution)/shard_map/ppermute | solution.py:367
  58.9 27.2 %collective-permute-start.8 = (bf16[25,256]{1,0:T(8,128)(2,1)S(1)}, bf16[25,256]{1,0:T(8,128)(2,1)S(1)}, u32[]{:S(2)}, u32[]{:S(2)}) collective-permute-start(bf16[25,256]{1,0:T(8,128)(2,1)S(1)} %get-tuple-element.25), channel_id=1, source_target_pairs={{0,2},{2,0},{1,3},{3,1},{4,6},{6,4},{5,7},{7,5},{8,10},{10,8},{9,1... | collective-permute-start | bytes 38408 | tf_op jit(solution)/shard_map/ppermute | solution.py:375

commit v4 on v3

--- a/solution.py
+++ b/solution.py
@@ -147,8 +147,7 @@
         mixed[:, cols(group)] = rows_of(dense, group).astype(bf16)
 
 
-def forward_first(x_hbm, weight, taps, token, out, x, rows, padded, dense, mixed, sem):
-    fetch(x_hbm, x, sem)
+def forward_first(x, weight, taps, token, out, rows, padded, dense, mixed):
     pack_rows(x, rows)
     mix(rows, padded, dense, mixed, taps)
     out[...] = (rows[...] + jnp.dot(mixed[...], weight[...], preferred_element_type=f32)).astype(bf16)
@@ -171,18 +170,22 @@
         fetch(rows, g_out, sem)
 
 
-def spread_grad(g, weight, grad_mixed):
-    product = lax.dot_general(
-        g[...], weight[...], (((1,), (1,)), ((), ())), preferred_element_type=f32
-    )
+def spread_grad(g, weight, grad_mixed, waits=()):
     zero_pad(grad_mixed)
-    for group in range(GROUPS):
-        spread_rows(grad_mixed, group, product[:, cols(group)])
-
-
-def finish_backward(tick, taps, wide, out, grad_mixed, rows, dense, mask):
-    mask[...] = pair_tick_spread(wide, tick)
-
+    for block in range(4):
+        if waits:
+            waits[block].wait()
+        product = lax.dot_general(
+            g[...],
+            weight[block * QUARTER : (block + 1) * QUARTER, :],
+            (((1,), (1,)), ((), ())),
+            preferred_element_type=f32,
+        )
+        for part in range(2):
+            spread_rows(grad_mixed, 2 * block + part, product[:, cols(part)])
+
+
+def finish_backward(taps, out, grad_mixed, rows, dense, mask):
     def emit(pixel, value):
         keep = tile_at(mask, pixel) > 0.0
         store_tile(dense)(pixel, jnp.where(keep, value, 0.0))
@@ -193,13 +196,14 @@
 
 
 def backward_first(
-    g_hbm, saved, w_hbm, taps_hbm, out, g_rows, weight, taps, g, rows, grad_mixed, dense, mask, pair, wide, sems
+    g_hbm, saved, w_hbm, taps_hbm, x_hbm, out, g_rows, weight, taps, pair, x, g, rows, grad_mixed, dense, mask, wide, sems
 ):
+    blocks = [slice(block * QUARTER, (block + 1) * QUARTER) for block in range(4)]
+    pieces = [(g_hbm, g), (saved, pair)]
+    pieces += [(w_hbm.at[rows_, :], weight.at[rows_, :]) for rows_ in blocks]
+    pieces += [(taps_hbm, taps), (x_hbm, x)]
     copies = [
-        pltpu.make_async_copy(src, dst, sems.at[i])
-        for i, (src, dst) in enumerate(
-            [(g_hbm, g), (w_hbm, weight), (saved, pair), (taps_hbm, taps)]
-        )
+        pltpu.make_async_copy(src, dst, sems.at[i]) for i, (src, dst) in enumerate(pieces)
     ]
     for copy in copies:
         copy.start()
@@ -207,60 +211,48 @@
     pack_rows(g, rows)
     g_rows[...] = rows[...].astype(bf16)
     copies[1].wait()
-    spread_grad(g_rows, weight, grad_mixed)
-    copies[2].wait()
     widen_pair(pair, wide)
-    copies[3].wait()
-    finish_backward(0, taps, wide, out, grad_mixed, rows, dense, mask)
-
-
-def backward_second(
-    g, saved, weight, taps, token, out, rows, grad_mixed, dense, mask, pair, wide, sem
-):
-    copy = pltpu.make_async_copy(saved, pair, sem)
-    copy.start()
+    mask[...] = pair_tick_spread(wide, 0)
+    spread_grad(g_rows, weight, grad_mixed, copies[2:6])
+    copies[6].wait()
+    finish_backward(taps, out, grad_mixed, rows, dense, mask)
+    copies[7].wait()
+
+
+def backward_second(g, pair, weight, taps, token, out, rows, grad_mixed, dense, mask, wide):
+    widen_pair(pair, wide)
+    mask[...] = pair_tick_spread(wide, 1)
     rows[...] = g[...].astype(f32)
     spread_grad(g, weight, grad_mixed)
-    copy.wait()
-    widen_pair(pair, wide)
-    finish_backward(1, taps, wide, out, grad_mixed, rows, dense, mask)
-
-
-def halves(core):
-    return [2 * core, 2 * core + 1, 4 + 2 * core, 5 + 2 * core]
-
-
-def factors_kernel(saved, taps, token, keep, send, keep_rect, rows, padded, dense, pair, wide, sem):
+    finish_backward(taps, out, grad_mixed, rows, dense, mask)
+
+
+def factors_kernel(pair, g_rows, taps, token, keep, send, padded, dense, wide):
     core = lax.rem(lax.axis_index("dp"), 2)
     high = lax.div(lax.axis_index("dp"), 2)
-    fetch(saved, pair, sem)
     widen_pair(pair, wide)
+    send[:, C : 2 * C] = g_rows[...]
     zero_pad(padded)
     for tick in range(TICKS):
         padded[TOP : TOP + DENSE_ROWS, :] = jnp.maximum(pair_tick_spread(wide, tick), 0.0)
-        for at, (mine, theirs) in enumerate(zip(halves(core), halves(1 - core))):
-            place = tick * HALF + at * LANES
-            keep_rect[:, place : place + LANES] = rows_of(padded, TOP + mine).astype(bf16)
-            send[:, C + place : C + place + LANES] = rows_of(padded, TOP + theirs).astype(bf16)
         conv(padded, taps, store_tile(dense), False)
-        for group in range(GROUPS):
-            rows[:, cols(group)] = rows_of(dense, group)
         for place in range(2):
             side = high if place == 0 else 1 - high
-            at = tick * HALF + place * QUARTER
-            own = pl.multiple_of((side * 2 + core) * QUARTER, QUARTER)
-            other = pl.multiple_of((side * 2 + 1 - core) * QUARTER, QUARTER)
-            keep[:, at : at + QUARTER] = rows[:, pl.ds(own, QUARTER)].astype(bf16)
-            send[:, at : at + QUARTER] = rows[:, pl.ds(other, QUARTER)].astype(bf16)
+            for part in range(2):
+                at = tick * HALF + (2 * place + part) * LANES
+                mine = 4 * side + 2 * core + part
+                theirs = 4 * side + 2 * (1 - core) + part
+                keep[:, at : at + LANES] = rows_of(dense, mine).astype(bf16)
+                send[:, at : at + LANES] = rows_of(dense, theirs).astype(bf16)
 
 
 def weight_term(factor, grads):
     return lax.dot_general(factor, grads, (((0,), (0,)), ((), ())), preferred_element_type=f32)
 
 
-def weight_first(keep, g_own, peer, g_peer, out):
+def weight_first(keep, g_own, peer, out):
     out[...] = weight_term(keep[:, :HALF], g_own[...])
-    out[...] += weight_term(peer[:, :HALF], g_peer[...])
+    out[...] += weight_term(peer[:, :HALF], peer[:, C : 2 * C])
 
 
 def weight_second(total, keep, g_own, peer, g_peer, own, other):
@@ -275,36 +267,30 @@
             other[...] = value.astype(bf16)
 
 
-def taps_kernel(keep_rect, peer, g0, g0_peer, g1, g1_peer, weight, token, own, far, rect, grad, sums):
+def taps_kernel(pair, g0, g1, weight, token, own, core_out, chip_out, both_out, rect, grad, sums, wide):
     core = lax.rem(lax.axis_index("dp"), 2)
     high = lax.div(lax.axis_index("dp"), 2)
+    widen_pair(pair, wide)
     zero_pad(rect)
-    zero_pad(grad)
-    sums[...] = jnp.zeros_like(sums)
     for tick in range(TICKS):
-        grads = (g0, g1)[tick][...], (g0_peer, g1_peer)[tick][...]
-        for image in range(2):
-            for side in range(2):
-                rows = weight[pl.ds(pl.multiple_of((2 * side + core) * QUARTER, QUARTER), QUARTER), :]
-                product = lax.dot_general(
-                    grads[image], rows, (((1,), (1,)), ((), ())), preferred_element_type=f32
-                )
-                for part in range(2):
-                    at = 2 * side + part
-                    spread_rows(grad, 4 * image + at, product[:, cols(part)])
-                    place = tick * HALF + at * LANES
-                    source = keep_rect if image == 0 else peer
-                    place += 0 if image == 0 else C
-                    spread_rows(rect, 4 * image + at, source[:, place : place + LANES].astype(f32))
+        rect[TOP : TOP + DENSE_ROWS, :] = jnp.maximum(pair_tick_spread(wide, tick), 0.0)
+        spread_grad((g0, g1)[tick], weight, grad)
         terms = tap_sums(rect, grad)
         for index in range(TAPS):
-            both = terms[index][0:4] + terms[index][4:8]
-            sums[index : index + 1, :HALF] += jnp.concatenate(
-                [both[i : i + 1] for i in range(4)], axis=1
-            )
-    low, top = sums[0:TAPS, 0:QUARTER], sums[0:TAPS, QUARTER:HALF]
-    own[...] = jnp.where(high == 0, low, top)
-    far[...] = jnp.where(high == 0, top, low).astype(bf16)
+            row = jnp.concatenate([terms[index][i : i + 1] for i in range(GROUPS)], axis=1)
+            if tick == 0:
+                sums[index : index + 1, :] = row
+            else:
+                sums[index : index + 1, :] += row
+
+    def block(side, which):
+        at = pl.multiple_of((2 * side + which) * QUARTER, QUARTER)
+        return sums[0:TAPS, pl.ds(at, QUARTER)]
+
+    own[...] = block(high, core)
+    core_out[...] = block(high, 1 - core).astype(bf16)
+    chip_out[...] = block(1 - high, core).astype(bf16)
+    both_out[...] = block(1 - high, 1 - core).astype(bf16)
 
 
 def final_kernel(own, arrived, out):
@@ -375,6 +361,10 @@
     return lax.ppermute(value, "dp", [(0, 2), (2, 0), (1, 3), (3, 1)])
 
 
+def other_both(value):
+    return lax.ppermute(value, "dp", [(0, 3), (3, 0), (1, 2), (2, 1)])
+
+
 def per_device(activations, incoming, saved, images, head_grads, pw_weight, dw_kernel):
     weight = pw_weight[0]
     taps = dw_kernel[0].reshape(TAPS, GROUPS, LANES)
@@ -382,53 +372,55 @@
     image_pair = pair_view(images[:, 0, 0])
     head_pair = pair_view(head_grads[:, 0, 0])
 
-    grad_in0, g0, w, t = call(
+    grad_in0, g0, w, t, pair, x0 = call(
         backward_first,
-        [HBM] * 4,
-        (
-            MESSAGE,
-            MESSAGE,
-            jax.ShapeDtypeStruct((C, C), bf16),
-            jax.ShapeDtypeStruct((TAPS, GROUPS, LANES), f32),
+        [HBM] * 5,
+        (MESSAGE, MESSAGE)
+        + tuple(
+            jax.ShapeDtypeStruct(shape, kind)
+            for shape, kind in (
+                ((C, C), bf16),
+                ((TAPS, GROUPS, LANES), f32),
+                (PAIR.shape, bf16),
+                (TILED.shape, bf16),
+            )
         ),
-        [TILED, ROWS, PADDED, DENSE, DENSE, PAIR, WIDE, sems(4)],
-        (incoming[0, 0, 0], saved_pair, weight, taps),
+        [TILED, ROWS, PADDED, DENSE, DENSE, WIDE, sems(8)],
+        (incoming[0, 0, 0], saved_pair, weight, taps, activations[0, 0, 0]),
     )
     g1 = shifted(grad_in0, -1)
+    keep, send = call(
+        factors_kernel,
+        [VMEM, VMEM, VMEM, ANY],
+        (MESSAGE, jax.ShapeDtypeStruct((PIX, 2 * C), bf16)),
+        [PADDED, DENSE, WIDE],
+        (pair, g0, t, grad_in0),
+    )
+    peer = other_core(send)
     out0 = call(
         forward_first,
-        [HBM, VMEM, VMEM, ANY],
+        [VMEM, VMEM, VMEM, ANY],
         MESSAGE,
-        [TILED, ROWS, PADDED, DENSE, MIXED, sems(1)],
-        (activations[0, 0, 0], w, t, grad_in0),
+        [ROWS, PADDED, DENSE, MIXED],
+        (x0, w, t, keep),
     )
     act1 = shifted(out0, 1)
-    keep, send, keep_rect = call(
-        factors_kernel,
-        [HBM, VMEM, ANY],
-        (MESSAGE, jax.ShapeDtypeStruct((PIX, 2 * C), bf16), MESSAGE),
-        [ROWS, PADDED, DENSE, PAIR, WIDE, sems(1)],
-        (saved_pair, t, out0),
-    )
-    peer = other_core(send)
-    g0_peer = other_core(g0)
-
     g1 = call(
         head_kernel,
         [ANY, HBM, ANY],
         MESSAGE,
         [PAIR, WIDE, MIXED, sems(1)],
-        (g1, head_pair, act1),
+        (g1, head_pair, out0),
         outs=ANY,
         input_output_aliases={0: 0},
     )
     g1_peer = other_core(g1)
     total = call(
         weight_first,
-        [VMEM] * 4,
+        [VMEM] * 3,
         jax.ShapeDtypeStruct((HALF, C), f32),
         [],
-        (keep, g0, peer, g0_peer),
+        (keep, g0, peer),
     )
     own, other = call(
         weight_second,
@@ -438,23 +430,34 @@
         (total, keep, g1, peer, g1_peer),
     )
     arrived = other_chip(other)
+    grad_in1 = call(
+        backward_second,
+        [VMEM, VMEM, VMEM, VMEM, ANY],
+        MESSAGE,
+        [ROWS, PADDED, DENSE, DENSE, WIDE],
+        (g1, pair, w, t, other),
+    )
+    g2 = shifted(grad_in1, -1)
     out1 = call(
         forward_second,
         [VMEM] * 3 + [HBM, ANY],
         MESSAGE,
         [ROWS, PADDED, DENSE, MIXED, PAIR, WIDE, sems(1)],
-        (act1, w, t, image_pair, other),
+        (act1, w, t, image_pair, grad_in1),
     )
     act2 = shifted(out1, 1)
-    grad_in1 = call(
-        backward_second,
-        [VMEM, HBM, VMEM, VMEM, ANY],
-        MESSAGE,
-        [ROWS, PADDED, DENSE, DENSE, PAIR, WIDE, sems(1)],
-        (g1, saved_pair, w, t, out1),
-    )
-    g2 = shifted(grad_in1, -1)
-
+
+    small = jax.ShapeDtypeStruct((TAPS, QUARTER), bf16)
+    own_k, core_k, chip_k, both_k = call(
+        taps_kernel,
+        [VMEM] * 4 + [ANY],
+        (jax.ShapeDtypeStruct((TAPS, QUARTER), f32), small, small, small),
+        [PADDED, PADDED, pltpu.VMEM((32, C), f32), WIDE],
+        (pair, g0, g1, w, out1),
+    )
+    scale = 1.0 / (lax.axis_size("dp") * TICKS)
+    far_k = other_chip(chip_k).astype(f32) + other_both(both_k).astype(f32)
+    k_grad = (own_k + other_core(core_k).astype(f32) + far_k) * scale
     act_out = call(
         functools.partial(unpack_kernel, is_first),
         [VMEM, HBM],
@@ -462,15 +465,6 @@
         [ROWS, PAIR, WIDE, sems(1)],
         (act2, image_pair),
     )
-    own_k, far_k = call(
-        taps_kernel,
-        [VMEM] * 7 + [ANY],
-        (jax.ShapeDtypeStruct((TAPS, QUARTER), f32), jax.ShapeDtypeStruct((TAPS, QUARTER), bf16)),
-        [PADDED, PADDED, pltpu.VMEM((32, HALF), f32)],
-        (keep_rect, peer, g0, g0_peer, g1, g1_peer, w, grad_in1),
-    )
-    scale = 1.0 / (lax.axis_size("dp") * TICKS)
-    k_grad = (own_k + other_chip(far_k).astype(f32)) * scale
     grad_out = call(
         functools.partial(unpack_kernel, is_last),
         [VMEM, HBM],

time: 92.7 us -> 90.6 us (0.977)
  the two profiles are of different devices: /device:TPU:1 before, /device:TPU:527 now
where the time goes in v4:
time: 90.6 us; the launch traced here: 90.2 us
  starting transfers between devices  50.1 us (55%)
  Pallas kernels  24.5 us (27%)
  waiting for transfers between devices  14.1 us (16%)
    ppermute x4, starting transfers between devices, shifted(): return lax.ppermute(value, 'section', pairs)  25.3 us
    pallas_call x12, Pallas kernels, call(): pl.pallas_call(kernel, in_specs=ins, out_specs=jax.tree.map(lambda _: VME...  24.5 us
    ppermute x2, waiting for transfers between devices, other_chip(): return lax.ppermute(value, 'dp', [(0, 2), (2, 0), (1, 3), (3, 1)])  11.9 us
    ppermute x2, starting transfers between devices, other_chip(): return lax.ppermute(value, 'dp', [(0, 2), (2, 0), (1, 3), (3, 1)])  10.4 us
    ppermute x3, starting transfers between devices, other_core(): return lax.ppermute(value, 'dp', [(0, 1), (1, 0), (2, 3), (3, 2)])  9.7 us
    ppermute x1, starting transfers between devices, other_both(): return lax.ppermute(value, 'dp', [(0, 3), (3, 0), (1, 2), (2, 1)])  4.61 us
    ppermute x4, waiting for transfers between devices, shifted(): return lax.ppermute(value, 'section', pairs)  1.86 us
  transfers between devices with their start and end apart: 10, of which 4 were waited for; matrix products, arithmetic and copies ran while one was open for 1% of the time, Pallas kernels for 21%

profile of v4, /device:TPU:527, one launch (start us, length us, event | category | flops | bytes accessed | tf_op | source)
XLA Modules:
  0.0 90.2 jit_solution(11659634746409696190)
XLA Ops:
  0.6 4.9 %shard_map.102 = (bf16[196,1024]{1,0:T(8,128)(2,1)S(1)}, bf16[196,1024]{1,0:T(8,128)(2,1)S(1)}, bf16[1024,1024]{1,0:T(8,128)(2,1)S(1)}, f32[25,8,128]{2,1,0:T(8,...) custom-call(bf16[14,14,1024]{2,1,0:T(8,128)(2,1)} %bitcast.43, ...), custom_call_target="tpu_custom_call" | custom-call | bytes 1024 | tf_op jit(solution)/shard_map/pallas_call | solution.py:314
  5.5 2.1 %collective-permute-start.1 = (bf16[196,1024]{1,0:T(8,128)(2,1)S(1)}, bf16[196,1024]{1,0:T(8,128)(2,1)S(1)}, u32[]{:S(2)}, u32[]{:S(2)}) collective-permute-start(bf16[196,1024]{1,0:T(8,128)(2,1)S(1)} %get-tuple-element.23.token), channel_id=1, source_target_pairs={{4,0},{8,4},{12,8},{16,12},{20,16},{24,20},{28,24},{32,28},{36,32}... | collective-permute-start | bytes 1204232 | tf_op jit(solution)/shard_map/ppermute | solution.py:353
  7.6 3.3 %shard_map.103 = (bf16[196,1024]{1,0:T(8,128)(2,1)S(1)}, bf16[196,2048]{1,0:T(8,128)(2,1)S(1)}) custom-call(bf16[196,16,128]{2,1,0:T(8,128)(2,1)S(1)} %get-tuple-element.21.pair, bf16[196,1024]{1,0:T(8,128)(2,1)S(1)} %get-tuple-element.22.g_rows.g_own.g0, f32[25,8,128]{2,1,0:T(8,128)S(1)} %get-tuple-element.20.taps, ...), custom_call_target="tpu_custom_call" | custom-call | bytes 1024 | tf_op jit(solution)/shard_map/pallas_call | solution.py:314
  10.9 2.9 %collective-permute-start.2 = (bf16[196,2048]{1,0:T(8,128)(2,1)S(1)}, bf16[196,2048]{1,0:T(8,128)(2,1)S(1)}, u32[]{:S(2)}, u32[]{:S(2)}) collective-permute-start(bf16[196,2048]{1,0:T(8,128)(2,1)S(1)} %get-tuple-element.25), channel_id=1, source_target_pairs={{0,1},{1,0},{2,3},{3,2},{4,5},{5,4},{6,7},{7,6},{8,9},{9,8},{10,11... | collective-permute-start | bytes 2408456 | tf_op jit(solution)/shard_map/ppermute | solution.py:357
  13.8 2.3 %shard_map.104.token = bf16[196,1024]{1,0:T(8,128)(2,1)S(1)} custom-call(bf16[14,14,1024]{2,1,0:T(8,128)(2,1)S(1)} %get-tuple-element.18.x, bf16[1024,1024]{1,0:T(8,128)(2,1)S(1)} %get-tuple-element.19.weight, f32[25,8,128]{2,1,0:T(8,128)S(1)} %get-tuple-element.20.taps, bf16[196,1024]{1,0:T(8,128)(2,1)S(1)} %get-tuple-element.24.token.keep), custom_call_target="tpu_custom_call" | custom-call | bytes 1024 | tf_op jit(solution)/shard_map/pallas_call | solution.py:314
  16.1 1.7 %collective-permute-done.1.g_in = bf16[196,1024]{1,0:T(8,128)(2,1)S(1)} collective-permute-done((bf16[196,1024]{1,0:T(8,128)(2,1)S(1)}, bf16[196,1024]{1,0:T(8,128)(2,1)S(1)}, u32[]{:S(2)}, u32[]{:S(2)}) %collective-permute-start.1) | collective-permute-done | bytes 401440 | tf_op jit(solution)/shard_map/ppermute | solution.py:353
  17.8 3.5 %collective-permute-start.3 = (bf16[196,1024]{1,0:T(8,128)(2,1)S(1)}, bf16[196,1024]{1,0:T(8,128)(2,1)S(1)}, u32[]{:S(2)}, u32[]{:S(2)}) collective-permute-start(bf16[196,1024]{1,0:T(8,128)(2,1)S(1)} %shard_map.105.g_own.g.g1), channel_id=1, source_target_pairs={{0,1},{1,0},{2,3},{3,2},{4,5},{5,4},{6,7},{7,6},{8,9},{9,8},{10,11... | collective-permute-start | bytes 1204232 | tf_op jit(solution)/shard_map/ppermute | solution.py:357
  21.2 3.2 %collective-permute-start = (bf16[196,1024]{1,0:T(8,128)(2,1)S(1)}, bf16[196,1024]{1,0:T(8,128)(2,1)S(1)}, u32[]{:S(2)}, u32[]{:S(2)}) collective-permute-start(bf16[196,1024]{1,0:T(8,128)(2,1)S(1)} %shard_map.104.token), channel_id=1, source_target_pairs={{0,4},{4,8},{8,12},{12,16},{16,20},{20,24},{24,28},{28,32},{32,36}... | collective-permute-start | bytes 1204232 | tf_op jit(solution)/shard_map/ppermute | solution.py:353
  24.4 0.0 collective-permute-done.2.peer
  24.5 0.7 shard_map.106.total
  25.2 0.0 collective-permute-done.3.g_peer
  25.2 0.7 shard_map.107
  26.0 5.7 %collective-permute-start.6 = (bf16[256,1024]{1,0:T(8,128)(2,1)S(1)}, bf16[256,1024]{1,0:T(8,128)(2,1)S(1)}, u32[]{:S(2)}, u32[]{:S(2)}) collective-permute-start(bf16[256,1024]{1,0:T(8,128)(2,1)S(1)} %get-tuple-element.26.token), channel_id=1, source_target_pairs={{0,2},{2,0},{1,3},{3,1},{4,6},{6,4},{5,7},{7,5},{8,10},{10,8},{9,1... | collective-permute-start | bytes 1572872 | tf_op jit(solution)/shard_map/ppermute | solution.py:361
  31.6 2.6 %shard_map.108.token = bf16[196,1024]{1,0:T(8,128)(2,1)S(1)} custom-call(bf16[196,1024]{1,0:T(8,128)(2,1)S(1)} %shard_map.105.g_own.g.g1, bf16[196,16,128]{2,1,0:T(8,128)(2,1)S(1)} %get-tuple-element.21.pair, bf16[1024,1024]{1,0:T(8,128)(2,1)S(1)} %get-tuple-element.19.weight, f32[25,8,128]{2,1,0:T(8,128)S(1)} %get-tuple-element.20.taps, ...), custom_call_target="tpu_custom_call" | custom-call | bytes 1024 | tf_op jit(solution)/shard_map/pallas_call | solution.py:314
  34.3 0.2 collective-permute-done.x
  34.4 2.3 %shard_map.109.token = bf16[196,1024]{1,0:T(8,128)(2,1)S(1)} custom-call(bf16[196,1024]{1,0:T(8,128)(2,1)S(1)} %collective-permute-done.x, bf16[1024,1024]{1,0:T(8,128)(2,1)S(1)} %get-tuple-element.19.weight, f32[25,8,128]{2,1,0:T(8,128)S(1)} %get-tuple-element.20.taps, bf16[196,16,128]{2,1,0:T(8,128)(2,1)} %bitcast.36, bf16[196,1024]{1,0:T(8,128)(2,1)S(1)} %shard_map.108.token), custom_call_target="tpu_custom_call" | custom-call | bytes 1024 | tf_op jit(solution)/shard_map/pallas_call | solution.py:314
  36.7 18.1 %collective-permute-start.4 = (bf16[196,1024]{1,0:T(8,128)(2,1)S(1)}, bf16[196,1024]{1,0:T(8,128)(2,1)S(1)}, u32[]{:S(2)}, u32[]{:S(2)}) collective-permute-start(bf16[196,1024]{1,0:T(8,128)(2,1)S(1)} %shard_map.109.token), channel_id=1, source_target_pairs={{0,4},{4,8},{8,12},{12,16},{16,20},{20,24},{24,28},{28,32},{32,36}... | collective-permute-start | bytes 1204232 | tf_op jit(solution)/shard_map/ppermute | solution.py:353
  54.8 1.9 %collective-permute-start.5 = (bf16[196,1024]{1,0:T(8,128)(2,1)S(1)}, bf16[196,1024]{1,0:T(8,128)(2,1)S(1)}, u32[]{:S(2)}, u32[]{:S(2)}) collective-permute-start(bf16[196,1024]{1,0:T(8,128)(2,1)S(1)} %shard_map.108.token), channel_id=1, source_target_pairs={{4,0},{8,4},{12,8},{16,12},{20,16},{24,20},{28,24},{32,28},{36,32}... | collective-permute-start | bytes 1204232 | tf_op jit(solution)/shard_map/ppermute | solution.py:353
  56.8 4.8 %shard_map.113 = (f32[25,256]{1,0:T(8,128)S(1)}, bf16[25,256]{1,0:T(8,128)(2,1)S(1)}, bf16[25,256]{1,0:T(8,128)(2,1)S(1)}, bf16[25,256]{1,0:T(8,128)(2,1)S(1)}) custom-call(bf16[196,16,128]{2,1,0:T(8,128)(2,1)S(1)} %get-tuple-element.21.pair, bf16[196,1024]{1,0:T(8,128)(2,1)S(1)} %get-tuple-element.22.g_rows.g_own.g0, ...), custom_call_target="tpu_custom_call" | custom-call | bytes 1024 | tf_op jit(solution)/shard_map/pallas_call | solution.py:314
  61.6 3.4 %collective-permute-start.7 = (bf16[25,256]{1,0:T(8,128)(2,1)S(1)}, bf16[25,256]{1,0:T(8,128)(2,1)S(1)}, u32[]{:S(2)}, u32[]{:S(2)}) collective-permute-start(bf16[25,256]{1,0:T(8,128)(2,1)S(1)} %get-tuple-element.29), channel_id=1, source_target_pairs={{0,1},{1,0},{2,3},{3,2},{4,5},{5,4},{6,7},{7,6},{8,9},{9,8},{10,11... | collective-permute-start | bytes 38408 | tf_op jit(solution)/shard_map/ppermute | solution.py:357
  64.9 4.8 %collective-permute-start.8 = (bf16[25,256]{1,0:T(8,128)(2,1)S(1)}, bf16[25,256]{1,0:T(8,128)(2,1)S(1)}, u32[]{:S(2)}, u32[]{:S(2)}) collective-permute-start(bf16[25,256]{1,0:T(8,128)(2,1)S(1)} %get-tuple-element.30), channel_id=1, source_target_pairs={{0,2},{2,0},{1,3},{3,1},{4,6},{6,4},{5,7},{7,5},{8,10},{10,8},{9,1... | collective-permute-start | bytes 38408 | tf_op jit(solution)/shard_map/ppermute | solution.py:361
  69.7 0.0 collective-permute-done.7
  69.7 4.6 %collective-permute-start.9 = (bf16[25,256]{1,0:T(8,128)(2,1)S(1)}, bf16[25,256]{1,0:T(8,128)(2,1)S(1)}, u32[]{:S(2)}, u32[]{:S(2)}) collective-permute-start(bf16[25,256]{1,0:T(8,128)(2,1)S(1)} %get-tuple-element.31), channel_id=1, source_target_pairs={{0,3},{3,0},{1,2},{2,1},{4,7},{7,4},{5,6},{6,5},{8,11},{11,8},{9,1... | collective-permute-start | bytes 38408 | tf_op jit(solution)/shard_map/ppermute | solution.py:365
  74.3 11.9 %collective-permute-done.8 = bf16[25,256]{1,0:T(8,128)(2,1)S(1)} collective-permute-done((bf16[25,256]{1,0:T(8,128)(2,1)S(1)}, bf16[25,256]{1,0:T(8,128)(2,1)S(1)}, u32[]{:S(2)}, u32[]{:S(2)}) %collective-permute-start.8) | collective-permute-done | bytes 12832 | tf_op jit(solution)/shard_map/ppermute | solution.py:361
  86.2 0.4 collective-permute-done.9
  86.6 0.6 copy.15
  87.2 0.0 collective-permute-done.4.message
  87.2 0.9 %shard_map.110 = bf16[14,14,1024]{2,1,0:T(8,128)(2,1)} custom-call(bf16[196,1024]{1,0:T(8,128)(2,1)S(1)} %collective-permute-done.4.message, bf16[196,16,128]{2,1,0:T(8,128)(2,1)} %bitcast.37), custom_call_target="tpu_custom_call" | custom-call | bytes 1024 | tf_op jit(solution)/shard_map/pallas_call | solution.py:314
  88.1 0.0 collective-permute-done.5.message
  88.2 0.9 %shard_map.111 = bf16[14,14,1024]{2,1,0:T(8,128)(2,1)} custom-call(bf16[196,1024]{1,0:T(8,128)(2,1)S(1)} %collective-permute-done.5.message, bf16[196,16,128]{2,1,0:T(8,128)(2,1)} %bitcast.39), custom_call_target="tpu_custom_call" | custom-call | bytes 1024 | tf_op jit(solution)/shard_map/pallas_call | solution.py:314
  89.1 0.0 collective-permute-done.6.arrived
  89.1 1.1 %shard_map.112 = f32[256,1024]{1,0:T(8,128)} custom-call(f32[256,1024]{1,0:T(8,128)S(1)} %get-tuple-element.27.own, bf16[256,1024]{1,0:T(8,128)(2,1)S(1)} %collective-permute-done.6.arrived), custom_call_target="tpu_custom_call" | custom-call | bytes 1024 | tf_op jit(solution)/shard_map/pallas_call | solution.py:314
  (2 shorter events, 0.0 us)
Async XLA Ops:
  5.5 12.2 %collective-permute-start.1 = (bf16[196,1024]{1,0:T(8,128)(2,1)S(1)}, bf16[196,1024]{1,0:T(8,128)(2,1)S(1)}, u32[]{:S(2)}, u32[]{:S(2)}) collective-permute-start(bf16[196,1024]{1,0:T(8,128)(2,1)S(1)} %get-tuple-element.23.token), channel_id=1, source_target_pairs={{4,0},{8,4},{12,8},{16,12},{20,16},{24,20},{28,24},{32,28},{36,32}... | collective-permute-start | bytes 1204232 | tf_op jit(solution)/shard_map/ppermute | solution.py:353
  10.9 13.5 %collective-permute-start.2 = (bf16[196,2048]{1,0:T(8,128)(2,1)S(1)}, bf16[196,2048]{1,0:T(8,128)(2,1)S(1)}, u32[]{:S(2)}, u32[]{:S(2)}) collective-permute-start(bf16[196,2048]{1,0:T(8,128)(2,1)S(1)} %get-tuple-element.25), channel_id=1, source_target_pairs={{0,1},{1,0},{2,3},{3,2},{4,5},{5,4},{6,7},{7,6},{8,9},{9,8},{10,11... | collective-permute-start | bytes 2408456 | tf_op jit(solution)/shard_map/ppermute | solution.py:357
  17.8 7.4 %collective-permute-start.3 = (bf16[196,1024]{1,0:T(8,128)(2,1)S(1)}, bf16[196,1024]{1,0:T(8,128)(2,1)S(1)}, u32[]{:S(2)}, u32[]{:S(2)}) collective-permute-start(bf16[196,1024]{1,0:T(8,128)(2,1)S(1)} %shard_map.105.g_own.g.g1), channel_id=1, source_target_pairs={{0,1},{1,0},{2,3},{3,2},{4,5},{5,4},{6,7},{7,6},{8,9},{9,8},{10,11... | collective-permute-start | bytes 1204232 | tf_op jit(solution)/shard_map/ppermute | solution.py:357
  21.2 13.2 %collective-permute-start = (bf16[196,1024]{1,0:T(8,128)(2,1)S(1)}, bf16[196,1024]{1,0:T(8,128)(2,1)S(1)}, u32[]{:S(2)}, u32[]{:S(2)}) collective-permute-start(bf16[196,1024]{1,0:T(8,128)(2,1)S(1)} %shard_map.104.token), channel_id=1, source_target_pairs={{0,4},{4,8},{8,12},{12,16},{16,20},{20,24},{24,28},{28,32},{32,36}... | collective-permute-start | bytes 1204232 | tf_op jit(solution)/shard_map/ppermute | solution.py:353
  26.0 63.1 %collective-permute-start.6 = (bf16[256,1024]{1,0:T(8,128)(2,1)S(1)}, bf16[256,1024]{1,0:T(8,128)(2,1)S(1)}, u32[]{:S(2)}, u32[]{:S(2)}) collective-permute-start(bf16[256,1024]{1,0:T(8,128)(2,1)S(1)} %get-tuple-element.26.token), channel_id=1, source_target_pairs={{0,2},{2,0},{1,3},{3,1},{4,6},{6,4},{5,7},{7,5},{8,10},{10,8},{9,1... | collective-permute-start | bytes 1572872 | tf_op jit(solution)/shard_map/ppermute | solution.py:361
  36.7 50.5 %collective-permute-start.4 = (bf16[196,1024]{1,0:T(8,128)(2,1)S(1)}, bf16[196,1024]{1,0:T(8,128)(2,1)S(1)}, u32[]{:S(2)}, u32[]{:S(2)}) collective-permute-start(bf16[196,1024]{1,0:T(8,128)(2,1)S(1)} %shard_map.109.token), channel_id=1, source_target_pairs={{0,4},{4,8},{8,12},{12,16},{16,20},{20,24},{24,28},{28,32},{32,36}... | collective-permute-start | bytes 1204232 | tf_op jit(solution)/shard_map/ppermute | solution.py:353
  54.8 33.3 %collective-permute-start.5 = (bf16[196,1024]{1,0:T(8,128)(2,1)S(1)}, bf16[196,1024]{1,0:T(8,128)(2,1)S(1)}, u32[]{:S(2)}, u32[]{:S(2)}) collective-permute-start(bf16[196,1024]{1,0:T(8,128)(2,1)S(1)} %shard_map.108.token), channel_id=1, source_target_pairs={{4,0},{8,4},{12,8},{16,12},{20,16},{24,20},{28,24},{32,28},{36,32}... | collective-permute-start | bytes 1204232 | tf_op jit(solution)/shard_map/ppermute | solution.py:353
  61.6 8.2 %collective-permute-start.7 = (bf16[25,256]{1,0:T(8,128)(2,1)S(1)}, bf16[25,256]{1,0:T(8,128)(2,1)S(1)}, u32[]{:S(2)}, u32[]{:S(2)}) collective-permute-start(bf16[25,256]{1,0:T(8,128)(2,1)S(1)} %get-tuple-element.29), channel_id=1, source_target_pairs={{0,1},{1,0},{2,3},{3,2},{4,5},{5,4},{6,7},{7,6},{8,9},{9,8},{10,11... | collective-permute-start | bytes 38408 | tf_op jit(solution)/shard_map/ppermute | solution.py:357
  64.9 21.3 %collective-permute-start.8 = (bf16[25,256]{1,0:T(8,128)(2,1)S(1)}, bf16[25,256]{1,0:T(8,128)(2,1)S(1)}, u32[]{:S(2)}, u32[]{:S(2)}) collective-permute-start(bf16[25,256]{1,0:T(8,128)(2,1)S(1)} %get-tuple-element.30), channel_id=1, source_target_pairs={{0,2},{2,0},{1,3},{3,1},{4,6},{6,4},{5,7},{7,5},{8,10},{10,8},{9,1... | collective-permute-start | bytes 38408 | tf_op jit(solution)/shard_map/ppermute | solution.py:361
  69.7 16.8 %collective-permute-start.9 = (bf16[25,256]{1,0:T(8,128)(2,1)S(1)}, bf16[25,256]{1,0:T(8,128)(2,1)S(1)}, u32[]{:S(2)}, u32[]{:S(2)}) collective-permute-start(bf16[25,256]{1,0:T(8,128)(2,1)S(1)} %get-tuple-element.31), channel_id=1, source_target_pairs={{0,3},{3,0},{1,2},{2,1},{4,7},{7,4},{5,6},{6,5},{8,11},{11,8},{9,1... | collective-permute-start | bytes 38408 | tf_op jit(solution)/shard_map/ppermute | solution.py:365

commit v5 on v4

--- a/solution.py
+++ b/solution.py
@@ -12,6 +12,7 @@
 TICKS = 2
 HW = 14
 PIX = HW * HW
+PIX_ROWS = -(-PIX // 8) * 8
 C = 1024
 LANES = 128
 GROUPS = C // LANES
@@ -192,7 +193,7 @@
 
     conv(grad_mixed, taps, emit, True)
     for group in range(GROUPS):
-        out[:, cols(group)] = (rows[:, cols(group)] + rows_of(dense, group)).astype(bf16)
+        out[0:PIX, cols(group)] = (rows[:, cols(group)] + rows_of(dense, group)).astype(bf16)
 
 
 def backward_first(
@@ -224,6 +225,7 @@
     mask[...] = pair_tick_spread(wide, 1)
     rows[...] = g[...].astype(f32)
     spread_grad(g, weight, grad_mixed)
+    out[PIX:PIX_ROWS, :] = jnp.zeros((PIX_ROWS - PIX, C), bf16)
     finish_backward(taps, out, grad_mixed, rows, dense, mask)
 
 
@@ -293,12 +295,23 @@
     both_out[...] = block(1 - high, 1 - core).astype(bf16)
 
 
+SCALE = 1.0 / (2 * 2 * TICKS)
+
+
 def final_kernel(own, arrived, out):
-    out[...] = (own[...] + arrived[...].astype(f32)) * (1.0 / (2 * 2 * TICKS))
-
-
-def unpack_kernel(edge, message, images, out, rows, pair, wide, sem):
-    rows[...] = message[...].astype(f32)
+    out[...] = (own[...] + arrived[...].astype(f32)) * SCALE
+
+
+def taps_final(own, from_core, from_chip, from_both, out):
+    total = own[...] + from_core[...].astype(f32) + from_chip[...].astype(f32)
+    total = (total + from_both[...].astype(f32)) * SCALE
+    for part in range(2):
+        out[:, part, :] = total[:, cols(part)]
+
+
+def unpack_kernel(edge, message, images, token, out, packed, rows, pair, wide, sem):
+    fetch(message, packed, sem)
+    rows[...] = packed[0:PIX, :].astype(f32)
     replace_at_edge(edge(), images, 1, pair, wide, rows, sem)
     for p in range(HW):
         out[p] = rows[p * HW : (p + 1) * HW, :].astype(bf16)
@@ -336,6 +349,7 @@
 TILED = pltpu.VMEM((HW, HW, C), bf16)
 IMAGE = jax.ShapeDtypeStruct((HW, HW, C), bf16)
 MESSAGE = jax.ShapeDtypeStruct((PIX, C), bf16)
+LONGER = jax.ShapeDtypeStruct((PIX_ROWS, C), bf16)
 
 
 def sems(count):
@@ -433,48 +447,53 @@
     grad_in1 = call(
         backward_second,
         [VMEM, VMEM, VMEM, VMEM, ANY],
-        MESSAGE,
+        LONGER,
         [ROWS, PADDED, DENSE, DENSE, WIDE],
         (g1, pair, w, t, other),
     )
     g2 = shifted(grad_in1, -1)
-    out1 = call(
-        forward_second,
-        [VMEM] * 3 + [HBM, ANY],
-        MESSAGE,
-        [ROWS, PADDED, DENSE, MIXED, PAIR, WIDE, sems(1)],
-        (act1, w, t, image_pair, grad_in1),
-    )
-    act2 = shifted(out1, 1)
-
     small = jax.ShapeDtypeStruct((TAPS, QUARTER), bf16)
     own_k, core_k, chip_k, both_k = call(
         taps_kernel,
         [VMEM] * 4 + [ANY],
         (jax.ShapeDtypeStruct((TAPS, QUARTER), f32), small, small, small),
         [PADDED, PADDED, pltpu.VMEM((32, C), f32), WIDE],
-        (pair, g0, g1, w, out1),
-    )
-    scale = 1.0 / (lax.axis_size("dp") * TICKS)
-    far_k = other_chip(chip_k).astype(f32) + other_both(both_k).astype(f32)
-    k_grad = (own_k + other_core(core_k).astype(f32) + far_k) * scale
+        (pair, g0, g1, w, grad_in1),
+    )
+    out1 = call(
+        forward_second,
+        [VMEM] * 3 + [HBM, ANY],
+        MESSAGE,
+        [ROWS, PADDED, DENSE, MIXED, PAIR, WIDE, sems(1)],
+        (act1, w, t, image_pair, own_k),
+    )
+    act2 = shifted(out1, 1)
+
+    k_grad = call(
+        taps_final,
+        [VMEM] * 4,
+        jax.ShapeDtypeStruct((TAPS, 2, LANES), f32),
+        [],
+        (own_k, other_core(core_k), other_chip(chip_k), other_both(both_k)),
+    )
+    w_grad = call(
+        final_kernel, [VMEM, VMEM], jax.ShapeDtypeStruct((QUARTER, C), f32), [], (own, arrived)
+    )
+    grad_out = call(
+        functools.partial(unpack_kernel, is_last),
+        [ANY, HBM, HBM],
+        IMAGE,
+        [pltpu.VMEM((PIX_ROWS, C), bf16), ROWS, PAIR, WIDE, sems(1)],
+        (g2, head_pair, w_grad),
+    )
     act_out = call(
         functools.partial(unpack_kernel, is_first),
-        [VMEM, HBM],
+        [ANY, HBM, HBM],
         IMAGE,
-        [ROWS, PAIR, WIDE, sems(1)],
-        (act2, image_pair),
-    )
-    grad_out = call(
-        functools.partial(unpack_kernel, is_last),
-        [VMEM, HBM],
-        IMAGE,
-        [ROWS, PAIR, WIDE, sems(1)],
-        (g2, head_pair),
-    )
-    w_grad = call(
-        final_kernel, [VMEM, VMEM], jax.ShapeDtypeStruct((QUARTER, C), f32), [], (own, arrived)
-    )
+        [MIXED, ROWS, PAIR, WIDE, sems(1)],
+        (act2, image_pair, grad_out),
+    )
+    k_grad = k_grad.reshape(TAPS, QUARTER)
     return (act_out[None, None, None], grad_out[None, None, None], w_grad[None], k_grad[None])
 
 

time: 90.6 us -> 89 us (0.982)
  the two profiles are of different devices: /device:TPU:527 before, /device:TPU:1 now
where the time goes in v5:
time: 89 us; the launch traced here: 87.3 us
  starting transfers between devices  38.3 us (43%)
  Pallas kernels  28.8 us (32%)
  waiting for transfers between devices  19.4 us (22%)
    pallas_call x13, Pallas kernels, call(): pl.pallas_call(kernel, in_specs=ins, out_specs=jax.tree.map(lambda _: VME...  28.8 us
    ppermute x3, starting transfers between devices, other_core(): return lax.ppermute(value, 'dp', [(0, 1), (1, 0), (2, 3), (3, 2)])  18.6 us
    ppermute x2, waiting for transfers between devices, other_chip(): return lax.ppermute(value, 'dp', [(0, 2), (2, 0), (1, 3), (3, 1)])  17.7 us
    ppermute x2, starting transfers between devices, other_chip(): return lax.ppermute(value, 'dp', [(0, 2), (2, 0), (1, 3), (3, 1)])  9.46 us
    ppermute x4, starting transfers between devices, shifted(): return lax.ppermute(value, 'section', pairs)  8.29 us
    ppermute x1, starting transfers between devices, other_both(): return lax.ppermute(value, 'dp', [(0, 3), (3, 0), (1, 2), (2, 1)])  1.92 us
  transfers between devices with their start and end apart: 10, of which 2 were waited for; matrix products, arithmetic and copies ran while one was open for 0% of the time, Pallas kernels for 24%

profile of v5, /device:TPU:1, one launch (start us, length us, event | category | flops | bytes accessed | tf_op | source)
XLA Modules:
  0.0 87.3 jit_solution(15914751616361375091)
XLA Ops:
  0.6 4.9 %shard_map.102 = (bf16[196,1024]{1,0:T(8,128)(2,1)S(1)}, bf16[196,1024]{1,0:T(8,128)(2,1)S(1)}, bf16[1024,1024]{1,0:T(8,128)(2,1)S(1)}, f32[25,8,128]{2,1,0:T(8,...) custom-call(bf16[14,14,1024]{2,1,0:T(8,128)(2,1)} %bitcast.43, ...), custom_call_target="tpu_custom_call" | custom-call | bytes 1024 | tf_op jit(solution)/shard_map/pallas_call | solution.py:327
  5.5 1.3 %collective-permute-start.1 = (bf16[196,1024]{1,0:T(8,128)(2,1)S(1)}, bf16[196,1024]{1,0:T(8,128)(2,1)S(1)}, u32[]{:S(2)}, u32[]{:S(2)}) collective-permute-start(bf16[196,1024]{1,0:T(8,128)(2,1)S(1)} %get-tuple-element.23.token), channel_id=1, source_target_pairs={{4,0},{8,4},{12,8},{16,12},{20,16},{24,20},{28,24},{32,28},{36,32}... | collective-permute-start | bytes 1204232 | tf_op jit(solution)/shard_map/ppermute | solution.py:367
  6.8 3.3 %shard_map.103 = (bf16[196,1024]{1,0:T(8,128)(2,1)S(1)}, bf16[196,2048]{1,0:T(8,128)(2,1)S(1)}) custom-call(bf16[196,16,128]{2,1,0:T(8,128)(2,1)S(1)} %get-tuple-element.21.pair, bf16[196,1024]{1,0:T(8,128)(2,1)S(1)} %get-tuple-element.22.g_rows.g_own.g0, f32[25,8,128]{2,1,0:T(8,128)S(1)} %get-tuple-element.20.taps, ...), custom_call_target="tpu_custom_call" | custom-call | bytes 1024 | tf_op jit(solution)/shard_map/pallas_call | solution.py:327
  10.1 12.4 %collective-permute-start.2 = (bf16[196,2048]{1,0:T(8,128)(2,1)S(1)}, bf16[196,2048]{1,0:T(8,128)(2,1)S(1)}, u32[]{:S(2)}, u32[]{:S(2)}) collective-permute-start(bf16[196,2048]{1,0:T(8,128)(2,1)S(1)} %get-tuple-element.25), channel_id=1, source_target_pairs={{0,1},{1,0},{2,3},{3,2},{4,5},{5,4},{6,7},{7,6},{8,9},{9,8},{10,11... | collective-permute-start | bytes 2408456 | tf_op jit(solution)/shard_map/ppermute | solution.py:371
  22.5 2.3 %shard_map.104.token = bf16[196,1024]{1,0:T(8,128)(2,1)S(1)} custom-call(bf16[14,14,1024]{2,1,0:T(8,128)(2,1)S(1)} %get-tuple-element.18.x, bf16[1024,1024]{1,0:T(8,128)(2,1)S(1)} %get-tuple-element.19.weight, f32[25,8,128]{2,1,0:T(8,128)S(1)} %get-tuple-element.20.taps, bf16[196,1024]{1,0:T(8,128)(2,1)S(1)} %get-tuple-element.24.token.keep), custom_call_target="tpu_custom_call" | custom-call | bytes 1024 | tf_op jit(solution)/shard_map/pallas_call | solution.py:327
  24.8 0.0 collective-permute-done.1.g_in
  24.9 2.9 %collective-permute-start.3 = (bf16[196,1024]{1,0:T(8,128)(2,1)S(1)}, bf16[196,1024]{1,0:T(8,128)(2,1)S(1)}, u32[]{:S(2)}, u32[]{:S(2)}) collective-permute-start(bf16[196,1024]{1,0:T(8,128)(2,1)S(1)} %shard_map.105.g_own.g.g1), channel_id=1, source_target_pairs={{0,1},{1,0},{2,3},{3,2},{4,5},{5,4},{6,7},{7,6},{8,9},{9,8},{10,11... | collective-permute-start | bytes 1204232 | tf_op jit(solution)/shard_map/ppermute | solution.py:371
  27.8 3.3 %collective-permute-start = (bf16[196,1024]{1,0:T(8,128)(2,1)S(1)}, bf16[196,1024]{1,0:T(8,128)(2,1)S(1)}, u32[]{:S(2)}, u32[]{:S(2)}) collective-permute-start(bf16[196,1024]{1,0:T(8,128)(2,1)S(1)} %shard_map.104.token), channel_id=1, source_target_pairs={{0,4},{4,8},{8,12},{12,16},{16,20},{20,24},{24,28},{28,32},{32,36}... | collective-permute-start | bytes 1204232 | tf_op jit(solution)/shard_map/ppermute | solution.py:367
  31.1 0.0 collective-permute-done.2.peer
  31.1 0.7 shard_map.106.total
  31.9 0.0 collective-permute-done.3.g_peer
  31.9 0.7 shard_map.107
  32.6 1.9 %collective-permute-start.6 = (bf16[256,1024]{1,0:T(8,128)(2,1)S(1)}, bf16[256,1024]{1,0:T(8,128)(2,1)S(1)}, u32[]{:S(2)}, u32[]{:S(2)}) collective-permute-start(bf16[256,1024]{1,0:T(8,128)(2,1)S(1)} %get-tuple-element.26.token), channel_id=1, source_target_pairs={{0,2},{2,0},{1,3},{3,1},{4,6},{6,4},{5,7},{7,5},{8,10},{10,8},{9,1... | collective-permute-start | bytes 1572872 | tf_op jit(solution)/shard_map/ppermute | solution.py:375
  34.5 2.7 %shard_map.108.token = bf16[200,1024]{1,0:T(8,128)(2,1)S(1)} custom-call(bf16[196,1024]{1,0:T(8,128)(2,1)S(1)} %shard_map.105.g_own.g.g1, bf16[196,16,128]{2,1,0:T(8,128)(2,1)S(1)} %get-tuple-element.21.pair, bf16[1024,1024]{1,0:T(8,128)(2,1)S(1)} %get-tuple-element.19.weight, f32[25,8,128]{2,1,0:T(8,128)S(1)} %get-tuple-element.20.taps, ...), custom_call_target="tpu_custom_call" | custom-call | bytes 1024 | tf_op jit(solution)/shard_map/pallas_call | solution.py:327
  37.2 1.3 %collective-permute-start.5 = (bf16[200,1024]{1,0:T(8,128)(2,1)S(1)}, bf16[200,1024]{1,0:T(8,128)(2,1)S(1)}, u32[]{:S(2)}, u32[]{:S(2)}) collective-permute-start(bf16[200,1024]{1,0:T(8,128)(2,1)S(1)} %shard_map.108.token), channel_id=1, source_target_pairs={{4,0},{8,4},{12,8},{16,12},{20,16},{24,20},{28,24},{32,28},{36,32}... | collective-permute-start | bytes 1228808 | tf_op jit(solution)/shard_map/ppermute | solution.py:367
  38.5 4.8 %shard_map.109 = (f32[25,256]{1,0:T(8,128)S(1)}, bf16[25,256]{1,0:T(8,128)(2,1)S(1)}, bf16[25,256]{1,0:T(8,128)(2,1)S(1)}, bf16[25,256]{1,0:T(8,128)(2,1)S(1)}) custom-call(bf16[196,16,128]{2,1,0:T(8,128)(2,1)S(1)} %get-tuple-element.21.pair, bf16[196,1024]{1,0:T(8,128)(2,1)S(1)} %get-tuple-element.22.g_rows.g_own.g0, ...), custom_call_target="tpu_custom_call" | custom-call | bytes 1024 | tf_op jit(solution)/shard_map/pallas_call | solution.py:327
  43.3 0.0 collective-permute-done.x
  43.3 3.9 %shard_map.110 = bf16[196,1024]{1,0:T(8,128)(2,1)S(1)} custom-call(bf16[196,1024]{1,0:T(8,128)(2,1)S(1)} %collective-permute-done.x, bf16[1024,1024]{1,0:T(8,128)(2,1)S(1)} %get-tuple-element.19.weight, f32[25,8,128]{2,1,0:T(8,128)S(1)} %get-tuple-element.20.taps, bf16[196,16,128]{2,1,0:T(8,128)(2,1)} %bitcast.36, f32[25,256]{1,0:T(8,128)S(1)} %get-tuple-element.27.token.own), custom_call_target="tpu_custom_call" | custom-call | bytes 1024 | tf_op jit(solution)/shard_map/pallas_call | solution.py:327
  47.2 2.4 %collective-permute-start.4 = (bf16[196,1024]{1,0:T(8,128)(2,1)S(1)}, bf16[196,1024]{1,0:T(8,128)(2,1)S(1)}, u32[]{:S(2)}, u32[]{:S(2)}) collective-permute-start(bf16[196,1024]{1,0:T(8,128)(2,1)S(1)} %shard_map.110), channel_id=1, source_target_pairs={{0,4},{4,8},{8,12},{12,16},{16,20},{20,24},{24,28},{28,32},{32,36}... | collective-permute-start | bytes 1204232 | tf_op jit(solution)/shard_map/ppermute | solution.py:367
  49.6 3.3 %collective-permute-start.7 = (bf16[25,256]{1,0:T(8,128)(2,1)S(1)}, bf16[25,256]{1,0:T(8,128)(2,1)S(1)}, u32[]{:S(2)}, u32[]{:S(2)}) collective-permute-start(bf16[25,256]{1,0:T(8,128)(2,1)S(1)} %get-tuple-element.29), channel_id=1, source_target_pairs={{0,1},{1,0},{2,3},{3,2},{4,5},{5,4},{6,7},{7,6},{8,9},{9,8},{10,11... | collective-permute-start | bytes 38408 | tf_op jit(solution)/shard_map/ppermute | solution.py:371
  52.9 7.5 %collective-permute-start.8 = (bf16[25,256]{1,0:T(8,128)(2,1)S(1)}, bf16[25,256]{1,0:T(8,128)(2,1)S(1)}, u32[]{:S(2)}, u32[]{:S(2)}) collective-permute-start(bf16[25,256]{1,0:T(8,128)(2,1)S(1)} %get-tuple-element.30), channel_id=1, source_target_pairs={{0,2},{2,0},{1,3},{3,1},{4,6},{6,4},{5,7},{7,5},{8,10},{10,8},{9,1... | collective-permute-start | bytes 38408 | tf_op jit(solution)/shard_map/ppermute | solution.py:375
  60.4 0.0 collective-permute-done.7.from_core
  60.4 1.9 %collective-permute-start.9 = (bf16[25,256]{1,0:T(8,128)(2,1)S(1)}, bf16[25,256]{1,0:T(8,128)(2,1)S(1)}, u32[]{:S(2)}, u32[]{:S(2)}) collective-permute-start(bf16[25,256]{1,0:T(8,128)(2,1)S(1)} %get-tuple-element.31), channel_id=1, source_target_pairs={{0,3},{3,0},{1,2},{2,1},{4,7},{7,4},{5,6},{6,5},{8,11},{11,8},{9,1... | collective-permute-start | bytes 38408 | tf_op jit(solution)/shard_map/ppermute | solution.py:379
  62.4 17.7 %collective-permute-done.8.from_chip = bf16[25,256]{1,0:T(8,128)(2,1)S(1)} collective-permute-done((bf16[25,256]{1,0:T(8,128)(2,1)S(1)}, bf16[25,256]{1,0:T(8,128)(2,1)S(1)}, u32[]{:S(2)}, u32[]{:S(2)}) %collective-permute-start.8) | collective-permute-done | bytes 12832 | tf_op jit(solution)/shard_map/ppermute | solution.py:375
  80.0 1.7 %collective-permute-done.9.from_both = bf16[25,256]{1,0:T(8,128)(2,1)S(1)} collective-permute-done((bf16[25,256]{1,0:T(8,128)(2,1)S(1)}, bf16[25,256]{1,0:T(8,128)(2,1)S(1)}, u32[]{:S(2)}, u32[]{:S(2)}) %collective-permute-start.9) | collective-permute-done | bytes 12832 | tf_op jit(solution)/shard_map/ppermute | solution.py:379
  81.8 0.6 shard_map.114
  82.4 0.0 collective-permute-done.6.arrived
  82.4 1.1 %shard_map.111.token = f32[256,1024]{1,0:T(8,128)} custom-call(f32[256,1024]{1,0:T(8,128)S(1)} %get-tuple-element.28.own, bf16[256,1024]{1,0:T(8,128)(2,1)S(1)} %collective-permute-done.6.arrived), custom_call_target="tpu_custom_call" | custom-call | bytes 1024 | tf_op jit(solution)/shard_map/pallas_call | solution.py:327
  83.5 0.0 collective-permute-done.5.message
  83.5 1.1 %shard_map.112.token = bf16[14,14,1024]{2,1,0:T(8,128)(2,1)} custom-call(bf16[200,1024]{1,0:T(8,128)(2,1)S(1)} %collective-permute-done.5.message, bf16[196,16,128]{2,1,0:T(8,128)(2,1)} %bitcast.39, f32[256,1024]{1,0:T(8,128)} %shard_map.111.token), custom_call_target="tpu_custom_call" | custom-call | bytes 1024 | tf_op jit(solution)/shard_map/pallas_call | solution.py:327
  84.6 0.0 collective-permute-done.4.message
  84.6 2.7 %shard_map.113 = bf16[14,14,1024]{2,1,0:T(8,128)(2,1)} custom-call(bf16[196,1024]{1,0:T(8,128)(2,1)S(1)} %collective-permute-done.4.message, bf16[196,16,128]{2,1,0:T(8,128)(2,1)} %bitcast.37, bf16[14,14,1024]{2,1,0:T(8,128)(2,1)} %shard_map.112.token), custom_call_target="tpu_custom_call" | custom-call | bytes 1024 | tf_op jit(solution)/shard_map/pallas_call | solution.py:327
  (1 shorter events, 0.0 us)
Async XLA Ops:
  5.5 19.3 %collective-permute-start.1 = (bf16[196,1024]{1,0:T(8,128)(2,1)S(1)}, bf16[196,1024]{1,0:T(8,128)(2,1)S(1)}, u32[]{:S(2)}, u32[]{:S(2)}) collective-permute-start(bf16[196,1024]{1,0:T(8,128)(2,1)S(1)} %get-tuple-element.23.token), channel_id=1, source_target_pairs={{4,0},{8,4},{12,8},{16,12},{20,16},{24,20},{28,24},{32,28},{36,32}... | collective-permute-start | bytes 1204232 | tf_op jit(solution)/shard_map/ppermute | solution.py:367
  10.1 21.0 %collective-permute-start.2 = (bf16[196,2048]{1,0:T(8,128)(2,1)S(1)}, bf16[196,2048]{1,0:T(8,128)(2,1)S(1)}, u32[]{:S(2)}, u32[]{:S(2)}) collective-permute-start(bf16[196,2048]{1,0:T(8,128)(2,1)S(1)} %get-tuple-element.25), channel_id=1, source_target_pairs={{0,1},{1,0},{2,3},{3,2},{4,5},{5,4},{6,7},{7,6},{8,9},{9,8},{10,11... | collective-permute-start | bytes 2408456 | tf_op jit(solution)/shard_map/ppermute | solution.py:371
  24.9 7.0 %collective-permute-start.3 = (bf16[196,1024]{1,0:T(8,128)(2,1)S(1)}, bf16[196,1024]{1,0:T(8,128)(2,1)S(1)}, u32[]{:S(2)}, u32[]{:S(2)}) collective-permute-start(bf16[196,1024]{1,0:T(8,128)(2,1)S(1)} %shard_map.105.g_own.g.g1), channel_id=1, source_target_pairs={{0,1},{1,0},{2,3},{3,2},{4,5},{5,4},{6,7},{7,6},{8,9},{9,8},{10,11... | collective-permute-start | bytes 1204232 | tf_op jit(solution)/shard_map/ppermute | solution.py:371
  27.8 15.5 %collective-permute-start = (bf16[196,1024]{1,0:T(8,128)(2,1)S(1)}, bf16[196,1024]{1,0:T(8,128)(2,1)S(1)}, u32[]{:S(2)}, u32[]{:S(2)}) collective-permute-start(bf16[196,1024]{1,0:T(8,128)(2,1)S(1)} %shard_map.104.token), channel_id=1, source_target_pairs={{0,4},{4,8},{8,12},{12,16},{16,20},{20,24},{24,28},{28,32},{32,36}... | collective-permute-start | bytes 1204232 | tf_op jit(solution)/shard_map/ppermute | solution.py:367
  32.6 49.8 %collective-permute-start.6 = (bf16[256,1024]{1,0:T(8,128)(2,1)S(1)}, bf16[256,1024]{1,0:T(8,128)(2,1)S(1)}, u32[]{:S(2)}, u32[]{:S(2)}) collective-permute-start(bf16[256,1024]{1,0:T(8,128)(2,1)S(1)} %get-tuple-element.26.token), channel_id=1, source_target_pairs={{0,2},{2,0},{1,3},{3,1},{4,6},{6,4},{5,7},{7,5},{8,10},{10,8},{9,1... | collective-permute-start | bytes 1572872 | tf_op jit(solution)/shard_map/ppermute | solution.py:375
  37.2 46.3 %collective-permute-start.5 = (bf16[200,1024]{1,0:T(8,128)(2,1)S(1)}, bf16[200,1024]{1,0:T(8,128)(2,1)S(1)}, u32[]{:S(2)}, u32[]{:S(2)}) collective-permute-start(bf16[200,1024]{1,0:T(8,128)(2,1)S(1)} %shard_map.108.token), channel_id=1, source_target_pairs={{4,0},{8,4},{12,8},{16,12},{20,16},{24,20},{28,24},{32,28},{36,32}... | collective-permute-start | bytes 1228808 | tf_op jit(solution)/shard_map/ppermute | solution.py:367
  47.2 37.4 %collective-permute-start.4 = (bf16[196,1024]{1,0:T(8,128)(2,1)S(1)}, bf16[196,1024]{1,0:T(8,128)(2,1)S(1)}, u32[]{:S(2)}, u32[]{:S(2)}) collective-permute-start(bf16[196,1024]{1,0:T(8,128)(2,1)S(1)} %shard_map.110), channel_id=1, source_target_pairs={{0,4},{4,8},{8,12},{12,16},{16,20},{20,24},{24,28},{28,32},{32,36}... | collective-permute-start | bytes 1204232 | tf_op jit(solution)/shard_map/ppermute | solution.py:367
  49.6 10.8 %collective-permute-start.7 = (bf16[25,256]{1,0:T(8,128)(2,1)S(1)}, bf16[25,256]{1,0:T(8,128)(2,1)S(1)}, u32[]{:S(2)}, u32[]{:S(2)}) collective-permute-start(bf16[25,256]{1,0:T(8,128)(2,1)S(1)} %get-tuple-element.29), channel_id=1, source_target_pairs={{0,1},{1,0},{2,3},{3,2},{4,5},{5,4},{6,7},{7,6},{8,9},{9,8},{10,11... | collective-permute-start | bytes 38408 | tf_op jit(solution)/shard_map/ppermute | solution.py:371
  52.9 27.1 %collective-permute-start.8 = (bf16[25,256]{1,0:T(8,128)(2,1)S(1)}, bf16[25,256]{1,0:T(8,128)(2,1)S(1)}, u32[]{:S(2)}, u32[]{:S(2)}) collective-permute-start(bf16[25,256]{1,0:T(8,128)(2,1)S(1)} %get-tuple-element.30), channel_id=1, source_target_pairs={{0,2},{2,0},{1,3},{3,1},{4,6},{6,4},{5,7},{7,5},{8,10},{10,8},{9,1... | collective-permute-start | bytes 38408 | tf_op jit(solution)/shard_map/ppermute | solution.py:375
  60.4 21.3 %collective-permute-start.9 = (bf16[25,256]{1,0:T(8,128)(2,1)S(1)}, bf16[25,256]{1,0:T(8,128)(2,1)S(1)}, u32[]{:S(2)}, u32[]{:S(2)}) collective-permute-start(bf16[25,256]{1,0:T(8,128)(2,1)S(1)} %get-tuple-element.31), channel_id=1, source_target_pairs={{0,3},{3,0},{1,2},{2,1},{4,7},{7,4},{5,6},{6,5},{8,11},{11,8},{9,1... | collective-permute-start | bytes 38408 | tf_op jit(solution)/shard_map/ppermute | solution.py:379

commit v6 on v5

--- a/solution.py
+++ b/solution.py
@@ -19,6 +19,10 @@
 ROW = HW * GROUPS
 HALF = C // 2
 QUARTER = C // 4
+FIRST = 160
+SECOND = QUARTER - FIRST
+TAP_ROWS = 32
+HALF_ROWS = TAP_ROWS // 2
 PAD_ROWS = (HW + KW - 1) * ROW
 DENSE_ROWS = PIX * GROUPS
 TOP = (KW // 2) * ROW
@@ -257,7 +261,7 @@
     out[...] += weight_term(peer[:, :HALF], peer[:, C : 2 * C])
 
 
-def weight_second(total, keep, g_own, peer, g_peer, own, other):
+def weight_second(total, keep, g_own, peer, g_peer, token, own, other_top, other_low):
     for place in range(2):
         rows = slice(place * QUARTER, (place + 1) * QUARTER)
         part = slice(HALF + place * QUARTER, HALF + (place + 1) * QUARTER)
@@ -266,10 +270,11 @@
         if place == 0:
             own[...] = value
         else:
-            other[...] = value.astype(bf16)
-
-
-def taps_kernel(pair, g0, g1, weight, token, own, core_out, chip_out, both_out, rect, grad, sums, wide):
+            other_top[...] = value[0:FIRST, :].astype(bf16)
+            other_low[...] = value[FIRST:QUARTER, :].astype(bf16)
+
+
+def taps_kernel(pair, g0, g1, weight, token, mine, theirs, rect, grad, sums, wide):
     core = lax.rem(lax.axis_index("dp"), 2)
     high = lax.div(lax.axis_index("dp"), 2)
     widen_pair(pair, wide)
@@ -278,6 +283,8 @@
         rect[TOP : TOP + DENSE_ROWS, :] = jnp.maximum(pair_tick_spread(wide, tick), 0.0)
         spread_grad((g0, g1)[tick], weight, grad)
         terms = tap_sums(rect, grad)
+        if tick == 0:
+            sums[TAPS:TAP_ROWS, :] = jnp.zeros((TAP_ROWS - TAPS, C), f32)
         for index in range(TAPS):
             row = jnp.concatenate([terms[index][i : i + 1] for i in range(GROUPS)], axis=1)
             if tick == 0:
@@ -287,26 +294,37 @@
 
     def block(side, which):
         at = pl.multiple_of((2 * side + which) * QUARTER, QUARTER)
-        return sums[0:TAPS, pl.ds(at, QUARTER)]
-
-    own[...] = block(high, core)
-    core_out[...] = block(high, 1 - core).astype(bf16)
-    chip_out[...] = block(1 - high, core).astype(bf16)
-    both_out[...] = block(1 - high, 1 - core).astype(bf16)
+        return sums[:, pl.ds(at, QUARTER)]
+
+    for place in range(2):
+        side = high if place == 0 else 1 - high
+        at = slice(place * QUARTER, (place + 1) * QUARTER)
+        mine[:, at] = block(side, core)
+        theirs[:, at] = block(side, 1 - core).astype(bf16)
+
+
+def pack_kernel(mine, arrived, other_low, own, message):
+    total = mine[...] + arrived[...].astype(f32)
+    own[...] = total[:, 0:QUARTER]
+    message[0:SECOND, :] = other_low[...]
+    for part in range(2):
+        taps = total[part * HALF_ROWS : (part + 1) * HALF_ROWS, QUARTER:HALF]
+        message[SECOND:, part * QUARTER : (part + 1) * QUARTER] = taps.astype(bf16)
+    message[SECOND:, HALF:] = jnp.zeros((HALF_ROWS, HALF), bf16)
 
 
 SCALE = 1.0 / (2 * 2 * TICKS)
 
 
-def final_kernel(own, arrived, out):
-    out[...] = (own[...] + arrived[...].astype(f32)) * SCALE
-
-
-def taps_final(own, from_core, from_chip, from_both, out):
-    total = own[...] + from_core[...].astype(f32) + from_chip[...].astype(f32)
-    total = (total + from_both[...].astype(f32)) * SCALE
+def final_kernel(own, top, low, own_k, out, out_k, taps):
+    out[0:FIRST, :] = (own[0:FIRST, :] + top[...].astype(f32)) * SCALE
+    out[FIRST:QUARTER, :] = (own[FIRST:QUARTER, :] + low[0:SECOND, :].astype(f32)) * SCALE
     for part in range(2):
-        out[:, part, :] = total[:, cols(part)]
+        rows = slice(part * HALF_ROWS, (part + 1) * HALF_ROWS)
+        arrived = low[SECOND:, part * QUARTER : (part + 1) * QUARTER].astype(f32)
+        taps[rows, :] = (own_k[rows, :] + arrived) * SCALE
+    for part in range(2):
+        out_k[:, part, :] = taps[0:TAPS, cols(part)]
 
 
 def unpack_kernel(edge, message, images, token, out, packed, rows, pair, wide, sem):
@@ -373,10 +391,6 @@
 
 def other_chip(value):
     return lax.ppermute(value, "dp", [(0, 2), (2, 0), (1, 3), (3, 1)])
-
-
-def other_both(value):
-    return lax.ppermute(value, "dp", [(0, 3), (3, 0), (1, 2), (2, 1)])
 
 
 def per_device(activations, incoming, saved, images, head_grads, pw_weight, dw_kernel):
@@ -429,6 +443,23 @@
         input_output_aliases={0: 0},
     )
     g1_peer = other_core(g1)
+    grad_in1 = call(
+        backward_second,
+        [VMEM, VMEM, VMEM, VMEM, ANY],
+        LONGER,
+        [ROWS, PADDED, DENSE, DENSE, WIDE],
+        (g1, pair, w, t, out0),
+    )
+    g2 = shifted(grad_in1, -1)
+    out1 = call(
+        forward_second,
+        [VMEM] * 3 + [HBM, ANY],
+        MESSAGE,
+        [ROWS, PADDED, DENSE, MIXED, PAIR, WIDE, sems(1)],
+        (act1, w, t, image_pair, grad_in1),
+    )
+    act2 = shifted(out1, 1)
+
     total = call(
         weight_first,
         [VMEM] * 3,
@@ -436,62 +467,62 @@
         [],
         (keep, g0, peer),
     )
-    own, other = call(
+    own, other_top, other_low = call(
         weight_second,
-        [VMEM] * 5,
-        (jax.ShapeDtypeStruct((QUARTER, C), f32), jax.ShapeDtypeStruct((QUARTER, C), bf16)),
+        [VMEM] * 5 + [ANY],
+        (
+            jax.ShapeDtypeStruct((QUARTER, C), f32),
+            jax.ShapeDtypeStruct((FIRST, C), bf16),
+            jax.ShapeDtypeStruct((SECOND, C), bf16),
+        ),
         [],
-        (total, keep, g1, peer, g1_peer),
-    )
-    arrived = other_chip(other)
-    grad_in1 = call(
-        backward_second,
-        [VMEM, VMEM, VMEM, VMEM, ANY],
-        LONGER,
-        [ROWS, PADDED, DENSE, DENSE, WIDE],
-        (g1, pair, w, t, other),
-    )
-    g2 = shifted(grad_in1, -1)
-    small = jax.ShapeDtypeStruct((TAPS, QUARTER), bf16)
-    own_k, core_k, chip_k, both_k = call(
+        (total, keep, g1, peer, g1_peer, out1),
+    )
+    top = other_chip(other_top)
+    mine, theirs = call(
         taps_kernel,
         [VMEM] * 4 + [ANY],
-        (jax.ShapeDtypeStruct((TAPS, QUARTER), f32), small, small, small),
-        [PADDED, PADDED, pltpu.VMEM((32, C), f32), WIDE],
-        (pair, g0, g1, w, grad_in1),
-    )
-    out1 = call(
-        forward_second,
-        [VMEM] * 3 + [HBM, ANY],
-        MESSAGE,
-        [ROWS, PADDED, DENSE, MIXED, PAIR, WIDE, sems(1)],
-        (act1, w, t, image_pair, own_k),
-    )
-    act2 = shifted(out1, 1)
-
-    k_grad = call(
-        taps_final,
-        [VMEM] * 4,
-        jax.ShapeDtypeStruct((TAPS, 2, LANES), f32),
+        (
+            jax.ShapeDtypeStruct((TAP_ROWS, HALF), f32),
+            jax.ShapeDtypeStruct((TAP_ROWS, HALF), bf16),
+        ),
+        [PADDED, PADDED, pltpu.VMEM((TAP_ROWS, C), f32), WIDE],
+        (pair, g0, g1, w, other_top),
+    )
+    own_k, message = call(
+        pack_kernel,
+        [VMEM] * 3,
+        (
+            jax.ShapeDtypeStruct((TAP_ROWS, QUARTER), f32),
+            jax.ShapeDtypeStruct((SECOND + HALF_ROWS, C), bf16),
+        ),
         [],
-        (own_k, other_core(core_k), other_chip(chip_k), other_both(both_k)),
-    )
-    w_grad = call(
-        final_kernel, [VMEM, VMEM], jax.ShapeDtypeStruct((QUARTER, C), f32), [], (own, arrived)
-    )
+        (mine, other_core(theirs), other_low),
+    )
+    low = other_chip(message)
     grad_out = call(
         functools.partial(unpack_kernel, is_last),
-        [ANY, HBM, HBM],
+        [ANY, HBM, ANY],
         IMAGE,
         [pltpu.VMEM((PIX_ROWS, C), bf16), ROWS, PAIR, WIDE, sems(1)],
-        (g2, head_pair, w_grad),
+        (g2, head_pair, own),
     )
     act_out = call(
         functools.partial(unpack_kernel, is_first),
-        [ANY, HBM, HBM],
+        [ANY, HBM, ANY],
         IMAGE,
         [MIXED, ROWS, PAIR, WIDE, sems(1)],
-        (act2, image_pair, grad_out),
+        (act2, image_pair, own),
+    )
+    w_grad, k_grad = call(
+        final_kernel,
+        [VMEM] * 4,
+        (
+            jax.ShapeDtypeStruct((QUARTER, C), f32),
+            jax.ShapeDtypeStruct((TAPS, 2, LANES), f32),
+        ),
+        [pltpu.VMEM((TAP_ROWS, QUARTER), f32)],
+        (own, top, low, own_k),
     )
     k_grad = k_grad.reshape(TAPS, QUARTER)
     return (act_out[None, None, None], grad_out[None, None, None], w_grad[None], k_grad[None])

time: 89 us -> 86.5 us (0.972)
  the two profiles are of different devices: /device:TPU:1 before, /device:TPU:513 now
where the time goes in v6:
time: 86.5 us; the launch traced here: 86.1 us
  starting transfers between devices  39.2 us (45%)
  Pallas kernels  25.1 us (29%)
  waiting for transfers between devices  21 us (24%)
    pallas_call x13, Pallas kernels, call(): pl.pallas_call(kernel, in_specs=ins, out_specs=jax.tree.map(lambda _: VME...  25.1 us
    ppermute x4, starting transfers between devices, shifted(): return lax.ppermute(value, 'section', pairs)  22.1 us
    ppermute x2, waiting for transfers between devices, other_chip(): return lax.ppermute(value, 'dp', [(0, 2), (2, 0), (1, 3), (3, 1)])  13.5 us
    ppermute x2, starting transfers between devices, other_chip(): return lax.ppermute(value, 'dp', [(0, 2), (2, 0), (1, 3), (3, 1)])  9.19 us
    ppermute x3, starting transfers between devices, other_core(): return lax.ppermute(value, 'dp', [(0, 1), (1, 0), (2, 3), (3, 2)])  7.93 us
    ppermute x4, waiting for transfers between devices, shifted(): return lax.ppermute(value, 'section', pairs)  6.62 us
  transfers between devices with their start and end apart: 9, of which 4 were waited for; matrix products, arithmetic and copies ran while one was open for 0% of the time, Pallas kernels for 22%

profile of v6, /device:TPU:513, one launch (start us, length us, event | category | flops | bytes accessed | tf_op | source)
XLA Modules:
  0.0 86.1 jit_solution(15159848873540254894)
XLA Ops:
  0.6 4.9 %shard_map.102 = (bf16[196,1024]{1,0:T(8,128)(2,1)S(1)}, bf16[196,1024]{1,0:T(8,128)(2,1)S(1)}, bf16[1024,1024]{1,0:T(8,128)(2,1)S(1)}, f32[25,8,128]{2,1,0:T(8,...) custom-call(bf16[14,14,1024]{2,1,0:T(8,128)(2,1)} %bitcast.41, ...), custom_call_target="tpu_custom_call" | custom-call | bytes 1024 | tf_op jit(solution)/shard_map/pallas_call | solution.py:345
  5.5 8.6 %collective-permute-start.1 = (bf16[196,1024]{1,0:T(8,128)(2,1)S(1)}, bf16[196,1024]{1,0:T(8,128)(2,1)S(1)}, u32[]{:S(2)}, u32[]{:S(2)}) collective-permute-start(bf16[196,1024]{1,0:T(8,128)(2,1)S(1)} %get-tuple-element.26.token), channel_id=1, source_target_pairs={{4,0},{8,4},{12,8},{16,12},{20,16},{24,20},{28,24},{32,28},{36,32}... | collective-permute-start | bytes 1204232 | tf_op jit(solution)/shard_map/ppermute | solution.py:385
  14.2 3.3 %shard_map.103 = (bf16[196,1024]{1,0:T(8,128)(2,1)S(1)}, bf16[196,2048]{1,0:T(8,128)(2,1)S(1)}) custom-call(bf16[196,16,128]{2,1,0:T(8,128)(2,1)S(1)} %get-tuple-element.24.pair, bf16[196,1024]{1,0:T(8,128)(2,1)S(1)} %get-tuple-element.25.g_rows.g_own.g0, f32[25,8,128]{2,1,0:T(8,128)S(1)} %get-tuple-element.23.taps, ...), custom_call_target="tpu_custom_call" | custom-call | bytes 1024 | tf_op jit(solution)/shard_map/pallas_call | solution.py:345
  17.4 2.9 %collective-permute-start.3 = (bf16[196,2048]{1,0:T(8,128)(2,1)S(1)}, bf16[196,2048]{1,0:T(8,128)(2,1)S(1)}, u32[]{:S(2)}, u32[]{:S(2)}) collective-permute-start(bf16[196,2048]{1,0:T(8,128)(2,1)S(1)} %get-tuple-element.28), channel_id=1, source_target_pairs={{0,1},{1,0},{2,3},{3,2},{4,5},{5,4},{6,7},{7,6},{8,9},{9,8},{10,11... | collective-permute-start | bytes 2408456 | tf_op jit(solution)/shard_map/ppermute | solution.py:389
  20.3 2.3 %shard_map.104.token = bf16[196,1024]{1,0:T(8,128)(2,1)S(1)} custom-call(bf16[14,14,1024]{2,1,0:T(8,128)(2,1)S(1)} %get-tuple-element.21.x, bf16[1024,1024]{1,0:T(8,128)(2,1)S(1)} %get-tuple-element.22.weight, f32[25,8,128]{2,1,0:T(8,128)S(1)} %get-tuple-element.23.taps, bf16[196,1024]{1,0:T(8,128)(2,1)S(1)} %get-tuple-element.27.token.keep), custom_call_target="tpu_custom_call" | custom-call | bytes 1024 | tf_op jit(solution)/shard_map/pallas_call | solution.py:345
  22.6 1.9 %collective-permute-start = (bf16[196,1024]{1,0:T(8,128)(2,1)S(1)}, bf16[196,1024]{1,0:T(8,128)(2,1)S(1)}, u32[]{:S(2)}, u32[]{:S(2)}) collective-permute-start(bf16[196,1024]{1,0:T(8,128)(2,1)S(1)} %shard_map.104.token), channel_id=1, source_target_pairs={{0,4},{4,8},{8,12},{12,16},{16,20},{20,24},{24,28},{28,32},{32,36}... | collective-permute-start | bytes 1204232 | tf_op jit(solution)/shard_map/ppermute | solution.py:385
  24.5 0.0 collective-permute-done.1.g_in
  24.6 1.9 %collective-permute-start.4 = (bf16[196,1024]{1,0:T(8,128)(2,1)S(1)}, bf16[196,1024]{1,0:T(8,128)(2,1)S(1)}, u32[]{:S(2)}, u32[]{:S(2)}) collective-permute-start(bf16[196,1024]{1,0:T(8,128)(2,1)S(1)} %shard_map.105.g.g_own.g1), channel_id=1, source_target_pairs={{0,1},{1,0},{2,3},{3,2},{4,5},{5,4},{6,7},{7,6},{8,9},{9,8},{10,11... | collective-permute-start | bytes 1204232 | tf_op jit(solution)/shard_map/ppermute | solution.py:389
  26.5 2.7 %shard_map.106.token = bf16[200,1024]{1,0:T(8,128)(2,1)S(1)} custom-call(bf16[196,1024]{1,0:T(8,128)(2,1)S(1)} %shard_map.105.g.g_own.g1, bf16[196,16,128]{2,1,0:T(8,128)(2,1)S(1)} %get-tuple-element.24.pair, bf16[1024,1024]{1,0:T(8,128)(2,1)S(1)} %get-tuple-element.22.weight, f32[25,8,128]{2,1,0:T(8,128)S(1)} %get-tuple-element.23.taps, ...), custom_call_target="tpu_custom_call" | custom-call | bytes 1024 | tf_op jit(solution)/shard_map/pallas_call | solution.py:345
  29.2 9.7 %collective-permute-start.5 = (bf16[200,1024]{1,0:T(8,128)(2,1)S(1)}, bf16[200,1024]{1,0:T(8,128)(2,1)S(1)}, u32[]{:S(2)}, u32[]{:S(2)}) collective-permute-start(bf16[200,1024]{1,0:T(8,128)(2,1)S(1)} %shard_map.106.token), channel_id=1, source_target_pairs={{4,0},{8,4},{12,8},{16,12},{20,16},{24,20},{28,24},{32,28},{36,32}... | collective-permute-start | bytes 1228808 | tf_op jit(solution)/shard_map/ppermute | solution.py:385
  38.8 2.8 %collective-permute-done.x = bf16[196,1024]{1,0:T(8,128)(2,1)S(1)} collective-permute-done((bf16[196,1024]{1,0:T(8,128)(2,1)S(1)}, bf16[196,1024]{1,0:T(8,128)(2,1)S(1)}, u32[]{:S(2)}, u32[]{:S(2)}) %collective-permute-start) | collective-permute-done | bytes 401440 | tf_op jit(solution)/shard_map/ppermute | solution.py:385
  41.7 2.3 %shard_map.107.token = bf16[196,1024]{1,0:T(8,128)(2,1)S(1)} custom-call(bf16[196,1024]{1,0:T(8,128)(2,1)S(1)} %collective-permute-done.x, bf16[1024,1024]{1,0:T(8,128)(2,1)S(1)} %get-tuple-element.22.weight, f32[25,8,128]{2,1,0:T(8,128)S(1)} %get-tuple-element.23.taps, bf16[196,16,128]{2,1,0:T(8,128)(2,1)} %bitcast.35, bf16[200,1024]{1,0:T(8,128)(2,1)S(1)} %shard_map.106.token), custom_call_target="tpu_custom_call" | custom-call | bytes 1024 | tf_op jit(solution)/shard_map/pallas_call | solution.py:345
  44.0 1.9 %collective-permute-start.2 = (bf16[196,1024]{1,0:T(8,128)(2,1)S(1)}, bf16[196,1024]{1,0:T(8,128)(2,1)S(1)}, u32[]{:S(2)}, u32[]{:S(2)}) collective-permute-start(bf16[196,1024]{1,0:T(8,128)(2,1)S(1)} %shard_map.107.token), channel_id=1, source_target_pairs={{0,4},{4,8},{8,12},{12,16},{16,20},{20,24},{24,28},{28,32},{32,36}... | collective-permute-start | bytes 1204232 | tf_op jit(solution)/shard_map/ppermute | solution.py:385
  45.9 0.0 collective-permute-done.3.peer
  45.9 0.7 shard_map.108.total
  46.6 0.0 collective-permute-done.4.g_peer
  46.7 0.7 shard_map.109
  47.4 4.8 %collective-permute-start.6 = (bf16[160,1024]{1,0:T(8,128)(2,1)S(1)}, bf16[160,1024]{1,0:T(8,128)(2,1)S(1)}, u32[]{:S(2)}, u32[]{:S(2)}) collective-permute-start(bf16[160,1024]{1,0:T(8,128)(2,1)S(1)} %get-tuple-element.30.token), channel_id=1, source_target_pairs={{0,2},{2,0},{1,3},{3,1},{4,6},{6,4},{5,7},{7,5},{8,10},{10,8},{9,1... | collective-permute-start | bytes 983048 | tf_op jit(solution)/shard_map/ppermute | solution.py:393
  52.2 4.8 %shard_map.112 = (f32[32,512]{1,0:T(8,128)S(1)}, bf16[32,512]{1,0:T(8,128)(2,1)S(1)}) custom-call(bf16[196,16,128]{2,1,0:T(8,128)(2,1)S(1)} %get-tuple-element.24.pair, bf16[196,1024]{1,0:T(8,128)(2,1)S(1)} %get-tuple-element.25.g_rows.g_own.g0, bf16[196,1024]{1,0:T(8,128)(2,1)S(1)} %shard_map.105.g.g_own.g1, ...), custom_call_target="tpu_custom_call" | custom-call | bytes 1024 | tf_op jit(solution)/shard_map/pallas_call | solution.py:345
  57.0 3.1 %collective-permute-start.7 = (bf16[32,512]{1,0:T(8,128)(2,1)S(1)}, bf16[32,512]{1,0:T(8,128)(2,1)S(1)}, u32[]{:S(2)}, u32[]{:S(2)}) collective-permute-start(bf16[32,512]{1,0:T(8,128)(2,1)S(1)} %get-tuple-element.32), channel_id=1, source_target_pairs={{0,1},{1,0},{2,3},{3,2},{4,5},{5,4},{6,7},{7,6},{8,9},{9,8},{10,11... | collective-permute-start | bytes 98312 | tf_op jit(solution)/shard_map/ppermute | solution.py:389
  60.1 0.8 collective-permute-done.7.arrived
  61.0 4.4 %collective-permute-start.8 = (bf16[112,1024]{1,0:T(8,128)(2,1)S(1)}, bf16[112,1024]{1,0:T(8,128)(2,1)S(1)}, u32[]{:S(2)}, u32[]{:S(2)}) collective-permute-start(bf16[112,1024]{1,0:T(8,128)(2,1)S(1)} %get-tuple-element.34), channel_id=1, source_target_pairs={{0,2},{2,0},{1,3},{3,1},{4,6},{6,4},{5,7},{7,5},{8,10},{10,8},{9,1... | collective-permute-start | bytes 688136 | tf_op jit(solution)/shard_map/ppermute | solution.py:393
  65.4 3.8 %collective-permute-done.2.message = bf16[196,1024]{1,0:T(8,128)(2,1)S(1)} collective-permute-done((bf16[196,1024]{1,0:T(8,128)(2,1)S(1)}, bf16[196,1024]{1,0:T(8,128)(2,1)S(1)}, u32[]{:S(2)}, u32[]{:S(2)}) %collective-permute-start.2) | collective-permute-done | bytes 401440 | tf_op jit(solution)/shard_map/ppermute | solution.py:385
  69.2 1.1 %shard_map.110 = bf16[14,14,1024]{2,1,0:T(8,128)(2,1)} custom-call(bf16[196,1024]{1,0:T(8,128)(2,1)S(1)} %collective-permute-done.2.message, bf16[196,16,128]{2,1,0:T(8,128)(2,1)} %bitcast.36, f32[256,1024]{1,0:T(8,128)S(1)} %get-tuple-element.29.token.own), custom_call_target="tpu_custom_call" | custom-call | bytes 1024 | tf_op jit(solution)/shard_map/pallas_call | solution.py:345
  70.3 0.0 collective-permute-done.5.message
  70.3 1.1 %shard_map.111 = bf16[14,14,1024]{2,1,0:T(8,128)(2,1)} custom-call(bf16[200,1024]{1,0:T(8,128)(2,1)S(1)} %collective-permute-done.5.message, bf16[196,16,128]{2,1,0:T(8,128)(2,1)} %bitcast.38, f32[256,1024]{1,0:T(8,128)S(1)} %get-tuple-element.29.token.own), custom_call_target="tpu_custom_call" | custom-call | bytes 1024 | tf_op jit(solution)/shard_map/pallas_call | solution.py:345
  71.4 13.5 %collective-permute-done.8.low = bf16[112,1024]{1,0:T(8,128)(2,1)S(1)} collective-permute-done((bf16[112,1024]{1,0:T(8,128)(2,1)S(1)}, bf16[112,1024]{1,0:T(8,128)(2,1)S(1)}, u32[]{:S(2)}, u32[]{:S(2)}) %collective-permute-start.8) | collective-permute-done | bytes 229408 | tf_op jit(solution)/shard_map/ppermute | solution.py:393
  85.0 0.0 collective-permute-done.6.top
  85.0 1.2 %shard_map.114 = (f32[256,1024]{1,0:T(8,128)}, f32[25,2,128]{2,1,0:T(2,128)}) custom-call(f32[256,1024]{1,0:T(8,128)S(1)} %get-tuple-element.29.token.own, bf16[160,1024]{1,0:T(8,128)(2,1)S(1)} %collective-permute-done.6.top, bf16[112,1024]{1,0:T(8,128)(2,1)S(1)} %collective-permute-done.8.low, f32[32,256]{1,0:T(8,128)S(1)} %get-tuple-element.35.own_k), custom_call_target="tpu_custom_call" | custom-call | bytes 1024 | tf_op jit(solution)/shard_map/pallas_call | solution.py:345
  (2 shorter events, 0.1 us)
Async XLA Ops:
  5.5 19.0 %collective-permute-start.1 = (bf16[196,1024]{1,0:T(8,128)(2,1)S(1)}, bf16[196,1024]{1,0:T(8,128)(2,1)S(1)}, u32[]{:S(2)}, u32[]{:S(2)}) collective-permute-start(bf16[196,1024]{1,0:T(8,128)(2,1)S(1)} %get-tuple-element.26.token), channel_id=1, source_target_pairs={{4,0},{8,4},{12,8},{16,12},{20,16},{24,20},{28,24},{32,28},{36,32}... | collective-permute-start | bytes 1204232 | tf_op jit(solution)/shard_map/ppermute | solution.py:385
  17.4 28.4 %collective-permute-start.3 = (bf16[196,2048]{1,0:T(8,128)(2,1)S(1)}, bf16[196,2048]{1,0:T(8,128)(2,1)S(1)}, u32[]{:S(2)}, u32[]{:S(2)}) collective-permute-start(bf16[196,2048]{1,0:T(8,128)(2,1)S(1)} %get-tuple-element.28), channel_id=1, source_target_pairs={{0,1},{1,0},{2,3},{3,2},{4,5},{5,4},{6,7},{7,6},{8,9},{9,8},{10,11... | collective-permute-start | bytes 2408456 | tf_op jit(solution)/shard_map/ppermute | solution.py:389
  22.6 19.1 %collective-permute-start = (bf16[196,1024]{1,0:T(8,128)(2,1)S(1)}, bf16[196,1024]{1,0:T(8,128)(2,1)S(1)}, u32[]{:S(2)}, u32[]{:S(2)}) collective-permute-start(bf16[196,1024]{1,0:T(8,128)(2,1)S(1)} %shard_map.104.token), channel_id=1, source_target_pairs={{0,4},{4,8},{8,12},{12,16},{16,20},{20,24},{24,28},{28,32},{32,36}... | collective-permute-start | bytes 1204232 | tf_op jit(solution)/shard_map/ppermute | solution.py:385
  24.6 22.1 %collective-permute-start.4 = (bf16[196,1024]{1,0:T(8,128)(2,1)S(1)}, bf16[196,1024]{1,0:T(8,128)(2,1)S(1)}, u32[]{:S(2)}, u32[]{:S(2)}) collective-permute-start(bf16[196,1024]{1,0:T(8,128)(2,1)S(1)} %shard_map.105.g.g_own.g1), channel_id=1, source_target_pairs={{0,1},{1,0},{2,3},{3,2},{4,5},{5,4},{6,7},{7,6},{8,9},{9,8},{10,11... | collective-permute-start | bytes 1204232 | tf_op jit(solution)/shard_map/ppermute | solution.py:389
  29.2 41.1 %collective-permute-start.5 = (bf16[200,1024]{1,0:T(8,128)(2,1)S(1)}, bf16[200,1024]{1,0:T(8,128)(2,1)S(1)}, u32[]{:S(2)}, u32[]{:S(2)}) collective-permute-start(bf16[200,1024]{1,0:T(8,128)(2,1)S(1)} %shard_map.106.token), channel_id=1, source_target_pairs={{4,0},{8,4},{12,8},{16,12},{20,16},{24,20},{28,24},{32,28},{36,32}... | collective-permute-start | bytes 1228808 | tf_op jit(solution)/shard_map/ppermute | solution.py:385
  44.0 25.2 %collective-permute-start.2 = (bf16[196,1024]{1,0:T(8,128)(2,1)S(1)}, bf16[196,1024]{1,0:T(8,128)(2,1)S(1)}, u32[]{:S(2)}, u32[]{:S(2)}) collective-permute-start(bf16[196,1024]{1,0:T(8,128)(2,1)S(1)} %shard_map.107.token), channel_id=1, source_target_pairs={{0,4},{4,8},{8,12},{12,16},{16,20},{20,24},{24,28},{28,32},{32,36}... | collective-permute-start | bytes 1204232 | tf_op jit(solution)/shard_map/ppermute | solution.py:385
  47.4 37.6 %collective-permute-start.6 = (bf16[160,1024]{1,0:T(8,128)(2,1)S(1)}, bf16[160,1024]{1,0:T(8,128)(2,1)S(1)}, u32[]{:S(2)}, u32[]{:S(2)}) collective-permute-start(bf16[160,1024]{1,0:T(8,128)(2,1)S(1)} %get-tuple-element.30.token), channel_id=1, source_target_pairs={{0,2},{2,0},{1,3},{3,1},{4,6},{6,4},{5,7},{7,5},{8,10},{10,8},{9,1... | collective-permute-start | bytes 983048 | tf_op jit(solution)/shard_map/ppermute | solution.py:393
  57.0 4.0 %collective-permute-start.7 = (bf16[32,512]{1,0:T(8,128)(2,1)S(1)}, bf16[32,512]{1,0:T(8,128)(2,1)S(1)}, u32[]{:S(2)}, u32[]{:S(2)}) collective-permute-start(bf16[32,512]{1,0:T(8,128)(2,1)S(1)} %get-tuple-element.32), channel_id=1, source_target_pairs={{0,1},{1,0},{2,3},{3,2},{4,5},{5,4},{6,7},{7,6},{8,9},{9,8},{10,11... | collective-permute-start | bytes 98312 | tf_op jit(solution)/shard_map/ppermute | solution.py:389
  61.0 24.0 %collective-permute-start.8 = (bf16[112,1024]{1,0:T(8,128)(2,1)S(1)}, bf16[112,1024]{1,0:T(8,128)(2,1)S(1)}, u32[]{:S(2)}, u32[]{:S(2)}) collective-permute-start(bf16[112,1024]{1,0:T(8,128)(2,1)S(1)} %get-tuple-element.34), channel_id=1, source_target_pairs={{0,2},{2,0},{1,3},{3,1},{4,6},{6,4},{5,7},{7,5},{8,10},{10,8},{9,1... | collective-permute-start | bytes 688136 | tf_op jit(solution)/shard_map/ppermute | solution.py:393

commit v7 on v6

--- a/solution.py
+++ b/solution.py
@@ -13,16 +13,17 @@
 HW = 14
 PIX = HW * HW
 PIX_ROWS = -(-PIX // 8) * 8
+ACT_ROWS = 216
 C = 1024
 LANES = 128
 GROUPS = C // LANES
 ROW = HW * GROUPS
 HALF = C // 2
 QUARTER = C // 4
-FIRST = 160
+FIRST = 208
 SECOND = QUARTER - FIRST
 TAP_ROWS = 32
-HALF_ROWS = TAP_ROWS // 2
+LAST_ROWS = TAP_ROWS // 4
 PAD_ROWS = (HW + KW - 1) * ROW
 DENSE_ROWS = PIX * GROUPS
 TOP = (KW // 2) * ROW
@@ -155,11 +156,12 @@
 def forward_first(x, weight, taps, token, out, rows, padded, dense, mixed):
     pack_rows(x, rows)
     mix(rows, padded, dense, mixed, taps)
-    out[...] = (rows[...] + jnp.dot(mixed[...], weight[...], preferred_element_type=f32)).astype(bf16)
+    out[PIX:ACT_ROWS, :] = jnp.zeros((ACT_ROWS - PIX, C), bf16)
+    out[0:PIX, :] = (rows[...] + jnp.dot(mixed[...], weight[...], preferred_element_type=f32)).astype(bf16)
 
 
 def forward_second(x, weight, taps, images, token, out, rows, padded, dense, mixed, pair, wide, sem):
-    rows[...] = x[...].astype(f32)
+    rows[...] = x[0:PIX, :].astype(f32)
     replace_at_edge(is_first(), images, 0, pair, wide, rows, sem)
     mix(rows, padded, dense, mixed, taps)
     out[...] = (rows[...] + jnp.dot(mixed[...], weight[...], preferred_element_type=f32)).astype(bf16)
@@ -204,9 +206,9 @@
     g_hbm, saved, w_hbm, taps_hbm, x_hbm, out, g_rows, weight, taps, pair, x, g, rows, grad_mixed, dense, mask, wide, sems
 ):
     blocks = [slice(block * QUARTER, (block + 1) * QUARTER) for block in range(4)]
-    pieces = [(g_hbm, g), (saved, pair)]
+    pieces = [(g_hbm, g)]
     pieces += [(w_hbm.at[rows_, :], weight.at[rows_, :]) for rows_ in blocks]
-    pieces += [(taps_hbm, taps), (x_hbm, x)]
+    pieces += [(saved, pair), (taps_hbm, taps), (x_hbm, x)]
     copies = [
         pltpu.make_async_copy(src, dst, sems.at[i]) for i, (src, dst) in enumerate(pieces)
     ]
@@ -215,10 +217,10 @@
     copies[0].wait()
     pack_rows(g, rows)
     g_rows[...] = rows[...].astype(bf16)
-    copies[1].wait()
+    spread_grad(g_rows, weight, grad_mixed, copies[1:5])
+    copies[5].wait()
     widen_pair(pair, wide)
     mask[...] = pair_tick_spread(wide, 0)
-    spread_grad(g_rows, weight, grad_mixed, copies[2:6])
     copies[6].wait()
     finish_backward(taps, out, grad_mixed, rows, dense, mask)
     copies[7].wait()
@@ -261,14 +263,15 @@
     out[...] += weight_term(peer[:, :HALF], peer[:, C : 2 * C])
 
 
-def weight_second(total, keep, g_own, peer, g_peer, token, own, other_top, other_low):
+def weight_second(total, keep, g_own, peer, g_peer, token, own_top, own_low, other_top, other_low):
     for place in range(2):
         rows = slice(place * QUARTER, (place + 1) * QUARTER)
         part = slice(HALF + place * QUARTER, HALF + (place + 1) * QUARTER)
         value = total[rows, :] + weight_term(keep[:, part], g_own[...])
         value += weight_term(peer[:, part], g_peer[...])
         if place == 0:
-            own[...] = value
+            own_top[...] = value[0:FIRST, :]
+            own_low[...] = value[FIRST:QUARTER, :]
         else:
             other_top[...] = value[0:FIRST, :].astype(bf16)
             other_low[...] = value[FIRST:QUARTER, :].astype(bf16)
@@ -307,24 +310,30 @@
     total = mine[...] + arrived[...].astype(f32)
     own[...] = total[:, 0:QUARTER]
     message[0:SECOND, :] = other_low[...]
-    for part in range(2):
-        taps = total[part * HALF_ROWS : (part + 1) * HALF_ROWS, QUARTER:HALF]
+    for part in range(4):
+        taps = total[part * LAST_ROWS : (part + 1) * LAST_ROWS, QUARTER:HALF]
         message[SECOND:, part * QUARTER : (part + 1) * QUARTER] = taps.astype(bf16)
-    message[SECOND:, HALF:] = jnp.zeros((HALF_ROWS, HALF), bf16)
 
 
 SCALE = 1.0 / (2 * 2 * TICKS)
 
 
-def final_kernel(own, top, low, own_k, out, out_k, taps):
-    out[0:FIRST, :] = (own[0:FIRST, :] + top[...].astype(f32)) * SCALE
-    out[FIRST:QUARTER, :] = (own[FIRST:QUARTER, :] + low[0:SECOND, :].astype(f32)) * SCALE
-    for part in range(2):
-        rows = slice(part * HALF_ROWS, (part + 1) * HALF_ROWS)
+def final_first(own, top, out, rows, sem):
+    rows[...] = (own[...] + top[...].astype(f32)) * SCALE
+    fetch(rows, out.at[0:FIRST, :], sem)
+
+
+def final_second(own, low, own_k, grads, out, out_k, rows, taps, sem):
+    rows[...] = (own[...] + low[0:SECOND, :].astype(f32)) * SCALE
+    copy = pltpu.make_async_copy(rows, out.at[FIRST:QUARTER, :], sem)
+    copy.start()
+    for part in range(4):
+        at = slice(part * LAST_ROWS, (part + 1) * LAST_ROWS)
         arrived = low[SECOND:, part * QUARTER : (part + 1) * QUARTER].astype(f32)
-        taps[rows, :] = (own_k[rows, :] + arrived) * SCALE
+        taps[at, :] = (own_k[at, :] + arrived) * SCALE
     for part in range(2):
         out_k[:, part, :] = taps[0:TAPS, cols(part)]
+    copy.wait()
 
 
 def unpack_kernel(edge, message, images, token, out, packed, rows, pair, wide, sem):
@@ -368,6 +377,7 @@
 IMAGE = jax.ShapeDtypeStruct((HW, HW, C), bf16)
 MESSAGE = jax.ShapeDtypeStruct((PIX, C), bf16)
 LONGER = jax.ShapeDtypeStruct((PIX_ROWS, C), bf16)
+ACTS = jax.ShapeDtypeStruct((ACT_ROWS, C), bf16)
 
 
 def sems(count):
@@ -428,7 +438,7 @@
     out0 = call(
         forward_first,
         [VMEM, VMEM, VMEM, ANY],
-        MESSAGE,
+        ACTS,
         [ROWS, PADDED, DENSE, MIXED],
         (x0, w, t, keep),
     )
@@ -443,12 +453,33 @@
         input_output_aliases={0: 0},
     )
     g1_peer = other_core(g1)
+
+    total = call(
+        weight_first,
+        [VMEM] * 3,
+        jax.ShapeDtypeStruct((HALF, C), f32),
+        [],
+        (keep, g0, peer),
+    )
+    own_top, own_low, other_top, other_low = call(
+        weight_second,
+        [VMEM] * 5 + [ANY],
+        (
+            jax.ShapeDtypeStruct((FIRST, C), f32),
+            jax.ShapeDtypeStruct((SECOND, C), f32),
+            jax.ShapeDtypeStruct((FIRST, C), bf16),
+            jax.ShapeDtypeStruct((SECOND, C), bf16),
+        ),
+        [],
+        (total, keep, g1, peer, g1_peer, out0),
+    )
+    top = other_chip(other_top)
     grad_in1 = call(
         backward_second,
         [VMEM, VMEM, VMEM, VMEM, ANY],
         LONGER,
         [ROWS, PADDED, DENSE, DENSE, WIDE],
-        (g1, pair, w, t, out0),
+        (g1, pair, w, t, other_top),
     )
     g2 = shifted(grad_in1, -1)
     out1 = call(
@@ -459,26 +490,6 @@
         (act1, w, t, image_pair, grad_in1),
     )
     act2 = shifted(out1, 1)
-
-    total = call(
-        weight_first,
-        [VMEM] * 3,
-        jax.ShapeDtypeStruct((HALF, C), f32),
-        [],
-        (keep, g0, peer),
-    )
-    own, other_top, other_low = call(
-        weight_second,
-        [VMEM] * 5 + [ANY],
-        (
-            jax.ShapeDtypeStruct((QUARTER, C), f32),
-            jax.ShapeDtypeStruct((FIRST, C), bf16),
-            jax.ShapeDtypeStruct((SECOND, C), bf16),
-        ),
-        [],
-        (total, keep, g1, peer, g1_peer, out1),
-    )
-    top = other_chip(other_top)
     mine, theirs = call(
         taps_kernel,
         [VMEM] * 4 + [ANY],
@@ -487,14 +498,14 @@
             jax.ShapeDtypeStruct((TAP_ROWS, HALF), bf16),
         ),
         [PADDED, PADDED, pltpu.VMEM((TAP_ROWS, C), f32), WIDE],
-        (pair, g0, g1, w, other_top),
+        (pair, g0, g1, w, out1),
     )
     own_k, message = call(
         pack_kernel,
         [VMEM] * 3,
         (
             jax.ShapeDtypeStruct((TAP_ROWS, QUARTER), f32),
-            jax.ShapeDtypeStruct((SECOND + HALF_ROWS, C), bf16),
+            jax.ShapeDtypeStruct((SECOND + LAST_ROWS, C), bf16),
         ),
         [],
         (mine, other_core(theirs), other_low),
@@ -505,24 +516,32 @@
         [ANY, HBM, ANY],
         IMAGE,
         [pltpu.VMEM((PIX_ROWS, C), bf16), ROWS, PAIR, WIDE, sems(1)],
-        (g2, head_pair, own),
+        (g2, head_pair, own_low),
     )
     act_out = call(
         functools.partial(unpack_kernel, is_first),
         [ANY, HBM, ANY],
         IMAGE,
         [MIXED, ROWS, PAIR, WIDE, sems(1)],
-        (act2, image_pair, own),
+        (act2, image_pair, own_low),
+    )
+    grads = jax.ShapeDtypeStruct((QUARTER, C), f32)
+    w_grad = call(
+        final_first,
+        [VMEM, VMEM],
+        grads,
+        [pltpu.VMEM((FIRST, C), f32), sems(1)],
+        (own_top, top),
+        outs=HBM,
     )
     w_grad, k_grad = call(
-        final_kernel,
-        [VMEM] * 4,
-        (
-            jax.ShapeDtypeStruct((QUARTER, C), f32),
-            jax.ShapeDtypeStruct((TAPS, 2, LANES), f32),
-        ),
-        [pltpu.VMEM((TAP_ROWS, QUARTER), f32)],
-        (own, top, low, own_k),
+        final_second,
+        [VMEM, VMEM, VMEM, ANY],
+        (grads, jax.ShapeDtypeStruct((TAPS, 2, LANES), f32)),
+        [pltpu.VMEM((SECOND, C), f32), pltpu.VMEM((TAP_ROWS, QUARTER), f32), sems(1)],
+        (own_low, low, own_k, w_grad),
+        outs=(HBM, VMEM),
+        input_output_aliases={3: 0},
     )
     k_grad = k_grad.reshape(TAPS, QUARTER)
     return (act_out[None, None, None], grad_out[None, None, None], w_grad[None], k_grad[None])

time: 86.5 us -> 84.1 us (0.972)
  the two profiles are of different devices: /device:TPU:513 before, /device:TPU:1 now
where the time goes in v7:
time: 84.1 us; the launch traced here: 83.7 us
  starting transfers between devices  31.2 us (37%)
  Pallas kernels  29.3 us (35%)
  waiting for transfers between devices  22.3 us (27%)
    pallas_call x14, Pallas kernels, call(): pl.pallas_call(kernel, in_specs=ins, out_specs=jax.tree.map(lambda _: VME...  29.3 us
    ppermute x3, starting transfers between devices, other_core(): return lax.ppermute(value, 'dp', [(0, 1), (1, 0), (2, 3), (3, 2)])  18 us
    ppermute x4, waiting for transfers between devices, shifted(): return lax.ppermute(value, 'section', pairs)  17.7 us
    ppermute x4, starting transfers between devices, shifted(): return lax.ppermute(value, 'section', pairs)  9.42 us
    ppermute x2, starting transfers between devices, other_chip(): return lax.ppermute(value, 'dp', [(0, 2), (2, 0), (1, 3), (3, 1)])  3.84 us
    ppermute x2, waiting for transfers between devices, other_chip(): return lax.ppermute(value, 'dp', [(0, 2), (2, 0), (1, 3), (3, 1)])  3.11 us
  transfers between devices with their start and end apart: 9, of which 5 were waited for; matrix products, arithmetic and copies ran while one was open for 0% of the time, Pallas kernels for 28%

profile of v7, /device:TPU:1, one launch (start us, length us, event | category | flops | bytes accessed | tf_op | source)
XLA Modules:
  0.0 83.7 jit_solution(11108156536828453109)
XLA Ops:
  0.6 4.8 %shard_map.102 = (bf16[196,1024]{1,0:T(8,128)(2,1)S(1)}, bf16[196,1024]{1,0:T(8,128)(2,1)S(1)}, bf16[1024,1024]{1,0:T(8,128)(2,1)S(1)}, f32[25,8,128]{2,1,0:T(8,...) custom-call(bf16[14,14,1024]{2,1,0:T(8,128)(2,1)} %bitcast.42, ...), custom_call_target="tpu_custom_call" | custom-call | bytes 1024 | tf_op jit(solution)/shard_map/pallas_call | solution.py:354
  5.4 1.3 %collective-permute-start.1 = (bf16[196,1024]{1,0:T(8,128)(2,1)S(1)}, bf16[196,1024]{1,0:T(8,128)(2,1)S(1)}, u32[]{:S(2)}, u32[]{:S(2)}) collective-permute-start(bf16[196,1024]{1,0:T(8,128)(2,1)S(1)} %get-tuple-element.27.token), channel_id=1, source_target_pairs={{4,0},{8,4},{12,8},{16,12},{20,16},{24,20},{28,24},{32,28},{36,32}... | collective-permute-start | bytes 1204232 | tf_op jit(solution)/shard_map/ppermute | solution.py:395
  6.7 3.3 %shard_map.103 = (bf16[196,1024]{1,0:T(8,128)(2,1)S(1)}, bf16[196,2048]{1,0:T(8,128)(2,1)S(1)}) custom-call(bf16[196,16,128]{2,1,0:T(8,128)(2,1)S(1)} %get-tuple-element.25.pair, bf16[196,1024]{1,0:T(8,128)(2,1)S(1)} %get-tuple-element.26.g_rows.g_own.g0, f32[25,8,128]{2,1,0:T(8,128)S(1)} %get-tuple-element.24.taps, ...), custom_call_target="tpu_custom_call" | custom-call | bytes 1024 | tf_op jit(solution)/shard_map/pallas_call | solution.py:354
  10.0 12.4 %collective-permute-start.2 = (bf16[196,2048]{1,0:T(8,128)(2,1)S(1)}, bf16[196,2048]{1,0:T(8,128)(2,1)S(1)}, u32[]{:S(2)}, u32[]{:S(2)}) collective-permute-start(bf16[196,2048]{1,0:T(8,128)(2,1)S(1)} %get-tuple-element.29), channel_id=1, source_target_pairs={{0,1},{1,0},{2,3},{3,2},{4,5},{5,4},{6,7},{7,6},{8,9},{9,8},{10,11... | collective-permute-start | bytes 2408456 | tf_op jit(solution)/shard_map/ppermute | solution.py:399
  22.4 2.3 %shard_map.104.token = bf16[216,1024]{1,0:T(8,128)(2,1)S(1)} custom-call(bf16[14,14,1024]{2,1,0:T(8,128)(2,1)S(1)} %get-tuple-element.22.x, bf16[1024,1024]{1,0:T(8,128)(2,1)S(1)} %get-tuple-element.23.weight, f32[25,8,128]{2,1,0:T(8,128)S(1)} %get-tuple-element.24.taps, bf16[196,1024]{1,0:T(8,128)(2,1)S(1)} %get-tuple-element.28.token.keep), custom_call_target="tpu_custom_call" | custom-call | bytes 1024 | tf_op jit(solution)/shard_map/pallas_call | solution.py:354
  24.7 4.3 %collective-permute-start = (bf16[216,1024]{1,0:T(8,128)(2,1)S(1)}, bf16[216,1024]{1,0:T(8,128)(2,1)S(1)}, u32[]{:S(2)}, u32[]{:S(2)}) collective-permute-start(bf16[216,1024]{1,0:T(8,128)(2,1)S(1)} %shard_map.104.token), channel_id=1, source_target_pairs={{0,4},{4,8},{8,12},{12,16},{16,20},{20,24},{24,28},{28,32},{32,36}... | collective-permute-start | bytes 1327112 | tf_op jit(solution)/shard_map/ppermute | solution.py:395
  29.0 0.0 collective-permute-done.1.g_in
  29.1 2.2 %collective-permute-start.3 = (bf16[196,1024]{1,0:T(8,128)(2,1)S(1)}, bf16[196,1024]{1,0:T(8,128)(2,1)S(1)}, u32[]{:S(2)}, u32[]{:S(2)}) collective-permute-start(bf16[196,1024]{1,0:T(8,128)(2,1)S(1)} %shard_map.105.g_own.g.g1), channel_id=1, source_target_pairs={{0,1},{1,0},{2,3},{3,2},{4,5},{5,4},{6,7},{7,6},{8,9},{9,8},{10,11... | collective-permute-start | bytes 1204232 | tf_op jit(solution)/shard_map/ppermute | solution.py:399
  31.3 0.0 collective-permute-done.2.peer
  31.3 0.7 shard_map.106.total
  32.0 0.7 collective-permute-done.3.g_peer
  32.7 0.7 shard_map.107
  33.4 1.9 %collective-permute-start.8 = (bf16[208,1024]{1,0:T(8,128)(2,1)S(1)}, bf16[208,1024]{1,0:T(8,128)(2,1)S(1)}, u32[]{:S(2)}, u32[]{:S(2)}) collective-permute-start(bf16[208,1024]{1,0:T(8,128)(2,1)S(1)} %get-tuple-element.30.token), channel_id=1, source_target_pairs={{0,2},{2,0},{1,3},{3,1},{4,6},{6,4},{5,7},{7,5},{8,10},{10,8},{9,1... | collective-permute-start | bytes 1277960 | tf_op jit(solution)/shard_map/ppermute | solution.py:403
  35.4 2.7 %shard_map.108.token = bf16[200,1024]{1,0:T(8,128)(2,1)S(1)} custom-call(bf16[196,1024]{1,0:T(8,128)(2,1)S(1)} %shard_map.105.g_own.g.g1, bf16[196,16,128]{2,1,0:T(8,128)(2,1)S(1)} %get-tuple-element.25.pair, bf16[1024,1024]{1,0:T(8,128)(2,1)S(1)} %get-tuple-element.23.weight, f32[25,8,128]{2,1,0:T(8,128)S(1)} %get-tuple-element.24.taps, ...), custom_call_target="tpu_custom_call" | custom-call | bytes 1024 | tf_op jit(solution)/shard_map/pallas_call | solution.py:354
  38.0 1.3 %collective-permute-start.5 = (bf16[200,1024]{1,0:T(8,128)(2,1)S(1)}, bf16[200,1024]{1,0:T(8,128)(2,1)S(1)}, u32[]{:S(2)}, u32[]{:S(2)}) collective-permute-start(bf16[200,1024]{1,0:T(8,128)(2,1)S(1)} %shard_map.108.token), channel_id=1, source_target_pairs={{4,0},{8,4},{12,8},{16,12},{20,16},{24,20},{28,24},{32,28},{36,32}... | collective-permute-start | bytes 1228808 | tf_op jit(solution)/shard_map/ppermute | solution.py:395
  39.3 17.1 %collective-permute-done.x = bf16[216,1024]{1,0:T(8,128)(2,1)S(1)} collective-permute-done((bf16[216,1024]{1,0:T(8,128)(2,1)S(1)}, bf16[216,1024]{1,0:T(8,128)(2,1)S(1)}, u32[]{:S(2)}, u32[]{:S(2)}) %collective-permute-start) | collective-permute-done | bytes 442400 | tf_op jit(solution)/shard_map/ppermute | solution.py:395
  56.5 3.9 %shard_map.109.token = bf16[196,1024]{1,0:T(8,128)(2,1)S(1)} custom-call(bf16[216,1024]{1,0:T(8,128)(2,1)S(1)} %collective-permute-done.x, bf16[1024,1024]{1,0:T(8,128)(2,1)S(1)} %get-tuple-element.23.weight, f32[25,8,128]{2,1,0:T(8,128)S(1)} %get-tuple-element.24.taps, bf16[196,16,128]{2,1,0:T(8,128)(2,1)} %bitcast.36, bf16[200,1024]{1,0:T(8,128)(2,1)S(1)} %shard_map.108.token), custom_call_target="tpu_custom_call" | custom-call | bytes 1024 | tf_op jit(solution)/shard_map/pallas_call | solution.py:354
  60.3 2.5 %collective-permute-start.4 = (bf16[196,1024]{1,0:T(8,128)(2,1)S(1)}, bf16[196,1024]{1,0:T(8,128)(2,1)S(1)}, u32[]{:S(2)}, u32[]{:S(2)}) collective-permute-start(bf16[196,1024]{1,0:T(8,128)(2,1)S(1)} %shard_map.109.token), channel_id=1, source_target_pairs={{0,4},{4,8},{8,12},{12,16},{16,20},{20,24},{24,28},{28,32},{32,36}... | collective-permute-start | bytes 1204232 | tf_op jit(solution)/shard_map/ppermute | solution.py:395
  62.9 4.8 %shard_map.112 = (f32[32,512]{1,0:T(8,128)S(1)}, bf16[32,512]{1,0:T(8,128)(2,1)S(1)}) custom-call(bf16[196,16,128]{2,1,0:T(8,128)(2,1)S(1)} %get-tuple-element.25.pair, bf16[196,1024]{1,0:T(8,128)(2,1)S(1)} %get-tuple-element.26.g_rows.g_own.g0, bf16[196,1024]{1,0:T(8,128)(2,1)S(1)} %shard_map.105.g_own.g.g1, ...), custom_call_target="tpu_custom_call" | custom-call | bytes 1024 | tf_op jit(solution)/shard_map/pallas_call | solution.py:354
  67.7 3.4 %collective-permute-start.6 = (bf16[32,512]{1,0:T(8,128)(2,1)S(1)}, bf16[32,512]{1,0:T(8,128)(2,1)S(1)}, u32[]{:S(2)}, u32[]{:S(2)}) collective-permute-start(bf16[32,512]{1,0:T(8,128)(2,1)S(1)} %get-tuple-element.33), channel_id=1, source_target_pairs={{0,1},{1,0},{2,3},{3,2},{4,5},{5,4},{6,7},{7,6},{8,9},{9,8},{10,11... | collective-permute-start | bytes 98312 | tf_op jit(solution)/shard_map/ppermute | solution.py:399
  71.0 0.8 %collective-permute-done.6.arrived = bf16[32,512]{1,0:T(8,128)(2,1)S(1)} collective-permute-done((bf16[32,512]{1,0:T(8,128)(2,1)S(1)}, bf16[32,512]{1,0:T(8,128)(2,1)S(1)}, u32[]{:S(2)}, u32[]{:S(2)}) %collective-permute-start.6) | collective-permute-done | bytes 32800 | tf_op jit(solution)/shard_map/ppermute | solution.py:399
  71.9 1.9 %collective-permute-start.7 = (bf16[56,1024]{1,0:T(8,128)(2,1)S(1)}, bf16[56,1024]{1,0:T(8,128)(2,1)S(1)}, u32[]{:S(2)}, u32[]{:S(2)}) collective-permute-start(bf16[56,1024]{1,0:T(8,128)(2,1)S(1)} %get-tuple-element.35), channel_id=1, source_target_pairs={{0,2},{2,0},{1,3},{3,1},{4,6},{6,4},{5,7},{7,5},{8,10},{10,8},{9,1... | collective-permute-start | bytes 344072 | tf_op jit(solution)/shard_map/ppermute | solution.py:403
  73.8 0.6 collective-permute-done.4.message
  74.4 2.7 %shard_map.110 = bf16[14,14,1024]{2,1,0:T(8,128)(2,1)} custom-call(bf16[196,1024]{1,0:T(8,128)(2,1)S(1)} %collective-permute-done.4.message, bf16[196,16,128]{2,1,0:T(8,128)(2,1)} %bitcast.37, f32[48,1024]{1,0:T(8,128)S(1)} %get-tuple-element.31.token.own), custom_call_target="tpu_custom_call" | custom-call | bytes 1024 | tf_op jit(solution)/shard_map/pallas_call | solution.py:354
  77.1 0.0 collective-permute-done.5.message
  77.1 1.1 %shard_map.111 = bf16[14,14,1024]{2,1,0:T(8,128)(2,1)} custom-call(bf16[200,1024]{1,0:T(8,128)(2,1)S(1)} %collective-permute-done.5.message, bf16[196,16,128]{2,1,0:T(8,128)(2,1)} %bitcast.39, f32[48,1024]{1,0:T(8,128)S(1)} %get-tuple-element.31.token.own), custom_call_target="tpu_custom_call" | custom-call | bytes 1024 | tf_op jit(solution)/shard_map/pallas_call | solution.py:354
  78.2 0.0 collective-permute-done.8.top
  78.2 1.0 %shard_map.114.grads = f32[256,1024]{1,0:T(8,128)} custom-call(f32[208,1024]{1,0:T(8,128)S(1)} %get-tuple-element.37.own, bf16[208,1024]{1,0:T(8,128)(2,1)S(1)} %collective-permute-done.8.top), custom_call_target="tpu_custom_call" | custom-call | bytes 1024 | tf_op jit(solution)/shard_map/pallas_call | solution.py:354
  79.3 3.1 %collective-permute-done.7.low = bf16[56,1024]{1,0:T(8,128)(2,1)S(1)} collective-permute-done((bf16[56,1024]{1,0:T(8,128)(2,1)S(1)}, bf16[56,1024]{1,0:T(8,128)(2,1)S(1)}, u32[]{:S(2)}, u32[]{:S(2)}) %collective-permute-start.7) | collective-permute-done | bytes 114720 | tf_op jit(solution)/shard_map/ppermute | solution.py:403
  82.4 1.3 %shard_map.115 = (f32[256,1024]{1,0:T(8,128)}, f32[25,2,128]{2,1,0:T(2,128)}) custom-call(f32[48,1024]{1,0:T(8,128)S(1)} %get-tuple-element.31.token.own, bf16[56,1024]{1,0:T(8,128)(2,1)S(1)} %collective-permute-done.7.low, f32[32,256]{1,0:T(8,128)S(1)} %get-tuple-element.36.own_k, f32[256,1024]{1,0:T(8,128)} %shard_map.114.grads), custom_call_target="tpu_custom_call", output_to_operand_aliasing={{0}: (3, {})} | custom-call | bytes 1024 | tf_op jit(solution)/shard_map/pallas_call | solution.py:354
  (2 shorter events, 0.0 us)
Async XLA Ops:
  5.4 23.6 %collective-permute-start.1 = (bf16[196,1024]{1,0:T(8,128)(2,1)S(1)}, bf16[196,1024]{1,0:T(8,128)(2,1)S(1)}, u32[]{:S(2)}, u32[]{:S(2)}) collective-permute-start(bf16[196,1024]{1,0:T(8,128)(2,1)S(1)} %get-tuple-element.27.token), channel_id=1, source_target_pairs={{4,0},{8,4},{12,8},{16,12},{20,16},{24,20},{28,24},{32,28},{36,32}... | collective-permute-start | bytes 1204232 | tf_op jit(solution)/shard_map/ppermute | solution.py:395
  10.0 21.3 %collective-permute-start.2 = (bf16[196,2048]{1,0:T(8,128)(2,1)S(1)}, bf16[196,2048]{1,0:T(8,128)(2,1)S(1)}, u32[]{:S(2)}, u32[]{:S(2)}) collective-permute-start(bf16[196,2048]{1,0:T(8,128)(2,1)S(1)} %get-tuple-element.29), channel_id=1, source_target_pairs={{0,1},{1,0},{2,3},{3,2},{4,5},{5,4},{6,7},{7,6},{8,9},{9,8},{10,11... | collective-permute-start | bytes 2408456 | tf_op jit(solution)/shard_map/ppermute | solution.py:399
  24.7 31.8 %collective-permute-start = (bf16[216,1024]{1,0:T(8,128)(2,1)S(1)}, bf16[216,1024]{1,0:T(8,128)(2,1)S(1)}, u32[]{:S(2)}, u32[]{:S(2)}) collective-permute-start(bf16[216,1024]{1,0:T(8,128)(2,1)S(1)} %shard_map.104.token), channel_id=1, source_target_pairs={{0,4},{4,8},{8,12},{12,16},{16,20},{20,24},{24,28},{28,32},{32,36}... | collective-permute-start | bytes 1327112 | tf_op jit(solution)/shard_map/ppermute | solution.py:395
  29.1 3.6 %collective-permute-start.3 = (bf16[196,1024]{1,0:T(8,128)(2,1)S(1)}, bf16[196,1024]{1,0:T(8,128)(2,1)S(1)}, u32[]{:S(2)}, u32[]{:S(2)}) collective-permute-start(bf16[196,1024]{1,0:T(8,128)(2,1)S(1)} %shard_map.105.g_own.g.g1), channel_id=1, source_target_pairs={{0,1},{1,0},{2,3},{3,2},{4,5},{5,4},{6,7},{7,6},{8,9},{9,8},{10,11... | collective-permute-start | bytes 1204232 | tf_op jit(solution)/shard_map/ppermute | solution.py:399
  33.4 44.8 %collective-permute-start.8 = (bf16[208,1024]{1,0:T(8,128)(2,1)S(1)}, bf16[208,1024]{1,0:T(8,128)(2,1)S(1)}, u32[]{:S(2)}, u32[]{:S(2)}) collective-permute-start(bf16[208,1024]{1,0:T(8,128)(2,1)S(1)} %get-tuple-element.30.token), channel_id=1, source_target_pairs={{0,2},{2,0},{1,3},{3,1},{4,6},{6,4},{5,7},{7,5},{8,10},{10,8},{9,1... | collective-permute-start | bytes 1277960 | tf_op jit(solution)/shard_map/ppermute | solution.py:403
  38.0 39.1 %collective-permute-start.5 = (bf16[200,1024]{1,0:T(8,128)(2,1)S(1)}, bf16[200,1024]{1,0:T(8,128)(2,1)S(1)}, u32[]{:S(2)}, u32[]{:S(2)}) collective-permute-start(bf16[200,1024]{1,0:T(8,128)(2,1)S(1)} %shard_map.108.token), channel_id=1, source_target_pairs={{4,0},{8,4},{12,8},{16,12},{20,16},{24,20},{28,24},{32,28},{36,32}... | collective-permute-start | bytes 1228808 | tf_op jit(solution)/shard_map/ppermute | solution.py:395
  60.3 14.1 %collective-permute-start.4 = (bf16[196,1024]{1,0:T(8,128)(2,1)S(1)}, bf16[196,1024]{1,0:T(8,128)(2,1)S(1)}, u32[]{:S(2)}, u32[]{:S(2)}) collective-permute-start(bf16[196,1024]{1,0:T(8,128)(2,1)S(1)} %shard_map.109.token), channel_id=1, source_target_pairs={{0,4},{4,8},{8,12},{12,16},{16,20},{20,24},{24,28},{28,32},{32,36}... | collective-permute-start | bytes 1204232 | tf_op jit(solution)/shard_map/ppermute | solution.py:395
  67.7 4.2 %collective-permute-start.6 = (bf16[32,512]{1,0:T(8,128)(2,1)S(1)}, bf16[32,512]{1,0:T(8,128)(2,1)S(1)}, u32[]{:S(2)}, u32[]{:S(2)}) collective-permute-start(bf16[32,512]{1,0:T(8,128)(2,1)S(1)} %get-tuple-element.33), channel_id=1, source_target_pairs={{0,1},{1,0},{2,3},{3,2},{4,5},{5,4},{6,7},{7,6},{8,9},{9,8},{10,11... | collective-permute-start | bytes 98312 | tf_op jit(solution)/shard_map/ppermute | solution.py:399
  71.9 10.5 %collective-permute-start.7 = (bf16[56,1024]{1,0:T(8,128)(2,1)S(1)}, bf16[56,1024]{1,0:T(8,128)(2,1)S(1)}, u32[]{:S(2)}, u32[]{:S(2)}) collective-permute-start(bf16[56,1024]{1,0:T(8,128)(2,1)S(1)} %get-tuple-element.35), channel_id=1, source_target_pairs={{0,2},{2,0},{1,3},{3,1},{4,6},{6,4},{5,7},{7,5},{8,10},{10,8},{9,1... | collective-permute-start | bytes 344072 | tf_op jit(solution)/shard_map/ppermute | solution.py:403

commit v8 on v7

--- a/solution.py
+++ b/solution.py
@@ -431,7 +431,7 @@
         factors_kernel,
         [VMEM, VMEM, VMEM, ANY],
         (MESSAGE, jax.ShapeDtypeStruct((PIX, 2 * C), bf16)),
-        [PADDED, DENSE, WIDE],
+        [PADDED, pltpu.VMEM((DENSE_ROWS + GROUPS, LANES), f32), WIDE],
         (pair, g0, t, grad_in0),
     )
     peer = other_core(send)

time: 84.1 us -> 84.1 us (level)
  no operation moved by 1% of the time
where the time goes in v8:
time: 84.1 us; the launch traced here: 83.7 us
  starting transfers between devices  31.2 us (37%)
  Pallas kernels  29.2 us (35%)
  waiting for transfers between devices  22.4 us (27%)
    pallas_call x14, Pallas kernels, call(): pl.pallas_call(kernel, in_specs=ins, out_specs=jax.tree.map(lambda _: VME...  29.2 us
    ppermute x3, starting transfers between devices, other_core(): return lax.ppermute(value, 'dp', [(0, 1), (1, 0), (2, 3), (3, 2)])  18 us
    ppermute x4, waiting for transfers between devices, shifted(): return lax.ppermute(value, 'section', pairs)  17.7 us
    ppermute x4, starting transfers between devices, shifted(): return lax.ppermute(value, 'section', pairs)  9.43 us
    ppermute x2, starting transfers between devices, other_chip(): return lax.ppermute(value, 'dp', [(0, 2), (2, 0), (1, 3), (3, 1)])  3.84 us
    ppermute x2, waiting for transfers between devices, other_chip(): return lax.ppermute(value, 'dp', [(0, 2), (2, 0), (1, 3), (3, 1)])  3.1 us
  transfers between devices with their start and end apart: 9, of which 5 were waited for; matrix products, arithmetic and copies ran while one was open for 0% of the time, Pallas kernels for 28%

profile of v8, /device:TPU:1, one launch (start us, length us, event | category | flops | bytes accessed | tf_op | source)
XLA Modules:
  0.0 83.7 jit_solution(13980002076472566285)
XLA Ops:
  0.6 4.8 %shard_map.102 = (bf16[196,1024]{1,0:T(8,128)(2,1)S(1)}, bf16[196,1024]{1,0:T(8,128)(2,1)S(1)}, bf16[1024,1024]{1,0:T(8,128)(2,1)S(1)}, f32[25,8,128]{2,1,0:T(8,...) custom-call(bf16[14,14,1024]{2,1,0:T(8,128)(2,1)} %bitcast.42, ...), custom_call_target="tpu_custom_call" | custom-call | bytes 1024 | tf_op jit(solution)/shard_map/pallas_call | solution.py:354
  5.4 1.3 %collective-permute-start.1 = (bf16[196,1024]{1,0:T(8,128)(2,1)S(1)}, bf16[196,1024]{1,0:T(8,128)(2,1)S(1)}, u32[]{:S(2)}, u32[]{:S(2)}) collective-permute-start(bf16[196,1024]{1,0:T(8,128)(2,1)S(1)} %get-tuple-element.27.token), channel_id=1, source_target_pairs={{4,0},{8,4},{12,8},{16,12},{20,16},{24,20},{28,24},{32,28},{36,32}... | collective-permute-start | bytes 1204232 | tf_op jit(solution)/shard_map/ppermute | solution.py:395
  6.7 3.3 %shard_map.103 = (bf16[196,1024]{1,0:T(8,128)(2,1)S(1)}, bf16[196,2048]{1,0:T(8,128)(2,1)S(1)}) custom-call(bf16[196,16,128]{2,1,0:T(8,128)(2,1)S(1)} %get-tuple-element.25.pair, bf16[196,1024]{1,0:T(8,128)(2,1)S(1)} %get-tuple-element.26.g_rows.g_own.g0, f32[25,8,128]{2,1,0:T(8,128)S(1)} %get-tuple-element.24.taps, ...), custom_call_target="tpu_custom_call" | custom-call | bytes 1024 | tf_op jit(solution)/shard_map/pallas_call | solution.py:354
  10.0 12.4 %collective-permute-start.2 = (bf16[196,2048]{1,0:T(8,128)(2,1)S(1)}, bf16[196,2048]{1,0:T(8,128)(2,1)S(1)}, u32[]{:S(2)}, u32[]{:S(2)}) collective-permute-start(bf16[196,2048]{1,0:T(8,128)(2,1)S(1)} %get-tuple-element.29), channel_id=1, source_target_pairs={{0,1},{1,0},{2,3},{3,2},{4,5},{5,4},{6,7},{7,6},{8,9},{9,8},{10,11... | collective-permute-start | bytes 2408456 | tf_op jit(solution)/shard_map/ppermute | solution.py:399
  22.4 2.3 %shard_map.104.token = bf16[216,1024]{1,0:T(8,128)(2,1)S(1)} custom-call(bf16[14,14,1024]{2,1,0:T(8,128)(2,1)S(1)} %get-tuple-element.22.x, bf16[1024,1024]{1,0:T(8,128)(2,1)S(1)} %get-tuple-element.23.weight, f32[25,8,128]{2,1,0:T(8,128)S(1)} %get-tuple-element.24.taps, bf16[196,1024]{1,0:T(8,128)(2,1)S(1)} %get-tuple-element.28.token.keep), custom_call_target="tpu_custom_call" | custom-call | bytes 1024 | tf_op jit(solution)/shard_map/pallas_call | solution.py:354
  24.7 4.3 %collective-permute-start = (bf16[216,1024]{1,0:T(8,128)(2,1)S(1)}, bf16[216,1024]{1,0:T(8,128)(2,1)S(1)}, u32[]{:S(2)}, u32[]{:S(2)}) collective-permute-start(bf16[216,1024]{1,0:T(8,128)(2,1)S(1)} %shard_map.104.token), channel_id=1, source_target_pairs={{0,4},{4,8},{8,12},{12,16},{16,20},{20,24},{24,28},{28,32},{32,36}... | collective-permute-start | bytes 1327112 | tf_op jit(solution)/shard_map/ppermute | solution.py:395
  29.0 0.0 collective-permute-done.1.g_in
  29.0 2.2 %collective-permute-start.3 = (bf16[196,1024]{1,0:T(8,128)(2,1)S(1)}, bf16[196,1024]{1,0:T(8,128)(2,1)S(1)}, u32[]{:S(2)}, u32[]{:S(2)}) collective-permute-start(bf16[196,1024]{1,0:T(8,128)(2,1)S(1)} %shard_map.105.g_own.g.g1), channel_id=1, source_target_pairs={{0,1},{1,0},{2,3},{3,2},{4,5},{5,4},{6,7},{7,6},{8,9},{9,8},{10,11... | collective-permute-start | bytes 1204232 | tf_op jit(solution)/shard_map/ppermute | solution.py:399
  31.2 0.0 collective-permute-done.2.peer
  31.3 0.7 shard_map.106.total
  32.0 0.7 collective-permute-done.3.g_peer
  32.7 0.7 shard_map.107
  33.4 1.9 %collective-permute-start.8 = (bf16[208,1024]{1,0:T(8,128)(2,1)S(1)}, bf16[208,1024]{1,0:T(8,128)(2,1)S(1)}, u32[]{:S(2)}, u32[]{:S(2)}) collective-permute-start(bf16[208,1024]{1,0:T(8,128)(2,1)S(1)} %get-tuple-element.30.token), channel_id=1, source_target_pairs={{0,2},{2,0},{1,3},{3,1},{4,6},{6,4},{5,7},{7,5},{8,10},{10,8},{9,1... | collective-permute-start | bytes 1277960 | tf_op jit(solution)/shard_map/ppermute | solution.py:403
  35.4 2.7 %shard_map.108.token = bf16[200,1024]{1,0:T(8,128)(2,1)S(1)} custom-call(bf16[196,1024]{1,0:T(8,128)(2,1)S(1)} %shard_map.105.g_own.g.g1, bf16[196,16,128]{2,1,0:T(8,128)(2,1)S(1)} %get-tuple-element.25.pair, bf16[1024,1024]{1,0:T(8,128)(2,1)S(1)} %get-tuple-element.23.weight, f32[25,8,128]{2,1,0:T(8,128)S(1)} %get-tuple-element.24.taps, ...), custom_call_target="tpu_custom_call" | custom-call | bytes 1024 | tf_op jit(solution)/shard_map/pallas_call | solution.py:354
  38.0 1.3 %collective-permute-start.5 = (bf16[200,1024]{1,0:T(8,128)(2,1)S(1)}, bf16[200,1024]{1,0:T(8,128)(2,1)S(1)}, u32[]{:S(2)}, u32[]{:S(2)}) collective-permute-start(bf16[200,1024]{1,0:T(8,128)(2,1)S(1)} %shard_map.108.token), channel_id=1, source_target_pairs={{4,0},{8,4},{12,8},{16,12},{20,16},{24,20},{28,24},{32,28},{36,32}... | collective-permute-start | bytes 1228808 | tf_op jit(solution)/shard_map/ppermute | solution.py:395
  39.3 17.1 %collective-permute-done.x = bf16[216,1024]{1,0:T(8,128)(2,1)S(1)} collective-permute-done((bf16[216,1024]{1,0:T(8,128)(2,1)S(1)}, bf16[216,1024]{1,0:T(8,128)(2,1)S(1)}, u32[]{:S(2)}, u32[]{:S(2)}) %collective-permute-start) | collective-permute-done | bytes 442400 | tf_op jit(solution)/shard_map/ppermute | solution.py:395
  56.5 3.9 %shard_map.109.token = bf16[196,1024]{1,0:T(8,128)(2,1)S(1)} custom-call(bf16[216,1024]{1,0:T(8,128)(2,1)S(1)} %collective-permute-done.x, bf16[1024,1024]{1,0:T(8,128)(2,1)S(1)} %get-tuple-element.23.weight, f32[25,8,128]{2,1,0:T(8,128)S(1)} %get-tuple-element.24.taps, bf16[196,16,128]{2,1,0:T(8,128)(2,1)} %bitcast.36, bf16[200,1024]{1,0:T(8,128)(2,1)S(1)} %shard_map.108.token), custom_call_target="tpu_custom_call" | custom-call | bytes 1024 | tf_op jit(solution)/shard_map/pallas_call | solution.py:354
  60.3 2.5 %collective-permute-start.4 = (bf16[196,1024]{1,0:T(8,128)(2,1)S(1)}, bf16[196,1024]{1,0:T(8,128)(2,1)S(1)}, u32[]{:S(2)}, u32[]{:S(2)}) collective-permute-start(bf16[196,1024]{1,0:T(8,128)(2,1)S(1)} %shard_map.109.token), channel_id=1, source_target_pairs={{0,4},{4,8},{8,12},{12,16},{16,20},{20,24},{24,28},{28,32},{32,36}... | collective-permute-start | bytes 1204232 | tf_op jit(solution)/shard_map/ppermute | solution.py:395
  62.9 4.8 %shard_map.112 = (f32[32,512]{1,0:T(8,128)S(1)}, bf16[32,512]{1,0:T(8,128)(2,1)S(1)}) custom-call(bf16[196,16,128]{2,1,0:T(8,128)(2,1)S(1)} %get-tuple-element.25.pair, bf16[196,1024]{1,0:T(8,128)(2,1)S(1)} %get-tuple-element.26.g_rows.g_own.g0, bf16[196,1024]{1,0:T(8,128)(2,1)S(1)} %shard_map.105.g_own.g.g1, ...), custom_call_target="tpu_custom_call" | custom-call | bytes 1024 | tf_op jit(solution)/shard_map/pallas_call | solution.py:354
  67.7 3.4 %collective-permute-start.6 = (bf16[32,512]{1,0:T(8,128)(2,1)S(1)}, bf16[32,512]{1,0:T(8,128)(2,1)S(1)}, u32[]{:S(2)}, u32[]{:S(2)}) collective-permute-start(bf16[32,512]{1,0:T(8,128)(2,1)S(1)} %get-tuple-element.33), channel_id=1, source_target_pairs={{0,1},{1,0},{2,3},{3,2},{4,5},{5,4},{6,7},{7,6},{8,9},{9,8},{10,11... | collective-permute-start | bytes 98312 | tf_op jit(solution)/shard_map/ppermute | solution.py:399
  71.0 0.8 %collective-permute-done.6.arrived = bf16[32,512]{1,0:T(8,128)(2,1)S(1)} collective-permute-done((bf16[32,512]{1,0:T(8,128)(2,1)S(1)}, bf16[32,512]{1,0:T(8,128)(2,1)S(1)}, u32[]{:S(2)}, u32[]{:S(2)}) %collective-permute-start.6) | collective-permute-done | bytes 32800 | tf_op jit(solution)/shard_map/ppermute | solution.py:399
  71.9 1.9 %collective-permute-start.7 = (bf16[56,1024]{1,0:T(8,128)(2,1)S(1)}, bf16[56,1024]{1,0:T(8,128)(2,1)S(1)}, u32[]{:S(2)}, u32[]{:S(2)}) collective-permute-start(bf16[56,1024]{1,0:T(8,128)(2,1)S(1)} %get-tuple-element.35), channel_id=1, source_target_pairs={{0,2},{2,0},{1,3},{3,1},{4,6},{6,4},{5,7},{7,5},{8,10},{10,8},{9,1... | collective-permute-start | bytes 344072 | tf_op jit(solution)/shard_map/ppermute | solution.py:403
  73.8 0.6 collective-permute-done.4.message
  74.4 2.7 %shard_map.110 = bf16[14,14,1024]{2,1,0:T(8,128)(2,1)} custom-call(bf16[196,1024]{1,0:T(8,128)(2,1)S(1)} %collective-permute-done.4.message, bf16[196,16,128]{2,1,0:T(8,128)(2,1)} %bitcast.37, f32[48,1024]{1,0:T(8,128)S(1)} %get-tuple-element.31.token.own), custom_call_target="tpu_custom_call" | custom-call | bytes 1024 | tf_op jit(solution)/shard_map/pallas_call | solution.py:354
  77.1 0.0 collective-permute-done.5.message
  77.1 1.1 %shard_map.111 = bf16[14,14,1024]{2,1,0:T(8,128)(2,1)} custom-call(bf16[200,1024]{1,0:T(8,128)(2,1)S(1)} %collective-permute-done.5.message, bf16[196,16,128]{2,1,0:T(8,128)(2,1)} %bitcast.39, f32[48,1024]{1,0:T(8,128)S(1)} %get-tuple-element.31.token.own), custom_call_target="tpu_custom_call" | custom-call | bytes 1024 | tf_op jit(solution)/shard_map/pallas_call | solution.py:354
  78.2 0.0 collective-permute-done.8.top
  78.2 1.0 %shard_map.114.grads = f32[256,1024]{1,0:T(8,128)} custom-call(f32[208,1024]{1,0:T(8,128)S(1)} %get-tuple-element.37.own, bf16[208,1024]{1,0:T(8,128)(2,1)S(1)} %collective-permute-done.8.top), custom_call_target="tpu_custom_call" | custom-call | bytes 1024 | tf_op jit(solution)/shard_map/pallas_call | solution.py:354
  79.2 3.1 %collective-permute-done.7.low = bf16[56,1024]{1,0:T(8,128)(2,1)S(1)} collective-permute-done((bf16[56,1024]{1,0:T(8,128)(2,1)S(1)}, bf16[56,1024]{1,0:T(8,128)(2,1)S(1)}, u32[]{:S(2)}, u32[]{:S(2)}) %collective-permute-start.7) | collective-permute-done | bytes 114720 | tf_op jit(solution)/shard_map/ppermute | solution.py:403
  82.3 1.3 %shard_map.115 = (f32[256,1024]{1,0:T(8,128)}, f32[25,2,128]{2,1,0:T(2,128)}) custom-call(f32[48,1024]{1,0:T(8,128)S(1)} %get-tuple-element.31.token.own, bf16[56,1024]{1,0:T(8,128)(2,1)S(1)} %collective-permute-done.7.low, f32[32,256]{1,0:T(8,128)S(1)} %get-tuple-element.36.own_k, f32[256,1024]{1,0:T(8,128)} %shard_map.114.grads), custom_call_target="tpu_custom_call", output_to_operand_aliasing={{0}: (3, {})} | custom-call | bytes 1024 | tf_op jit(solution)/shard_map/pallas_call | solution.py:354
  (2 shorter events, 0.0 us)
Async XLA Ops:
  5.4 23.6 %collective-permute-start.1 = (bf16[196,1024]{1,0:T(8,128)(2,1)S(1)}, bf16[196,1024]{1,0:T(8,128)(2,1)S(1)}, u32[]{:S(2)}, u32[]{:S(2)}) collective-permute-start(bf16[196,1024]{1,0:T(8,128)(2,1)S(1)} %get-tuple-element.27.token), channel_id=1, source_target_pairs={{4,0},{8,4},{12,8},{16,12},{20,16},{24,20},{28,24},{32,28},{36,32}... | collective-permute-start | bytes 1204232 | tf_op jit(solution)/shard_map/ppermute | solution.py:395
  10.0 21.3 %collective-permute-start.2 = (bf16[196,2048]{1,0:T(8,128)(2,1)S(1)}, bf16[196,2048]{1,0:T(8,128)(2,1)S(1)}, u32[]{:S(2)}, u32[]{:S(2)}) collective-permute-start(bf16[196,2048]{1,0:T(8,128)(2,1)S(1)} %get-tuple-element.29), channel_id=1, source_target_pairs={{0,1},{1,0},{2,3},{3,2},{4,5},{5,4},{6,7},{7,6},{8,9},{9,8},{10,11... | collective-permute-start | bytes 2408456 | tf_op jit(solution)/shard_map/ppermute | solution.py:399
  24.7 31.8 %collective-permute-start = (bf16[216,1024]{1,0:T(8,128)(2,1)S(1)}, bf16[216,1024]{1,0:T(8,128)(2,1)S(1)}, u32[]{:S(2)}, u32[]{:S(2)}) collective-permute-start(bf16[216,1024]{1,0:T(8,128)(2,1)S(1)} %shard_map.104.token), channel_id=1, source_target_pairs={{0,4},{4,8},{8,12},{12,16},{16,20},{20,24},{24,28},{28,32},{32,36}... | collective-permute-start | bytes 1327112 | tf_op jit(solution)/shard_map/ppermute | solution.py:395
  29.0 3.6 %collective-permute-start.3 = (bf16[196,1024]{1,0:T(8,128)(2,1)S(1)}, bf16[196,1024]{1,0:T(8,128)(2,1)S(1)}, u32[]{:S(2)}, u32[]{:S(2)}) collective-permute-start(bf16[196,1024]{1,0:T(8,128)(2,1)S(1)} %shard_map.105.g_own.g.g1), channel_id=1, source_target_pairs={{0,1},{1,0},{2,3},{3,2},{4,5},{5,4},{6,7},{7,6},{8,9},{9,8},{10,11... | collective-permute-start | bytes 1204232 | tf_op jit(solution)/shard_map/ppermute | solution.py:399
  33.4 44.8 %collective-permute-start.8 = (bf16[208,1024]{1,0:T(8,128)(2,1)S(1)}, bf16[208,1024]{1,0:T(8,128)(2,1)S(1)}, u32[]{:S(2)}, u32[]{:S(2)}) collective-permute-start(bf16[208,1024]{1,0:T(8,128)(2,1)S(1)} %get-tuple-element.30.token), channel_id=1, source_target_pairs={{0,2},{2,0},{1,3},{3,1},{4,6},{6,4},{5,7},{7,5},{8,10},{10,8},{9,1... | collective-permute-start | bytes 1277960 | tf_op jit(solution)/shard_map/ppermute | solution.py:403
  38.0 39.1 %collective-permute-start.5 = (bf16[200,1024]{1,0:T(8,128)(2,1)S(1)}, bf16[200,1024]{1,0:T(8,128)(2,1)S(1)}, u32[]{:S(2)}, u32[]{:S(2)}) collective-permute-start(bf16[200,1024]{1,0:T(8,128)(2,1)S(1)} %shard_map.108.token), channel_id=1, source_target_pairs={{4,0},{8,4},{12,8},{16,12},{20,16},{24,20},{28,24},{32,28},{36,32}... | collective-permute-start | bytes 1228808 | tf_op jit(solution)/shard_map/ppermute | solution.py:395
  60.3 14.1 %collective-permute-start.4 = (bf16[196,1024]{1,0:T(8,128)(2,1)S(1)}, bf16[196,1024]{1,0:T(8,128)(2,1)S(1)}, u32[]{:S(2)}, u32[]{:S(2)}) collective-permute-start(bf16[196,1024]{1,0:T(8,128)(2,1)S(1)} %shard_map.109.token), channel_id=1, source_target_pairs={{0,4},{4,8},{8,12},{12,16},{16,20},{20,24},{24,28},{28,32},{32,36}... | collective-permute-start | bytes 1204232 | tf_op jit(solution)/shard_map/ppermute | solution.py:395
  67.7 4.2 %collective-permute-start.6 = (bf16[32,512]{1,0:T(8,128)(2,1)S(1)}, bf16[32,512]{1,0:T(8,128)(2,1)S(1)}, u32[]{:S(2)}, u32[]{:S(2)}) collective-permute-start(bf16[32,512]{1,0:T(8,128)(2,1)S(1)} %get-tuple-element.33), channel_id=1, source_target_pairs={{0,1},{1,0},{2,3},{3,2},{4,5},{5,4},{6,7},{7,6},{8,9},{9,8},{10,11... | collective-permute-start | bytes 98312 | tf_op jit(solution)/shard_map/ppermute | solution.py:399
  71.9 10.5 %collective-permute-start.7 = (bf16[56,1024]{1,0:T(8,128)(2,1)S(1)}, bf16[56,1024]{1,0:T(8,128)(2,1)S(1)}, u32[]{:S(2)}, u32[]{:S(2)}) collective-permute-start(bf16[56,1024]{1,0:T(8,128)(2,1)S(1)} %get-tuple-element.35), channel_id=1, source_target_pairs={{0,2},{2,0},{1,3},{3,1},{4,6},{6,4},{5,7},{7,5},{8,10},{10,8},{9,1... | collective-permute-start | bytes 344072 | tf_op jit(solution)/shard_map/ppermute | solution.py:403
